TPU v7x, 256 devices: a whole 4x4x8 slice. The times are simulated.
256 devices in a mesh: space: 64 (over z, y, core), view: 4 (over x).
Axes of the slice: x: 4, y: 4, z: 8, core: 2. Of those that a mesh axis runs over, the one named last changes fastest.
Arguments:
- gaussians: float32 [59, 524288], P(None, 'space'), as said below
- camera_table: float32 [16, 8], replicated, as said below
- view_camera: int32 [4], P('view'), may hold values from 0 to 15
- tile_plan: int32 [4, 1024], P('view', 'space'), may hold values from 2204 to 5955, as said below
- requests: int32 [4, 64, 64, 128], P('view', 'space'), may hold values from 0 to 8191, as said below
- tile_lists: int32 [4, 1024, 512], P('view', 'space'), may hold values from 0 to 8191, as said below
- tile_lengths: int32 [4, 1024], P('view', 'space'), may hold values from 128 to 512, as said below
- pixel_grad: float32 [4, 1024, 3, 256], P('view', 'space'), may hold values from -0.625 to 0.625
Outputs:
- rendered: float32 [4, 1024, 3, 256], P('view', 'space')
- gaussian_grad: float32 [59, 524288], P(None, 'space')
Inputs may be any that keep to these rules, and one draw needn't show every extreme that they name: `tile_plan`: tile ids count 120 tiles to a row; within a view every tile k < 1024 of tile row 18 + floor(k / 32) and tile column 44 + (k mod 32) appears exactly once. `requests`: slots of the owner's 8192 Gaussians; within a view no slot of an owner is requested twice, by one renderer or by two. `tile_lists`: position o * 128 + k names the k-th slot the renderer requested of owner o; the lists of one renderer's tiles together name each of its requested rows exactly once, each list the same number of rows of every owner, ordered by owner and within an owner by slot; entries from the tile's length on are padding. `tile_lengths`: every view has a tile with all 512 entries live. `camera_table`: quaternion rows lead with 2 to 3 and the rest within 0.3; offsets lie within 0.2 across and 4 to 5 in depth; focal lengths 1.8 to 2.4. `gaussians`: the first quaternion entry lies in 1 to 2.
All inputs are finite; a program needn't handle non-finite values.
Results may differ from a plain program's by a relative error of at most 0.0003.
Values sent between devices are 32-bit elements; how exact they have to be, the bound alone decides.
No kernel may reach another device: no remote copies, remote signals or barrier semaphores. Data moves between devices by JAX's collectives and lax.ppermute only.
A program may use at most 256 MiB of HBM per device.

v0:
```python
import jax
import jax.numpy as jnp
from jax import lax
from jax.sharding import PartitionSpec as P

sh_zero = 0.28209479177387814
sh_one = 0.4886025119029199
sh_two = (
    1.0925484305920792,
    -1.0925484305920792,
    0.31539156525252005,
    -1.0925484305920792,
    0.5462742152960396,
)
sh_three = (
    -0.5900435899266435,
    2.890611442640554,
    -0.4570457994644658,
    0.3731763325901154,
    -0.4570457994644658,
    1.445305721320277,
    -0.5900435899266435,
)
dilation = 0.3 / 291600.0
highest = lax.Precision.HIGHEST


def quat_matrix(quat_w, quat_x, quat_y, quat_z):
    length = jnp.sqrt(quat_w * quat_w + quat_x * quat_x + quat_y * quat_y + quat_z * quat_z)
    unit_w = quat_w / length
    unit_x = quat_x / length
    unit_y = quat_y / length
    unit_z = quat_z / length
    return [
        [
            1.0 - 2.0 * (unit_y * unit_y + unit_z * unit_z),
            2.0 * (unit_x * unit_y - unit_w * unit_z),
            2.0 * (unit_x * unit_z + unit_w * unit_y),
        ],
        [
            2.0 * (unit_x * unit_y + unit_w * unit_z),
            1.0 - 2.0 * (unit_x * unit_x + unit_z * unit_z),
            2.0 * (unit_y * unit_z - unit_w * unit_x),
        ],
        [
            2.0 * (unit_x * unit_z - unit_w * unit_y),
            2.0 * (unit_y * unit_z + unit_w * unit_x),
            1.0 - 2.0 * (unit_x * unit_x + unit_y * unit_y),
        ],
    ]


def sh_basis(dir_x, dir_y, dir_z):
    sq_x = dir_x * dir_x
    sq_y = dir_y * dir_y
    sq_z = dir_z * dir_z
    return [
        sh_zero * jnp.ones_like(dir_x),
        -sh_one * dir_y,
        sh_one * dir_z,
        -sh_one * dir_x,
        sh_two[0] * dir_x * dir_y,
        sh_two[1] * dir_y * dir_z,
        sh_two[2] * (2.0 * sq_z - sq_x - sq_y),
        sh_two[3] * dir_x * dir_z,
        sh_two[4] * (sq_x - sq_y),
        sh_three[0] * dir_y * (3.0 * sq_x - sq_y),
        sh_three[1] * dir_x * dir_y * dir_z,
        sh_three[2] * dir_y * (4.0 * sq_z - sq_x - sq_y),
        sh_three[3] * dir_z * (2.0 * sq_z - 3.0 * sq_x - 3.0 * sq_y),
        sh_three[4] * dir_x * (4.0 * sq_z - sq_x - sq_y),
        sh_three[5] * dir_z * (sq_x - sq_y),
        sh_three[6] * dir_x * (sq_x - 3.0 * sq_y),
    ]


def project(params, camera):
    center = [params[0], params[1], params[2]]
    scales = [jnp.exp(params[3]), jnp.exp(params[4]), jnp.exp(params[5])]
    own_rot = quat_matrix(params[6], params[7], params[8], params[9])
    view_rot = quat_matrix(camera[0], camera[1], camera[2], camera[3])
    offset_cam = [camera[4], camera[5], camera[6]]
    focal_len = camera[7]
    in_camera = [
        sum((view_rot[i][j] * center[j] for j in range(3))) + offset_cam[i] for i in range(3)
    ]
    shaped = [[own_rot[i][k] * scales[k] for k in range(3)] for i in range(3)]
    turned = [
        [sum((view_rot[i][j] * shaped[j][k] for j in range(3))) for k in range(3)] for i in range(3)
    ]
    inv_depth = 1.0 / in_camera[2]
    screen_u = focal_len * in_camera[0] * inv_depth
    screen_v = focal_len * in_camera[1] * inv_depth
    jac_u = [
        focal_len * inv_depth * turned[0][k] - screen_u * inv_depth * turned[2][k] for k in range(3)
    ]
    jac_v = [
        focal_len * inv_depth * turned[1][k] - screen_v * inv_depth * turned[2][k] for k in range(3)
    ]
    cov_uu = sum((jac_u[k] * jac_u[k] for k in range(3))) + dilation
    cov_uv = sum((jac_u[k] * jac_v[k] for k in range(3)))
    cov_vv = sum((jac_v[k] * jac_v[k] for k in range(3))) + dilation
    determinant = cov_uu * cov_vv - cov_uv * cov_uv
    opacity = jax.nn.sigmoid(params[10])
    eye_pos = [-sum((view_rot[j][i] * offset_cam[j] for j in range(3))) for i in range(3)]
    toward = [center[i] - eye_pos[i] for i in range(3)]
    length = jnp.sqrt(toward[0] * toward[0] + toward[1] * toward[1] + toward[2] * toward[2])
    basis = sh_basis(toward[0] / length, toward[1] / length, toward[2] / length)
    colors = [0.5 + sum((basis[k] * params[11 + 3 * k + h] for k in range(16))) for h in range(3)]
    return jnp.stack(
        [
            screen_u,
            screen_v,
            cov_vv / determinant,
            -cov_uv / determinant,
            cov_uu / determinant,
            opacity,
        ]
        + colors
    )


def pixel_points(tile_ids):
    pixel = jnp.arange(256, dtype=jnp.int32)[None, :]
    column = tile_ids[:, None] % 120 * 16 + pixel % 16
    row_at = tile_ids[:, None] // 120 * 16 + pixel // 16
    point_u = (column.astype(jnp.float32) + 0.5 - 960.0) / 540.0
    point_v = (row_at.astype(jnp.float32) + 0.5 - 540.0) / 540.0
    return (point_u, point_v)


def block_alpha(cols, point_u, point_v, lengths):
    width = cols.shape[2]
    diff_u = point_u[:, :, None] - cols[0][:, None, :]
    diff_v = point_v[:, :, None] - cols[1][:, None, :]
    power = -0.5 * (
        cols[2][:, None, :] * diff_u * diff_u
        + 2.0 * cols[3][:, None, :] * diff_u * diff_v
        + cols[4][:, None, :] * diff_v * diff_v
    )
    alpha = cols[5][:, None, :] * jnp.exp(power)
    alive = jnp.arange(width, dtype=jnp.int32)[None, :] < lengths[:, None]
    return jnp.where(alive[:, None, :], alpha, 0.0)


def triangle(width):
    return (
        lax.broadcasted_iota(jnp.int32, (width, width), 0)
        < lax.broadcasted_iota(jnp.int32, (width, width), 1)
    ).astype(jnp.float32)


def composite(features, entries, lengths, tile_ids):
    tile_count, span = entries.shape
    columns = jnp.take(features, entries.reshape(-1), axis=1).reshape(
        features.shape[0], tile_count, span
    )
    point_u, point_v = pixel_points(tile_ids)
    alpha = block_alpha(columns, point_u, point_v, lengths)
    logs = jnp.log1p(-alpha)
    before = jnp.einsum("tpk,kj->tpj", logs, triangle(span), precision=highest)
    weights = alpha * jnp.exp(before)
    return jnp.einsum("ctk,tpk->tcp", columns[6:9], weights, precision=highest)


def per_device(
    gaussians, camera_table, view_camera, tile_plan, requests, tile_lists, tile_lengths, pixel_grad
):
    table_rows = camera_table.shape[0]
    chosen = (jnp.arange(table_rows, dtype=jnp.int32) == view_camera[0]).astype(jnp.float32)
    camera = jnp.sum(camera_table * chosen[:, None], axis=0)
    wanted = requests[0, 0].reshape(-1)
    incoming = lax.all_to_all(wanted, "space", split_axis=0, concat_axis=0, tiled=True)

    def draw_image(features):
        return composite(features, tile_lists[0], tile_lengths[0], tile_plan[0])

    outgoing = jnp.take(gaussians, incoming, axis=1)
    arrived = lax.all_to_all(outgoing, "space", split_axis=1, concat_axis=1, tiled=True)

    def draw_from_params(params):
        return draw_image(project(params, camera))

    image, back_render = jax.vjp(draw_from_params, arrived)
    (row_grad,) = back_render(pixel_grad[0])
    returned = lax.all_to_all(row_grad, "space", split_axis=1, concat_axis=1, tiled=True)
    local_grad = jnp.zeros_like(gaussians).at[:, incoming].add(returned)
    total = lax.psum(local_grad, "view")
    return (image[None], total)


def solution(mesh):
    placed = (
        P(None, "space"),
        P(),
        P("view"),
        P("view", "space"),
        P("view", "space", None, None),
        P("view", "space", None),
        P("view", "space"),
        P("view", "space", None, None),
    )
    return jax.shard_map(
        per_device,
        mesh=mesh,
        in_specs=placed,
        out_specs=(P("view", "space", None, None), P(None, "space")),
        check_vma=False,
    )
```

profile of v0, /device:TPU:6, one launch (start us, length us, event | category | flops | bytes accessed | tf_op | source)
XLA Modules:
  0.0 578.2 jit_solution(9926619483632685027)
XLA Ops:
  7.2 12.2 %all-to-all-start = ((s32[64,128,1]{1,2,0:T(1,128)}), s32[64,128,1]{1,2,0:T(1,128)S(1)}, u32[]{:S(2)}, u32[]{:S(2)}) async-start(s32[64,128,1]{1,2,0:T(1,128)} %bitcast.866), calls=%async_computation | async-start | bytes 65536 | tf_op jit(solution)/shard_map/all_to_all | solution.py:173
  19.4 3.9 copy.559
  23.3 5.7 all-to-all-done
  29.6 30.1 %gather_fusion = f32[8192,59]{1,0:T(8,128)} fusion(f32[59,8192]{0,1:T(8,128)} %copy.559, s32[8192]{0:T(1024)S(1)} %broadcast_clamp_fusion.1), kind=kCustom, calls=%fused_computation | custom fusion | bytes 3899392 | tf_op jit(solution)/shard_map/jit(_take)/gather | solution.py:178
  59.7 2.9 copy.560
  62.7 1.6 broadcast_select_fusion
  64.3 4.7 all-to-all-start.1
  87.5 32.8 %all-to-all-done.1 = f32[59,64,128]{2,0,1:T(8,128)S(1)} async-done(((f32[59,64,128]{2,0,1:T(8,128)}), f32[59,64,128]{2,0,1:T(8,128)S(1)}, u32[]{:S(2)}, u32[]{:S(2)}) %all-to-all-start.1) | async-done | bytes 1933344 | tf_op jit(solution)/shard_map/all_to_all | solution.py:179
  121.3 3.2 add_multiply_fusion.8
  124.8 3.0 fusion.122
  128.4 1.6 add_add_fusion.18
  130.0 1.3 add_add_fusion.19
  131.3 1.3 add_add_fusion.20
  132.6 2.0 stack.2
  134.6 2.9 copy.620
  137.5 32.8 %gather_fusion.1 = f32[8192,9]{1,0:T(8,128)} fusion(f32[9,8192]{0,1:T(8,128)} %copy.620, s32[8192]{0:T(1024)} %broadcast_clamp_fusion), kind=kCustom, calls=%fused_computation.1 | custom fusion | bytes 622592 | tf_op jit(solution)/shard_map/jvp(jit(_take))/gather | solution.py:155
  170.3 2.9 copy.621
  174.0 14.0 %fusion.21 = f32[16,256,512]{2,1,0:T(8,128)S(1)} fusion(f32[16,512]{1,0:T(8,128)S(1)} %mul.10814, f32[16,512]{1,0:T(8,128)S(1)} %sub.1658, f32[16,256]{1,0:T(8,128)} %get-tuple-element.222, f32[16,512]{1,0:T(8,128)S(1)} %mul.10809, f32[16,512]{1,0:T(8,128)S(1)} %sub.1650, f32[16,256]{1,0:T(8,128)} %get-tuple-element.223, f32[16,512]{1,0:T(8,128)S(1)} %mul.10803, ...), kind=kOutput, calls=%fused_computation.39 | convolution fusion | flops 12914524160 | bytes 8626176 | tf_op jit(solution)/shard_map/jvp(tpk,kj->tpj)/dot_general | solution.py:161
  188.0 11.1 %fusion.41 = f32[3,16,512]{2,0,1:T(4,128)S(1)} fusion(f32[16,256,512]{2,1,0:T(8,128)S(1)} %fusion.21, f32[16,512]{1,0:T(8,128)S(1)} %mul.10814, f32[16,512]{1,0:T(8,128)S(1)} %sub.1658, f32[16,256]{1,0:T(8,128)S(1)} %copy-done.50, f32[16,512]{1,0:T(8,128)S(1)} %mul.10809, f32[16,512]{1,0:T(8,128)S(1)} %sub.1650, f32[16,256]{1,0:T(8,128)S(1)} %copy-done.52, ...), kind=kOutput, calls=%fused_computation.58 | convolution fusion | flops 104857600 | bytes 8773632 | tf_op jit(solution)/shard_map/transpose(jvp(ctk,tpk->tcp))/dot_general | solution.py:163
  199.1 6.7 %fusion.46 = f32[16,512,256]{1,2,0:T(8,128)S(1)} fusion(f32[3,16,512]{2,0,1:T(4,128)S(1)} %bitcast.832, f32[16,3,256]{2,0,1:T(8,128)S(1)} %bitcast.799), kind=kOutput, calls=%fused_computation.69 | convolution fusion | flops 75497472 | bytes 8536064 | tf_op jit(solution)/shard_map/transpose(jvp(ctk,tpk->tcp))/dot_general | solution.py:163
  205.9 27.0 %fusion.13 = (f32[16,512]{1,0:T(8,128)S(1)}, f32[16,512]{1,0:T(8,128)S(1)}, f32[16,512]{1,0:T(8,128)S(1)}, f32[16,512]{1,0:T(8,128)S(1)}, f32[16,512]{1,0:T(8,128)S(1)}, /*index=5*/f32[16,512]{1,0:T(8,128)S(1)}) fusion(f32[16,512]{1,0:T(8,128)S(1)} %sub.1658, f32[16,256]{1,0:T(8,128)S(1)} %copy-done.50, f32[16,512]{1,0:T(8,128)S(1)} %mul.10814, ...), kind=kOutput, calls=%fused_computation.28 | convolution fusion | flops 13010944000 | bytes 17211392 | tf_op jit(solution)/shard_map/transpose(jvp(tpk,kj->tpj))/dot_general | solution.py:161
  234.0 2.7 copy.627
  236.8 46.5 %scatter_custom_fusion = f32[9,8192]{0,1:T(8,128)} fusion(s32[8192]{0:T(1024)} %bitcast.860, f32[8192,9]{1,0:T(8,128)} %copy.627, f32[]{:T(128)} %constant.73.clone.1), kind=kCustom, calls=%fused_computation.54 | custom fusion | flops 73728 | bytes 295424 | tf_op jit(solution)/shard_map/transpose(jvp(jit(_take)))/scatter-add | solution.py:155
  283.2 34.0 %fusion.126 = (f32[1,8192]{0,1:T(8,128)}, f32[1,8192]{0,1:T(8,128)}, f32[1,8192]{0,1:T(8,128)}, f32[1,8192]{0,1:T(8,128)}, f32[1,8192]{0,1:T(8,128)}, /*index=5*...) fusion(f32[9,8192]{0,1:T(8,128)} %scatter_custom_fusion), kind=kLoop, calls=%fused_computation.383 | loop fusion | bytes 589824 | tf_op jit(solution)/shard_map/transpose(jvp())/unstack | solution.py:110
  317.3 2.8 copy.704
  320.8 2.8 copy.701
  323.6 2.8 copy.703
  326.5 2.8 copy.702
  329.3 3.4 copy.708
  332.8 2.8 copy.707
  335.6 3.5 copy.706
  339.0 3.5 copy.705
  342.5 3.5 copy.709
  346.3 1.2 multiply_add_fusion.34
  348.4 1.7 fusion.115
  350.1 2.4 add_add_fusion.12
  352.8 3.9 multiply_add_fusion.7
  357.2 1.5 add_add_fusion.9
  359.2 5.3 pad_add_fusion
  365.1 1.1 copy.637
  366.2 56.5 %all_to_all.33 = f32[59,64,128]{2,0,1:T(8,128)S(1)} all-to-all(f32[59,64,128]{2,0,1:T(8,128)S(1)} %copy.637), channel_id=1, replica_groups=mesh['space'=64,'view'=4] {'space'}, dimensions={1} | all-to-all | bytes 3866624 | tf_op jit(solution)/shard_map/all_to_all | solution.py:186
  422.7 1.1 copy.638
  424.2 1.2 copy.714
  425.4 2.8 copy.639
  428.2 46.5 %scatter_custom_fusion.1 = f32[59,8192]{0,1:T(8,128)} fusion(s32[8192]{0:T(1024)} %bitcast.858, f32[8192,59]{1,0:T(8,128)} %copy.639, f32[]{:T(128)} %constant.73.clone.1), kind=kCustom, calls=%fused_computation.56 | custom fusion | flops 483328 | bytes 1933824 | tf_op jit(solution)/shard_map/scatter-add | solution.py:187
  474.9 13.9 %fusion.42 = f32[1,16,3,256]{3,2,1,0:T(4,128)S(1)} fusion(f32[3,16,512]{2,0,1:T(4,128)S(1)} %bitcast.833, f32[16,256,512]{2,1,0:T(8,128)} %copy-done.59, f32[16,512]{1,0:T(8,128)S(1)} %copy-done.41, f32[16,512]{1,0:T(8,128)S(1)} %copy-done.43, f32[16,256]{1,0:T(8,128)S(1)} %copy-done.51, f32[16,512]{1,0:T(8,128)S(1)} %copy-done.45, ...), kind=kOutput, calls=%fused_computation.59 | convolution fusion | flops 104857600 | bytes 8773632 | tf_op jit(solution)/shard_map/jvp(ctk,tpk->tcp)/dot_general | solution.py:163
  489.5 77.6 %all-reduce.68.cloned.1.call-done = f32[59,8192]{0,1:T(8,128)} async-done(((f32[59,8192]{0,1:T(8,128)}), f32[59,8192]{0,1:T(8,128)}) %all-reduce.68.cloned.1.call-update) | async-done | bytes 1933328 | tf_op jit(solution)/shard_map/psum | solution.py:188
  567.1 3.8 copy.641
  (183 shorter events, 12.9 us)
Async XLA Ops:
  7.2 180.8 %copy-start = (f32[1,16,3,256]{3,1,2,0:T(8,128)S(1)}, f32[1,16,3,256]{3,1,2,0:T(8,128)}, u32[]{:S(2)}) copy-start(f32[1,16,3,256]{3,1,2,0:T(8,128)} %param.15) | copy-start | bytes 147460
  7.2 21.8 %all-to-all-start = ((s32[64,128,1]{1,2,0:T(1,128)}), s32[64,128,1]{1,2,0:T(1,128)S(1)}, u32[]{:S(2)}, u32[]{:S(2)}) async-start(s32[64,128,1]{1,2,0:T(1,128)} %bitcast.866), calls=%async_computation | async-start | bytes 65536 | tf_op jit(solution)/shard_map/all_to_all | solution.py:173
  62.6 7.1 %copy-start.56 = (f32[16,8]{0,1:T(8,128)S(1)}, f32[16,8]{0,1:T(8,128)}, u32[]{:S(2)}) copy-start(f32[16,8]{0,1:T(8,128)} %param.9) | copy-start | bytes 1540
  62.6 21.6 %copy-start.34 = (s32[1,16,512]{2,1,0:T(8,128)S(1)}, s32[1,16,512]{2,1,0:T(8,128)}, u32[]{:S(2)}) copy-start(s32[1,16,512]{2,1,0:T(8,128)} %param.13) | copy-start | bytes 98308
  62.6 21.6 %copy-start.58 = (s32[1,16]{1,0:T(1,128)S(1)}, s32[1,16]{1,0:T(1,128)}, u32[]{:S(2)}) copy-start(s32[1,16]{1,0:T(1,128)} %param.11) | copy-start | bytes 196
  62.7 21.7 %copy-start.57 = (s32[1,16]{1,0:T(1,128)S(1)}, s32[1,16]{1,0:T(1,128)}, u32[]{:S(2)}) copy-start(s32[1,16]{1,0:T(1,128)} %param.14) | copy-start | bytes 196
  64.3 56.1 %all-to-all-start.1 = ((f32[59,64,128]{2,0,1:T(8,128)}), f32[59,64,128]{2,0,1:T(8,128)S(1)}, u32[]{:S(2)}, u32[]{:S(2)}) async-start(f32[59,64,128]{2,0,1:T(8,128)} %broadcast_select_fusion), calls=%async_computation.1 | async-start | bytes 4194304 | tf_op jit(solution)/shard_map/all_to_all | solution.py:179
  69.0 498.1 %all-reduce.68.cloned.1.call-start = ((), (), s32[]{:S(2)}) async-start(), calls=%async_computation.3 | async-start | bytes 8388608 | tf_op jit(solution)/shard_map/psum | solution.py:188
  124.5 13.0 %copy-start.6 = (f32[1,64,128]{2,1,0:T(8,128)}, f32[1,64,128]{2,1,0:T(8,128)S(1)}, u32[]{:S(2)}) copy-start(f32[1,64,128]{2,1,0:T(8,128)S(1)} %get-tuple-element.171) | copy-start | bytes 98308
  127.7 42.6 %copy-start.2 = (f32[1,8192]{1,0:T(1,128)}, f32[1,8192]{1,0:T(1,128)S(1)}, u32[]{:S(2)}) copy-start(f32[1,8192]{1,0:T(1,128)S(1)} %get-tuple-element.119) | copy-start | bytes 98308
  127.7 42.5 %copy-start.10 = (f32[1,8192]{1,0:T(1,128)}, f32[1,8192]{1,0:T(1,128)S(1)}, u32[]{:S(2)}) copy-start(f32[1,8192]{1,0:T(1,128)S(1)} %get-tuple-element.88) | copy-start | bytes 98308
  127.7 42.5 %copy-start.12 = (f32[1,8192]{1,0:T(1,128)}, f32[1,8192]{1,0:T(1,128)S(1)}, u32[]{:S(2)}) copy-start(f32[1,8192]{1,0:T(1,128)S(1)} %get-tuple-element.90) | copy-start | bytes 98308
  173.8 32.0 %copy-start.38 = (f32[16,512]{1,0:T(8,128)}, f32[16,512]{1,0:T(8,128)S(1)}, u32[]{:S(2)}) copy-start(f32[16,512]{1,0:T(8,128)S(1)} %mul.10801) | copy-start | bytes 98308
  173.8 32.0 %copy-start.40 = (f32[16,512]{1,0:T(8,128)}, f32[16,512]{1,0:T(8,128)S(1)}, u32[]{:S(2)}) copy-start(f32[16,512]{1,0:T(8,128)S(1)} %mul.10814) | copy-start | bytes 98308
  173.8 32.0 %copy-start.42 = (f32[16,512]{1,0:T(8,128)}, f32[16,512]{1,0:T(8,128)S(1)}, u32[]{:S(2)}) copy-start(f32[16,512]{1,0:T(8,128)S(1)} %sub.1658) | copy-start | bytes 98308
  173.9 32.0 %copy-start.44 = (f32[16,512]{1,0:T(8,128)}, f32[16,512]{1,0:T(8,128)S(1)}, u32[]{:S(2)}) copy-start(f32[16,512]{1,0:T(8,128)S(1)} %mul.10809) | copy-start | bytes 98308
  173.9 32.0 %copy-start.46 = (f32[16,512]{1,0:T(8,128)}, f32[16,512]{1,0:T(8,128)S(1)}, u32[]{:S(2)}) copy-start(f32[16,512]{1,0:T(8,128)S(1)} %sub.1650) | copy-start | bytes 98308
  173.9 32.0 %copy-start.48 = (f32[16,512]{1,0:T(8,128)}, f32[16,512]{1,0:T(8,128)S(1)}, u32[]{:S(2)}) copy-start(f32[16,512]{1,0:T(8,128)S(1)} %mul.10803) | copy-start | bytes 98308
  173.9 14.0 %copy-start.50 = (f32[16,256]{1,0:T(8,128)S(1)}, f32[16,256]{1,0:T(8,128)}, u32[]{:S(2)}) copy-start(f32[16,256]{1,0:T(8,128)} %get-tuple-element.222) | copy-start | bytes 49156
  173.9 14.0 %copy-start.52 = (f32[16,256]{1,0:T(8,128)S(1)}, f32[16,256]{1,0:T(8,128)}, u32[]{:S(2)}) copy-start(f32[16,256]{1,0:T(8,128)} %get-tuple-element.223) | copy-start | bytes 49156
  173.9 14.0 %copy-start.54 = (pred[16,512]{1,0:T(8,128)(4,1)S(1)}, pred[16,512]{1,0:T(8,128)(4,1)}, u32[]{:S(2)}) copy-start(pred[16,512]{1,0:T(8,128)(4,1)} %iota_compare_fusion.1) | copy-start | bytes 24580
  188.0 17.9 %copy-start.59 = (f32[16,256,512]{2,1,0:T(8,128)}, f32[16,256,512]{2,1,0:T(8,128)S(1)}, u32[]{:S(2)}) copy-start(f32[16,256,512]{2,1,0:T(8,128)S(1)} %fusion.21) | copy-start | bytes 25165828
  339.0 7.2 %copy-start.11 = (f32[1,8192]{1,0:T(1,128)S(1)}, f32[1,8192]{1,0:T(1,128)}, u32[]{:S(2)}) copy-start(f32[1,8192]{1,0:T(1,128)} %copy-done.10) | copy-start | bytes 98308
  339.0 7.2 %copy-start.13 = (f32[1,8192]{1,0:T(1,128)S(1)}, f32[1,8192]{1,0:T(1,128)}, u32[]{:S(2)}) copy-start(f32[1,8192]{1,0:T(1,128)} %copy-done.12) | copy-start | bytes 98308
  339.0 7.2 %copy-start.15 = (f32[1,8192]{1,0:T(1,128)S(1)}, f32[1,8192]{1,0:T(1,128)}, u32[]{:S(2)}) copy-start(f32[1,8192]{1,0:T(1,128)} %copy-done.14) | copy-start | bytes 98308
  342.5 10.2 %copy-start.3 = (f32[1,8192]{1,0:T(1,128)S(1)}, f32[1,8192]{1,0:T(1,128)}, u32[]{:S(2)}) copy-start(f32[1,8192]{1,0:T(1,128)} %copy-done.2) | copy-start | bytes 98308
  342.5 10.2 %copy-start.5 = (f32[1,64,128]{2,1,0:T(8,128)S(1)}, f32[1,64,128]{2,1,0:T(8,128)}, u32[]{:S(2)}) copy-start(f32[1,64,128]{2,1,0:T(8,128)} %copy-done.4) | copy-start | bytes 98308
  342.5 10.2 %copy-start.7 = (f32[1,64,128]{2,1,0:T(8,128)S(1)}, f32[1,64,128]{2,1,0:T(8,128)}, u32[]{:S(2)}) copy-start(f32[1,64,128]{2,1,0:T(8,128)} %copy-done.6) | copy-start | bytes 98308
  346.0 11.0 %copy-start.8 = (f32[1,8192]{1,0:T(1,128)S(1)}, f32[1,8192]{1,0:T(1,128)}, u32[]{:S(2)}) copy-start(f32[1,8192]{1,0:T(1,128)} %get-tuple-element.114) | copy-start | bytes 98308
  346.0 11.0 %copy-start.9 = (f32[1,8192]{1,0:T(1,128)S(1)}, f32[1,8192]{1,0:T(1,128)}, u32[]{:S(2)}) copy-start(f32[1,8192]{1,0:T(1,128)} %get-tuple-element.115) | copy-start | bytes 98308
  346.0 11.0 %copy-start.32 = (f32[1,8192]{1,0:T(1,128)S(1)}, f32[1,8192]{1,0:T(1,128)}, u32[]{:S(2)}) copy-start(f32[1,8192]{1,0:T(1,128)} %get-tuple-element.102) | copy-start | bytes 98308
  346.0 11.0 %copy-start.33 = (f32[1,8192]{1,0:T(1,128)S(1)}, f32[1,8192]{1,0:T(1,128)}, u32[]{:S(2)}) copy-start(f32[1,8192]{1,0:T(1,128)} %get-tuple-element.103) | copy-start | bytes 98308
  348.4 10.3 %copy-start.27 = (f32[1,8192]{1,0:T(1,128)S(1)}, f32[1,8192]{1,0:T(1,128)}, u32[]{:S(2)}) copy-start(f32[1,8192]{1,0:T(1,128)} %get-tuple-element.107) | copy-start | bytes 98308
  348.4 10.3 %copy-start.28 = (f32[1,8192]{1,0:T(1,128)S(1)}, f32[1,8192]{1,0:T(1,128)}, u32[]{:S(2)}) copy-start(f32[1,8192]{1,0:T(1,128)} %get-tuple-element.108) | copy-start | bytes 98308
  348.4 10.3 %copy-start.29 = (f32[1,8192]{1,0:T(1,128)S(1)}, f32[1,8192]{1,0:T(1,128)}, u32[]{:S(2)}) copy-start(f32[1,8192]{1,0:T(1,128)} %get-tuple-element.112) | copy-start | bytes 98308
  348.4 10.3 %copy-start.30 = (f32[1,8192]{1,0:T(1,128)S(1)}, f32[1,8192]{1,0:T(1,128)}, u32[]{:S(2)}) copy-start(f32[1,8192]{1,0:T(1,128)} %get-tuple-element.113) | copy-start | bytes 98308
  348.4 10.3 %copy-start.31 = (f32[1,8192]{1,0:T(1,128)S(1)}, f32[1,8192]{1,0:T(1,128)}, u32[]{:S(2)}) copy-start(f32[1,8192]{1,0:T(1,128)} %get-tuple-element.116) | copy-start | bytes 98308
  350.1 9.1 %copy-start.25 = (f32[1,8192]{1,0:T(1,128)S(1)}, f32[1,8192]{1,0:T(1,128)}, u32[]{:S(2)}) copy-start(f32[1,8192]{1,0:T(1,128)} %fusion.49) | copy-start | bytes 98308
  428.1 46.6 %copy-start.39 = (f32[16,512]{1,0:T(8,128)S(1)}, f32[16,512]{1,0:T(8,128)}, u32[]{:S(2)}) copy-start(f32[16,512]{1,0:T(8,128)} %copy-done.38) | copy-start | bytes 98308
  428.1 46.6 %copy-start.41 = (f32[16,512]{1,0:T(8,128)S(1)}, f32[16,512]{1,0:T(8,128)}, u32[]{:S(2)}) copy-start(f32[16,512]{1,0:T(8,128)} %copy-done.40) | copy-start | bytes 98308
  428.1 46.6 %copy-start.43 = (f32[16,512]{1,0:T(8,128)S(1)}, f32[16,512]{1,0:T(8,128)}, u32[]{:S(2)}) copy-start(f32[16,512]{1,0:T(8,128)} %copy-done.42) | copy-start | bytes 98308
  428.2 46.7 %copy-start.45 = (f32[16,512]{1,0:T(8,128)S(1)}, f32[16,512]{1,0:T(8,128)}, u32[]{:S(2)}) copy-start(f32[16,512]{1,0:T(8,128)} %copy-done.44) | copy-start | bytes 98308
  428.2 46.7 %copy-start.47 = (f32[16,512]{1,0:T(8,128)S(1)}, f32[16,512]{1,0:T(8,128)}, u32[]{:S(2)}) copy-start(f32[16,512]{1,0:T(8,128)} %copy-done.46) | copy-start | bytes 98308
  428.2 46.7 %copy-start.49 = (f32[16,512]{1,0:T(8,128)S(1)}, f32[16,512]{1,0:T(8,128)}, u32[]{:S(2)}) copy-start(f32[16,512]{1,0:T(8,128)} %copy-done.48) | copy-start | bytes 98308
  428.2 46.7 %copy-start.51 = (f32[16,256]{1,0:T(8,128)S(1)}, f32[16,256]{1,0:T(8,128)}, u32[]{:S(2)}) copy-start(f32[16,256]{1,0:T(8,128)} %get-tuple-element.222) | copy-start | bytes 49156
  428.2 46.7 %copy-start.53 = (f32[16,256]{1,0:T(8,128)S(1)}, f32[16,256]{1,0:T(8,128)}, u32[]{:S(2)}) copy-start(f32[16,256]{1,0:T(8,128)} %get-tuple-element.223) | copy-start | bytes 49156
  428.2 46.7 %copy-start.55 = (pred[16,512]{1,0:T(8,128)(4,1)S(1)}, pred[16,512]{1,0:T(8,128)(4,1)}, u32[]{:S(2)}) copy-start(pred[16,512]{1,0:T(8,128)(4,1)} %iota_compare_fusion.1) | copy-start | bytes 24580
  474.9 96.1 %copy-start.1 = (f32[1,16,3,256]{3,1,2,0:T(8,128)S(1)}, f32[1,16,3,256]{3,1,2,0:T(8,128)}, u32[]{:S(2)}) copy-start(f32[1,16,3,256]{3,1,2,0:T(8,128)} %param.15) | copy-start | bytes 147460
  (15 other events, 72.0 us)
Sparse Core Ops, SparseCore 0:
  474.9 92.1 all-reduce.67
where the time goes:
time: 590 us; the launch traced here: 578 us
  local copies, waits for them, and re-layouts  157 us (27%)
  other arithmetic  129 us (22%)
  waiting for transfers between devices  116 us (20%)
  matrix products  72.7 us (12%)
  blocking collectives  56.5 us (10%)
  between operations  30 us (5%)
  starting transfers between devices  17 us (3%)
    psum x1, waiting for transfers between devices, per_device(): total = lax.psum(local_grad, 'view')  77.6 us
    all_to_all x1, blocking collectives, per_device(): lax.all_to_all(row_grad, 'space', split_axis=1, concat_axis=1, tiled=True)  56.5 us
    scatter-add x1, other arithmetic, per_device(): local_grad = jnp.zeros_like(gaussians).at[:, incoming].add(returned)  46.5 us
    scatter-add x1, other arithmetic, composite(): jnp.take(features, entries.reshape(-1), axis=1)  46.5 us
    dot_general x2, matrix products, composite(): before = jnp.einsum('tpk,kj->tpj', logs, triangle(span), precision=highest)  40.9 us
    unnamed x139, local copies, waits for them, and re-layouts  40.1 us
    another operation x3, local copies, waits for them, and re-layouts, project(): jnp.stack([screen_u, screen_v, cov_vv / determinant, -cov_uv / determinan...  38.9 us
    gather x2, local copies, waits for them, and re-layouts, composite(): jnp.take(features, entries.reshape(-1), axis=1)  35.6 us
  transfers between devices with their start and end apart: 3, of which 3 were waited for; matrix products, arithmetic and copies ran while one was open for 4% of the time, Pallas kernels for 0%

commit v1 on v0

v1 whole, which is shorter than its diff:
```python
import jax
import jax.numpy as jnp
from jax import lax
from jax.experimental import pallas as pl
from jax.experimental.pallas import tpu as pltpu
from jax.sharding import PartitionSpec as P

sh_zero = 0.28209479177387814
sh_one = 0.4886025119029199
sh_two = (
    1.0925484305920792,
    -1.0925484305920792,
    0.31539156525252005,
    -1.0925484305920792,
    0.5462742152960396,
)
sh_three = (
    -0.5900435899266435,
    2.890611442640554,
    -0.4570457994644658,
    0.3731763325901154,
    -0.4570457994644658,
    1.445305721320277,
    -0.5900435899266435,
)
dilation = 0.3 / 291600.0
log2e = 1.4426950408889634
unit = 1080.0
params_n = 59
feats = 9
owners = 64
slots = 8192
pitch = 72
half_rows = 296
vmem = pl.BlockSpec(memory_space=pltpu.VMEM)
smem = pl.BlockSpec(memory_space=pltpu.SMEM)
f32 = jnp.float32
bf16 = jnp.bfloat16


def quat_matrix(quat_w, quat_x, quat_y, quat_z):
    inv = 1.0 / jnp.sqrt(
        quat_w * quat_w + quat_x * quat_x + quat_y * quat_y + quat_z * quat_z
    )
    unit_w = quat_w * inv
    unit_x = quat_x * inv
    unit_y = quat_y * inv
    unit_z = quat_z * inv
    return [
        [
            1.0 - 2.0 * (unit_y * unit_y + unit_z * unit_z),
            2.0 * (unit_x * unit_y - unit_w * unit_z),
            2.0 * (unit_x * unit_z + unit_w * unit_y),
        ],
        [
            2.0 * (unit_x * unit_y + unit_w * unit_z),
            1.0 - 2.0 * (unit_x * unit_x + unit_z * unit_z),
            2.0 * (unit_y * unit_z - unit_w * unit_x),
        ],
        [
            2.0 * (unit_x * unit_z - unit_w * unit_y),
            2.0 * (unit_y * unit_z + unit_w * unit_x),
            1.0 - 2.0 * (unit_x * unit_x + unit_y * unit_y),
        ],
    ]


def sh_basis(dir_x, dir_y, dir_z):
    sq_x = dir_x * dir_x
    sq_y = dir_y * dir_y
    sq_z = dir_z * dir_z
    return [
        sh_zero,
        -sh_one * dir_y,
        sh_one * dir_z,
        -sh_one * dir_x,
        sh_two[0] * dir_x * dir_y,
        sh_two[1] * dir_y * dir_z,
        sh_two[2] * (2.0 * sq_z - sq_x - sq_y),
        sh_two[3] * dir_x * dir_z,
        sh_two[4] * (sq_x - sq_y),
        sh_three[0] * dir_y * (3.0 * sq_x - sq_y),
        sh_three[1] * dir_x * dir_y * dir_z,
        sh_three[2] * dir_y * (4.0 * sq_z - sq_x - sq_y),
        sh_three[3] * dir_z * (2.0 * sq_z - 3.0 * sq_x - 3.0 * sq_y),
        sh_three[4] * dir_x * (4.0 * sq_z - sq_x - sq_y),
        sh_three[5] * dir_z * (sq_x - sq_y),
        sh_three[6] * dir_x * (sq_x - 3.0 * sq_y),
    ]


def shape_matrix(params):
    scales = [jnp.exp(params[3]), jnp.exp(params[4]), jnp.exp(params[5])]
    own_rot = quat_matrix(params[6], params[7], params[8], params[9])
    return [[own_rot[i][k] * scales[k] for k in range(3)] for i in range(3)]


def view_values(camera):
    view_rot = quat_matrix(camera[0], camera[1], camera[2], camera[3])
    offset_cam = [camera[4], camera[5], camera[6]]
    back = [sum(view_rot[j][i] * offset_cam[j] for j in range(3)) for i in range(3)]
    return view_rot, offset_cam, camera[7], back


def project(params, shaped, view):
    view_rot, offset_cam, focal_len, back = view
    center = [params[0], params[1], params[2]]
    in_camera = [
        sum(view_rot[i][j] * center[j] for j in range(3)) + offset_cam[i] for i in range(3)
    ]
    turned = [
        [sum(view_rot[i][j] * shaped[j][k] for j in range(3)) for k in range(3)] for i in range(3)
    ]
    inv_depth = 1.0 / in_camera[2]
    near = focal_len * inv_depth
    screen_u = near * in_camera[0]
    screen_v = near * in_camera[1]
    slope_u = screen_u * inv_depth
    slope_v = screen_v * inv_depth
    jac_u = [near * turned[0][k] - slope_u * turned[2][k] for k in range(3)]
    jac_v = [near * turned[1][k] - slope_v * turned[2][k] for k in range(3)]
    cov_uu = sum(jac_u[k] * jac_u[k] for k in range(3)) + dilation
    cov_uv = sum(jac_u[k] * jac_v[k] for k in range(3))
    cov_vv = sum(jac_v[k] * jac_v[k] for k in range(3)) + dilation
    inv_det = 1.0 / (cov_uu * cov_vv - cov_uv * cov_uv)
    toward = [center[i] + back[i] for i in range(3)]
    inv_len = 1.0 / jnp.sqrt(
        toward[0] * toward[0] + toward[1] * toward[1] + toward[2] * toward[2]
    )
    basis = sh_basis(toward[0] * inv_len, toward[1] * inv_len, toward[2] * inv_len)
    colors = [0.5 + sum(basis[k] * params[11 + 3 * k + h] for k in range(16)) for h in range(3)]
    return [
        screen_u,
        screen_v,
        cov_vv * inv_det,
        -cov_uv * inv_det,
        cov_uu * inv_det,
    ] + colors


def log_opacity(logit):
    return jnp.minimum(logit, 0.0) - jnp.log1p(jnp.exp(-jnp.abs(logit)))


def pieces(value, count):
    out = []
    for _ in range(count - 1):
        top = value.astype(bf16).astype(f32)
        out.append(top)
        value = value - top
    out.append(value.astype(bf16).astype(f32))
    return out


def iota(shape, axis):
    return lax.broadcasted_iota(jnp.int32, shape, axis)


def spread_rows(gauss_ref, spread):
    def step(tile, carry):
        column = pl.ds(pl.multiple_of(tile * 128, 128), 128)
        row = pl.multiple_of(tile * pitch, 8)
        spread[pl.ds(row, 56), :] = gauss_ref[0:56, column]
        spread[pl.ds(row + 56, 3), :] = gauss_ref[56:59, column]
        return carry

    lax.fori_loop(0, 64, step, 0, unroll=4)


def order_kernel(requests_ref, lists_ref, out_ref, turned):
    lists = lists_ref[...].astype(f32)
    turned[...] = jnp.concatenate([lists, jnp.zeros((112, 512), f32)], axis=0).T
    group = iota((64, 128), 1) // 16
    entry = jnp.zeros((64, 128), f32)
    for j in range(8):
        piece = turned[pl.ds(j, 64, stride=8), :]
        if j:
            piece = pltpu.roll(piece, 16 * j, 1)
        entry = jnp.where(group == j, piece, entry)
    place = entry.astype(jnp.int32) & 127
    out_ref[...] = jnp.take_along_axis(requests_ref[...], place, axis=1)


def camera_values(table_ref, view_ref):
    row = view_ref[0]
    return [jnp.full((8, 128), table_ref[row, i], f32) for i in range(8)]


def project_kernel(table_ref, view_ref, gauss_ref, out_ref, spread, held):
    view = view_values(camera_values(table_ref, view_ref))
    spread_rows(gauss_ref, spread)

    def step(i, carry):
        params = [
            spread[pl.ds(i * (8 * pitch) + p, 8, stride=pitch), :] for p in range(params_n)
        ]
        out = project(params, shape_matrix(params), view)
        out = out[:5] + [log_opacity(params[10])] + out[5:]
        for f in range(feats):
            held[f, pl.ds(pl.multiple_of(i * 8, 8), 8), :] = out[f]
        return carry

    lax.fori_loop(0, 8, step, 0)
    for f in range(feats):
        for part, value in enumerate(pieces(held[f], 3)):
            row = (part * feats + f) * 32
            out_ref[row : row + 32, 0:128] = value[0:32].astype(bf16)
            out_ref[row : row + 32, 128:256] = value[32:64].astype(bf16)


def slot_hot(index):
    place = (index >> 12) * 128 + (index & 127)
    return (iota((256, index.shape[1]), 0) == place).astype(f32).astype(bf16)


def pick_kernel(index_ref, table_ref, out_ref, held):
    table = table_ref[...]

    def step(pair, carry):
        index = jnp.concatenate(
            [index_ref[pl.ds(2 * pair, 1), :], index_ref[pl.ds(2 * pair + 1, 1), :]], axis=1
        )
        got = jnp.dot(table, slot_hot(index), preferred_element_type=f32)
        rows = feats * 32
        got = got[0:rows] + got[rows : 2 * rows] + got[2 * rows : 3 * rows]
        level = (index >> 7) & 31
        keep = iota((32, 256), 0) == level
        for f in range(feats):
            value = jnp.sum(jnp.where(keep, got[32 * f : 32 * f + 32], 0.0), axis=0, keepdims=True)
            held[f, pl.ds(2 * pair, 1), :] = value[:, 0:128]
            held[f, pl.ds(2 * pair + 1, 1), :] = value[:, 128:256]
        return carry

    lax.fori_loop(0, 32, step, 0)
    for f in range(feats):
        out_ref[pl.ds(f, 64, stride=feats), :] = held[f]


def place_kernel(table_ref, view_ref, index_ref, grad_ref, out_ref, total):
    total[...] = jnp.zeros_like(total)
    rows = feats * 32

    def step(pair, carry):
        index = jnp.concatenate(
            [index_ref[pl.ds(2 * pair, 1), :], index_ref[pl.ds(2 * pair + 1, 1), :]], axis=1
        )
        level = (index >> 7) & 31
        keep = iota((32, 256), 0) == level
        parts = [[], []]
        for f in range(feats):
            value = jnp.concatenate(
                [
                    grad_ref[pl.ds(2 * pair * feats + f, 1), :],
                    grad_ref[pl.ds((2 * pair + 1) * feats + f, 1), :],
                ],
                axis=1,
            )
            for part, piece in enumerate(pieces(value, 2)):
                parts[part].append(jnp.where(keep, piece, 0.0).astype(bf16))
        hot = slot_hot(index)
        for part in parts:
            total[...] += lax.dot_general(
                jnp.concatenate(part, axis=0),
                hot,
                (((1,), (1,)), ((), ())),
                preferred_element_type=f32,
            )
        return carry

    lax.fori_loop(0, 32, step, 0)
    lane = iota((8, 128), 1)
    camera = jnp.zeros((8, 128), f32)
    for i in range(8):
        camera = jnp.where(lane == i, table_ref[view_ref[0], i], camera)
    for half in range(2):
        row = half * half_rows
        out_ref[row : row + rows, :] = total[:, 128 * half : 128 * half + 128]
        out_ref[row + rows : row + rows + 8, :] = camera


def render_kernel(
    plan_ref, length_ref, rows_ref, cot_ref, image_ref, out_ref, coef, turned, alphas, weights, moments, shades
):
    lane_tile = iota((8, 128), 1) & 15
    lane_step = iota((8, 128), 1) >> 4
    center_u = jnp.zeros((8, 128), f32)
    center_v = jnp.zeros((8, 128), f32)
    length = jnp.zeros((8, 128), jnp.int32)
    for t in range(16):
        tile = plan_ref[0, t]
        down = tile // 120
        across = tile - down * 120
        at_u = (across * 16 + 8 - 960).astype(f32)
        at_v = (down * 16 + 8 - 540).astype(f32)
        center_u = jnp.where(lane_tile == t, at_u, center_u)
        center_v = jnp.where(lane_tile == t, at_v, center_v)
        length = jnp.where(lane_tile == t, length_ref[0, t], length)
    center_u = center_u / 540.0
    center_v = center_v / 540.0

    def feature(i, f):
        return rows_ref[pl.ds(i * (8 * feats) + f, 8, stride=feats), :]

    coef[...] = jnp.zeros_like(coef)

    def prepare(i, carry):
        off_u = (feature(i, 0) - center_u) * unit
        off_v = (feature(i, 1) - center_v) * unit
        quad_u = feature(i, 2) * (-0.5 * log2e / (unit * unit))
        quad_m = feature(i, 3) * (-log2e / (unit * unit))
        quad_v = feature(i, 4) * (-0.5 * log2e / (unit * unit))
        lead = quad_u * off_u + quad_m * off_v
        base = off_u * lead + quad_v * off_v * off_v + feature(i, 5) * log2e
        alive = (iota((8, 128), 0) + 8 * i) * 8 + lane_step < length
        values = [
            jnp.where(alive, base, -30000.0),
            jnp.where(alive, -(lead + quad_u * off_u), 0.0),
            jnp.where(alive, -(2.0 * quad_v * off_v + quad_m * off_u), 0.0),
            jnp.where(alive, quad_u, 0.0),
            jnp.where(alive, quad_m, 0.0),
            jnp.where(alive, quad_v, 0.0),
            feature(i, 6),
            feature(i, 7),
            feature(i, 8),
        ]
        for m, value in enumerate(values):
            coef[pl.ds(i * 128 + m, 8, stride=16), :] = value
        return carry

    lax.fori_loop(0, 8, prepare, 0)

    def monomials(shape):
        row = iota(shape, 0) & 15
        pixel = iota(shape, 1)
        at_x = ((pixel & 15) * 2 - 15).astype(f32)
        at_y = ((pixel >> 4) * 2 - 15).astype(f32)
        out = jnp.where(row == 0, 1.0, 0.0)
        out = jnp.where(row == 1, at_x, out)
        out = jnp.where(row == 2, at_y, out)
        out = jnp.where(row == 3, at_x * at_x, out)
        out = jnp.where(row == 4, at_x * at_y, out)
        return jnp.where(row == 5, at_y * at_y, out)

    terms = jnp.where(iota((64, 256), 0) >= 16, monomials((64, 256)), 0.0).astype(bf16)
    moment_terms = monomials((16, 256)).astype(bf16)
    cots = [cot_ref[h] for h in range(3)]
    cot_parts = [pieces(cot, 2) for cot in cots]
    cot_high = jnp.concatenate([p[0] for p in cot_parts], axis=0).astype(bf16)
    cot_low = jnp.concatenate([p[1] for p in cot_parts], axis=0).astype(bf16)
    cot_both = jnp.concatenate([cot_high, cot_low], axis=0)
    same_tile = (iota((48, 256), 0) & 15) == (iota((48, 256), 1) & 15)
    across = (((1,), (1,)), ((), ()))

    def forward(i, clear):
        blocks = []
        for own in range(2):
            raw = coef[pl.ds(pl.multiple_of(i * 32 + own * 16, 16), 16), :]
            blocks.append(jnp.concatenate([raw] + pieces(raw, 3), axis=0).T)
        block = jnp.concatenate(blocks, axis=0)
        base = pl.multiple_of(i * 256, 256)
        turned[pl.ds(base, 256), :] = block
        power = jnp.dot(block.astype(bf16), terms, preferred_element_type=f32)
        alpha = jnp.exp2(power)
        alphas[pl.ds(base, 256), :] = alpha
        pieces_w = []
        for k in range(16):
            weight = alpha[16 * k : 16 * k + 16] * clear
            clear = clear - weight
            pieces_w.append(weight)
        weight = jnp.concatenate(pieces_w, axis=0)
        weights[pl.ds(base, 256), :] = weight
        top = weight.astype(bf16)
        low = (weight - top.astype(f32)).astype(bf16)
        both = lax.dot_general(cot_both, top, across, preferred_element_type=f32)
        shade = both[0:48] + both[48:96]
        shade += lax.dot_general(cot_high, low, across, preferred_element_type=f32)
        shade = jnp.where(same_tile, shade, 0.0)
        for h in range(3):
            value = jnp.sum(shade[16 * h : 16 * h + 16], axis=0, keepdims=True)
            for own in range(2):
                shades[h, pl.ds(2 * i + own, 1), :] = value[:, 128 * own : 128 * own + 128]
        return clear

    lax.fori_loop(0, 32, forward, jnp.ones((16, 256), f32))

    def backward(step, behind):
        i = 31 - step
        base = pl.multiple_of(i * 256, 256)
        behind = list(behind)
        pieces_d = [None] * 16
        for k in range(15, -1, -1):
            rows = pl.ds(base + 16 * k, 16)
            alpha = alphas[rows, :]
            pull = None
            for h in range(3):
                gap = turned[rows, 6 + h : 7 + h] - behind[h]
                behind[h] = behind[h] + alpha * gap
                pull = cots[h] * gap if pull is None else pull + cots[h] * gap
            pieces_d[k] = weights[rows, :] * pull
        slope = jnp.concatenate(pieces_d, axis=0)
        top = slope.astype(bf16)
        low = (slope - top.astype(f32)).astype(bf16)
        moment = lax.dot_general(moment_terms, top, across, preferred_element_type=f32)
        moment += lax.dot_general(moment_terms, low, across, preferred_element_type=f32)
        for own in range(2):
            moments[pl.ds(pl.multiple_of(i * 32 + own * 16, 16), 16), :] = moment[
                :, 128 * own : 128 * own + 128
            ]
        return tuple(behind)

    blank = jnp.zeros((16, 256), f32)
    image = lax.fori_loop(0, 32, backward, (blank, blank, blank))
    for h in range(3):
        image_ref[h] = image[h]

    def finish(i, carry):
        off_u = (feature(i, 0) - center_u) * unit
        off_v = (feature(i, 1) - center_v) * unit
        m_one, m_x, m_y, m_xx, m_xy, m_yy = [
            moments[pl.ds(i * 128 + m, 8, stride=16), :] for m in range(6)
        ]
        n_x = m_x - off_u * m_one
        n_y = m_y - off_v * m_one
        n_xx = m_xx - off_u * (m_x + n_x)
        n_xy = m_xy - off_u * m_y - off_v * n_x
        n_yy = m_yy - off_v * (m_y + n_y)
        values = [
            (feature(i, 2) * n_x + feature(i, 3) * n_y) * (1.0 / unit),
            (feature(i, 3) * n_x + feature(i, 4) * n_y) * (1.0 / unit),
            n_xx * (-0.5 / (unit * unit)),
            n_xy * (-1.0 / (unit * unit)),
            n_yy * (-0.5 / (unit * unit)),
            m_one,
        ]
        for h in range(3):
            values.append(shades[h, pl.ds(pl.multiple_of(i * 8, 8), 8), :])
        for f, value in enumerate(values):
            out_ref[pl.ds(i * (8 * feats) + f, 8, stride=feats), :] = value
        return carry

    lax.fori_loop(0, 8, finish, 0)


def gradient_kernel(gauss_ref, own_ref, left_ref, right_ref, far_low_ref, far_high_ref, out_ref, spread, held):
    spread_rows(gauss_ref, spread)
    for half in range(2):
        far_ref = (far_low_ref, far_high_ref)[half]
        sources = [
            (own_ref, half * half_rows),
            (left_ref, half * half_rows),
            (right_ref, half * half_rows),
            (far_ref, 0),
        ]
        views = []
        for ref, base in sources:
            line = ref[base + feats * 32 : base + feats * 32 + 8, :]
            views.append(
                view_values([jnp.broadcast_to(line[:, i : i + 1], (8, 128)) for i in range(8)])
            )

        def step(i, carry):
            at = (i + 4 * half) * (8 * pitch)
            params = [spread[pl.ds(at + p, 8, stride=pitch), :] for p in range(params_n)]

            def every(*params):
                shaped = shape_matrix(params)
                out = []
                for view in views:
                    out += project(params, shaped, view)
                return out + [log_opacity(params[10])]

            _, back = jax.vjp(every, *params)
            cots = []
            opaque = None
            for ref, base in sources:
                rows = [ref[pl.ds(base + 32 * f + 8 * i, 8), :] for f in range(feats)]
                cots += rows[:5] + rows[6:]
                opaque = rows[5] if opaque is None else opaque + rows[5]
            grads = back(cots + [opaque])
            for p in range(params_n):
                held[pl.ds(at + p, 8, stride=pitch), :] = grads[p]
            return carry

        lax.fori_loop(0, 4, step, 0)

    def collect(tile, carry):
        column = pl.ds(pl.multiple_of(tile * 128, 128), 128)
        row = pl.multiple_of(tile * pitch, 8)
        out_ref[0:56, column] = held[pl.ds(row, 56), :]
        out_ref[56:59, column] = held[pl.ds(row + 56, 3), :]
        return carry

    lax.fori_loop(0, 64, collect, 0, unroll=4)


def call(kernel, out, args, specs, scratch, limit=48):
    return pl.pallas_call(
        kernel,
        out_shape=out,
        in_specs=specs,
        out_specs=jax.tree.map(lambda _: vmem, out),
        scratch_shapes=scratch,
        compiler_params=pltpu.CompilerParams(vmem_limit_bytes=limit * 1024 * 1024),
    )(*args)


def exchange(rows, width):
    parts = rows.reshape(owners, width, 1, 128)
    parts = lax.all_to_all(parts, "space", split_axis=0, concat_axis=0, tiled=True)
    return parts.reshape(owners * width, 128)


def per_device(
    gaussians, camera_table, view_camera, tile_plan, requests, tile_lists, tile_lengths, pixel_grad
):
    shape = jax.ShapeDtypeStruct
    ordered = call(
        order_kernel,
        shape((64, 128), jnp.int32),
        (requests[0, 0], tile_lists[0]),
        [vmem, vmem],
        [pltpu.VMEM((512, 128), f32)],
    )
    incoming = exchange(ordered, 1)
    spread = pltpu.VMEM((64 * pitch, 128), f32)
    table = call(
        project_kernel,
        shape((3 * feats * 32, 256), bf16),
        (camera_table, view_camera, gaussians),
        [smem, smem, vmem],
        [spread, pltpu.VMEM((feats, 64, 128), f32)],
    )
    picked = call(
        pick_kernel,
        shape((64 * feats, 128), f32),
        (incoming, table),
        [vmem, vmem],
        [pltpu.VMEM((feats, 64, 128), f32)],
    )
    arrived = exchange(picked, feats)
    image, row_grad = call(
        render_kernel,
        (shape((3, 16, 256), f32), shape((64 * feats, 128), f32)),
        (tile_plan, tile_lengths, arrived, jnp.transpose(pixel_grad[0], (1, 0, 2))),
        [smem, smem, vmem, vmem],
        [
            pltpu.VMEM((1024, 128), f32),
            pltpu.VMEM((8192, 64), f32),
            pltpu.VMEM((8192, 256), f32),
            pltpu.VMEM((8192, 256), f32),
            pltpu.VMEM((1024, 128), f32),
            pltpu.VMEM((3, 64, 128), f32),
        ],
    )
    returned = exchange(row_grad, feats)
    own = call(
        place_kernel,
        shape((2 * half_rows, 128), f32),
        (camera_table, view_camera, incoming, returned),
        [smem, smem, vmem, vmem],
        [pltpu.VMEM((feats * 32, 256), f32)],
    )
    ahead = [(i, (i + 1) % 4) for i in range(4)]
    behind = [(i, (i - 1) % 4) for i in range(4)]
    left = lax.ppermute(own, "view", ahead)
    right = lax.ppermute(own, "view", behind)
    far_low = lax.ppermute(left[:half_rows], "view", ahead)
    far_high = lax.ppermute(right[half_rows:], "view", behind)
    total = call(
        gradient_kernel,
        shape((params_n, slots), f32),
        (gaussians, own, left, right, far_low, far_high),
        [vmem] * 6,
        [spread, spread],
    )
    return (jnp.transpose(image, (1, 0, 2))[None], total)


def solution(mesh):
    placed = (
        P(None, "space"),
        P(),
        P("view"),
        P("view", "space"),
        P("view", "space", None, None),
        P("view", "space", None),
        P("view", "space"),
        P("view", "space", None, None),
    )
    return jax.shard_map(
        per_device,
        mesh=mesh,
        in_specs=placed,
        out_specs=(P("view", "space", None, None), P(None, "space")),
        check_vma=False,
    )
```

time: 590 us -> 135 us (0.23); the launches traced: 578 us -> 133 us
  local copies, waits for them, and re-layouts: 157 us -> 3.91 us
  other arithmetic: 129 us -> 0 us
  waiting for transfers between devices: 116 us -> 15.5 us
  matrix products: 72.7 us -> 0 us
  Pallas kernels: 0 us -> 56.5 us
  between operations: 30 us -> 1.37 us
  blocking collectives: 56.5 us -> 37.1 us
    scatter-add x2 -> x0, other arithmetic: 93 us -> none  [the longest x1 46.5 us: per_device(): local_grad = jnp.zeros_like(gaussians).at[:, incoming].add(returned)]
    psum x1 -> x0, waiting for transfers between devices: 77.6 us -> none  [per_device(): total = lax.psum(local_grad, 'view')]
    dot_general x5 -> x0, matrix products: 72.7 us -> none  [the longest x2 40.9 us: composite(): before = jnp.einsum('tpk,kj->tpj', logs, triangle(span), precision=highest)]
    gather x4 -> x0, local copies, waits for them, and re-layouts: 68.6 us -> none  [the longest x2 35.6 us: composite(): jnp.take(features, entries.reshape(-1), axis=1)]
    pallas_call x0 -> x6, Pallas kernels: none -> 56.5 us  [call(): pl.pallas_call(kernel, out_shape=out, in_specs=specs, out_specs=jax.tree....]
    another operation x3 -> x0, local copies, waits for them, and re-layouts: 38.9 us -> none  [project(): jnp.stack([screen_u, screen_v, cov_vv / determinant, -cov_uv / determinan...]
    unnamed x139 -> x15, local copies, waits for them, and re-layouts: 40.1 us -> 3.89 us
    all_to_all x2 -> x1, waiting for transfers between devices: 38.4 us -> 4.79 us  [exchange(): lax.all_to_all(parts, 'space', split_axis=0, concat_axis=0, tiled=True)]
  transfers between devices with their start and end apart: 3 -> 5, of which waited for: 3 -> 3; matrix products, arithmetic and copies ran while one was open for 4% -> 1% of each run, Pallas kernels for 0% -> 1%
where the time goes in v1:
time: 135 us; the launch traced here: 133 us
  Pallas kernels  56.5 us (42%)
  blocking collectives  37.1 us (27%)
  starting transfers between devices  18.8 us (14%)
  waiting for transfers between devices  15.5 us (11%)
  local copies, waits for them, and re-layouts  3.91 us (3%)
  between operations  1.37 us (1%)
    pallas_call x6, Pallas kernels, call(): pl.pallas_call(kernel, out_shape=out, in_specs=specs, out_specs=jax.tree....  56.5 us
    all_to_all x2, blocking collectives, exchange(): lax.all_to_all(parts, 'space', split_axis=0, concat_axis=0, tiled=True)  37.1 us
    all_to_all x1, starting transfers between devices, exchange(): lax.all_to_all(parts, 'space', split_axis=0, concat_axis=0, tiled=True)  12.1 us
    ppermute x1, waiting for transfers between devices, per_device(): right = lax.ppermute(own, 'view', behind)  7.42 us
    all_to_all x1, waiting for transfers between devices, exchange(): lax.all_to_all(parts, 'space', split_axis=0, concat_axis=0, tiled=True)  4.79 us
    unnamed x15, local copies, waits for them, and re-layouts  3.89 us
    ppermute x1, starting transfers between devices, per_device(): far_low = lax.ppermute(left[:half_rows], 'view', ahead)  3.29 us
    ppermute x1, waiting for transfers between devices, per_device(): far_high = lax.ppermute(right[half_rows:], 'view', behind)  3.28 us
  transfers between devices with their start and end apart: 5, of which 3 were waited for; matrix products, arithmetic and copies ran while one was open for 1% of the time, Pallas kernels for 1%

profile of v1, /device:TPU:6, one launch (start us, length us, event | category | flops | bytes accessed | tf_op | source)
XLA Modules:
  0.0 133.2 jit_solution(17709947587999623677)
XLA Ops:
  0.6 0.0 copy-start.2
  0.6 0.0 copy-start.3
  0.7 0.8 copy-done.3
  1.4 0.0 copy-start.4
  1.4 0.8 copy-done.4
  2.2 0.0 copy-start.5
  2.2 0.0 copy-start.6
  2.2 1.0 shard_map.95
  3.1 12.1 %all-to-all-start = ((s32[64,1,1,128]{3,2,1,0:T(1,128)}), s32[64,1,1,128]{3,2,1,0:T(1,128)S(1)}, u32[]{:S(2)}, u32[]{:S(2)}) async-start(s32[64,1,1,128]{3,2,1,0:T(1,128)} %bitcast.3), calls=%async_computation | async-start | bytes 65536 | tf_op jit(solution)/shard_map/all_to_all | solution.py:509
  15.9 0.8 copy.15.table_ref
  16.7 0.0 copy-start
  16.7 1.6 %copy-done = f32[59,8192]{1,0:T(8,128)S(1)} copy-done((f32[59,8192]{1,0:T(8,128)S(1)}, f32[59,8192]{1,0:T(8,128)}, u32[]{:S(2)}) %copy-start) | copy-done | bytes 1933336
  18.3 1.7 %shard_map.96.table_ref = bf16[864,256]{1,0:T(8,128)(2,1)S(1)} custom-call(f32[16,8]{1,0:T(8,128)S(1)} %copy.15.table_ref, s32[1]{0:T(128)S(6)} %copy.19.view_ref, f32[59,8192]{1,0:T(8,128)S(1)} %copy-done), custom_call_target="tpu_custom_call" | custom-call | tf_op jit(solution)/shard_map/pallas_call | solution.py:497
  20.0 0.0 copy-start.1
  20.0 4.8 %all-to-all-done = s32[64,1,1,128]{3,2,1,0:T(1,128)S(1)} async-done(((s32[64,1,1,128]{3,2,1,0:T(1,128)}), s32[64,1,1,128]{3,2,1,0:T(1,128)S(1)}, u32[]{:S(2)}, u32[]{:S(2)}) %all-to-all-start) | async-done | bytes 32800 | tf_op jit(solution)/shard_map/all_to_all | solution.py:509
  24.8 9.9 %shard_map.97 = f32[576,128]{1,0:T(8,128)S(1)} custom-call(s32[64,128]{1,0:T(8,128)S(1)} %bitcast.19, bf16[864,256]{1,0:T(8,128)(2,1)S(1)} %shard_map.96.table_ref), custom_call_target="tpu_custom_call" | custom-call | tf_op jit(solution)/shard_map/pallas_call | solution.py:497
  34.7 18.7 %all_to_all.15 = f32[64,9,1,128]{3,2,1,0:T(1,128)S(1)} all-to-all(f32[64,9,1,128]{3,2,1,0:T(1,128)S(1)} %bitcast.16), channel_id=1, replica_groups=mesh['space'=64,'view'=4] {'space'}, dimensions={0} | all-to-all | bytes 589824 | tf_op jit(solution)/shard_map/all_to_all | solution.py:509
  53.4 0.0 copy-done.2
  53.4 0.0 copy-done.5
  53.4 0.0 copy-done.6
  53.4 28.4 %shard_map.98 = (f32[3,16,256]{2,1,0:T(8,128)}, f32[576,128]{1,0:T(8,128)S(1)}) custom-call(s32[1,16]{1,0:T(1,128)S(1)} %copy-done.5, s32[1,16]{1,0:T(1,128)S(1)} %copy-done.6, f32[576,128]{1,0:T(8,128)S(1)} %bitcast.18, f32[3,16,256]{2,1,0:T(8,128)S(1)} %bitcast.22), custom_call_target="tpu_custom_call" | custom-call | tf_op jit(solution)/shard_map/pallas_call | solution.py:497
  81.9 18.4 %all_to_all.16 = f32[64,9,1,128]{3,2,1,0:T(1,128)S(1)} all-to-all(f32[64,9,1,128]{3,2,1,0:T(1,128)S(1)} %bitcast.21), channel_id=1, replica_groups=mesh['space'=64,'view'=4] {'space'}, dimensions={0} | all-to-all | bytes 589824 | tf_op jit(solution)/shard_map/all_to_all | solution.py:509
  100.2 9.9 %shard_map.99.own_ref = f32[592,128]{1,0:T(8,128)S(1)} custom-call(f32[16,8]{1,0:T(8,128)S(1)} %copy.15.table_ref, s32[1]{0:T(128)S(6)} %copy.19.view_ref, s32[64,128]{1,0:T(8,128)S(1)} %bitcast.20, f32[576,128]{1,0:T(8,128)S(1)} %bitcast.17), custom_call_target="tpu_custom_call" | custom-call | tf_op jit(solution)/shard_map/pallas_call | solution.py:497
  110.2 0.9 collective-permute-start.1
  111.1 2.4 %collective-permute-start = (f32[592,128]{1,0:T(8,128)S(1)}, f32[592,128]{1,0:T(8,128)S(1)}, u32[]{:S(2)}, u32[]{:S(2)}) collective-permute-start(f32[592,128]{1,0:T(8,128)S(1)} %shard_map.99.own_ref), channel_id=1, source_target_pairs={{0,1},{1,2},{2,3},{3,0},{4,5},{5,6},{6,7},{7,4},{8,9},{9,10},{10,1... | collective-permute-start | bytes 909320 | tf_op jit(solution)/shard_map/ppermute | solution.py:565
  113.5 7.4 %collective-permute-done.1.right_ref = f32[592,128]{1,0:T(8,128)S(1)} collective-permute-done((f32[592,128]{1,0:T(8,128)S(1)}, f32[592,128]{1,0:T(8,128)S(1)}, u32[]{:S(2)}, u32[]{:S(2)}) %collective-permute-start.1) | collective-permute-done | bytes 303136 | tf_op jit(solution)/shard_map/ppermute | solution.py:566
  120.9 0.1 collective-permute-start.3
  121.0 0.0 collective-permute-done.left_ref
  121.0 3.3 %collective-permute-start.2 = (f32[296,128]{1,0:T(8,128)S(1)}, f32[296,128]{1,0:T(8,128)S(1)}, u32[]{:S(2)}, u32[]{:S(2)}) collective-permute-start(f32[296,128]{1,0:T(8,128)S(1)} %slice.8), channel_id=1, source_target_pairs={{0,1},{1,2},{2,3},{3,0},{4,5},{5,6},{6,7},{7,4},{8,9},{9,10},{10,1... | collective-permute-start | bytes 454664 | tf_op jit(solution)/shard_map/ppermute | solution.py:567
  124.3 3.3 %collective-permute-done.3.far_high_ref = f32[296,128]{1,0:T(8,128)S(1)} collective-permute-done((f32[296,128]{1,0:T(8,128)S(1)}, f32[296,128]{1,0:T(8,128)S(1)}, u32[]{:S(2)}, u32[]{:S(2)}) %collective-permute-start.3) | collective-permute-done | bytes 151584 | tf_op jit(solution)/shard_map/ppermute | solution.py:568
  127.6 0.0 collective-permute-done.2.far_low_ref
  127.6 0.0 copy-done.1
  127.6 5.5 %shard_map.100 = f32[59,8192]{1,0:T(8,128)} custom-call(f32[59,8192]{1,0:T(8,128)S(1)} %copy-done.1, f32[592,128]{1,0:T(8,128)S(1)} %shard_map.99.own_ref, f32[592,128]{1,0:T(8,128)S(1)} %collective-permute-done.left_ref, f32[592,128]{1,0:T(8,128)S(1)} %collective-permute-done.1.right_ref, f32[296,128]{1,0:T(8,128)S(1)} %collective-permute-done.2.far_low_ref, ...), custom_call_target="tpu_custom_call" | custom-call | tf_op jit(solution)/shard_map/pallas_call | solution.py:497
  (2 shorter events, 0.0 us)
Async XLA Ops:
  0.6 52.8 %copy-start.2 = (f32[1,16,3,256]{3,1,2,0:T(8,128)S(1)}, f32[1,16,3,256]{3,1,2,0:T(8,128)}, u32[]{:S(2)}) copy-start(f32[1,16,3,256]{3,1,2,0:T(8,128)} %param.15) | copy-start | bytes 147460
  0.6 0.8 copy-start.3
  1.4 0.8 copy-start.4
  2.2 51.3 %copy-start.5 = (s32[1,16]{1,0:T(1,128)S(1)}, s32[1,16]{1,0:T(1,128)}, u32[]{:S(2)}) copy-start(s32[1,16]{1,0:T(1,128)} %plan_ref.1) | copy-start | bytes 196
  2.2 51.3 %copy-start.6 = (s32[1,16]{1,0:T(1,128)S(1)}, s32[1,16]{1,0:T(1,128)}, u32[]{:S(2)}) copy-start(s32[1,16]{1,0:T(1,128)} %length_ref.1) | copy-start | bytes 196
  3.1 21.6 %all-to-all-start = ((s32[64,1,1,128]{3,2,1,0:T(1,128)}), s32[64,1,1,128]{3,2,1,0:T(1,128)S(1)}, u32[]{:S(2)}, u32[]{:S(2)}) async-start(s32[64,1,1,128]{3,2,1,0:T(1,128)} %bitcast.3), calls=%async_computation | async-start | bytes 65536 | tf_op jit(solution)/shard_map/all_to_all | solution.py:509
  16.7 1.6 %copy-start = (f32[59,8192]{1,0:T(8,128)S(1)}, f32[59,8192]{1,0:T(8,128)}, u32[]{:S(2)}) copy-start(f32[59,8192]{1,0:T(8,128)} %gauss_ref.3) | copy-start | bytes 5799940
  20.0 107.6 %copy-start.1 = (f32[59,8192]{1,0:T(8,128)S(1)}, f32[59,8192]{1,0:T(8,128)}, u32[]{:S(2)}) copy-start(f32[59,8192]{1,0:T(8,128)} %gauss_ref.3) | copy-start | bytes 5799940
  110.2 10.8 %collective-permute-start.1 = (f32[592,128]{1,0:T(8,128)S(1)}, f32[592,128]{1,0:T(8,128)S(1)}, u32[]{:S(2)}, u32[]{:S(2)}) collective-permute-start(f32[592,128]{1,0:T(8,128)S(1)} %shard_map.99.own_ref), channel_id=1, source_target_pairs={{0,3},{1,0},{2,1},{3,2},{4,7},{5,4},{6,5},{7,6},{8,11},{9,8},{10,9... | collective-permute-start | bytes 909320 | tf_op jit(solution)/shard_map/ppermute | solution.py:566
  111.1 9.9 %collective-permute-start = (f32[592,128]{1,0:T(8,128)S(1)}, f32[592,128]{1,0:T(8,128)S(1)}, u32[]{:S(2)}, u32[]{:S(2)}) collective-permute-start(f32[592,128]{1,0:T(8,128)S(1)} %shard_map.99.own_ref), channel_id=1, source_target_pairs={{0,1},{1,2},{2,3},{3,0},{4,5},{5,6},{6,7},{7,4},{8,9},{9,10},{10,1... | collective-permute-start | bytes 909320 | tf_op jit(solution)/shard_map/ppermute | solution.py:565
  120.9 6.7 %collective-permute-start.3 = (f32[296,128]{1,0:T(8,128)S(1)}, f32[296,128]{1,0:T(8,128)S(1)}, u32[]{:S(2)}, u32[]{:S(2)}) collective-permute-start(f32[296,128]{1,0:T(8,128)S(1)} %slice.9), channel_id=1, source_target_pairs={{0,3},{1,0},{2,1},{3,2},{4,7},{5,4},{6,5},{7,6},{8,11},{9,8},{10,9... | collective-permute-start | bytes 454664 | tf_op jit(solution)/shard_map/ppermute | solution.py:568
  121.0 6.6 %collective-permute-start.2 = (f32[296,128]{1,0:T(8,128)S(1)}, f32[296,128]{1,0:T(8,128)S(1)}, u32[]{:S(2)}, u32[]{:S(2)}) collective-permute-start(f32[296,128]{1,0:T(8,128)S(1)} %slice.8), channel_id=1, source_target_pairs={{0,1},{1,2},{2,3},{3,0},{4,5},{5,6},{6,7},{7,4},{8,9},{9,10},{10,1... | collective-permute-start | bytes 454664 | tf_op jit(solution)/shard_map/ppermute | solution.py:567

commit v2 on v1

--- a/solution.py
+++ b/solution.py
@@ -32,6 +32,10 @@
 slots = 8192
 pitch = 72
 half_rows = 296
+lay_unroll = 4
+forward_unroll = 8
+backward_unroll = 8
+pick_unroll = 8
 vmem = pl.BlockSpec(memory_space=pltpu.VMEM)
 smem = pl.BlockSpec(memory_space=pltpu.SMEM)
 f32 = jnp.float32
@@ -90,8 +94,8 @@
 
 
 def shape_matrix(params):
-    scales = [jnp.exp(params[3]), jnp.exp(params[4]), jnp.exp(params[5])]
-    own_rot = quat_matrix(params[6], params[7], params[8], params[9])
+    scales = [jnp.exp(params[0]), jnp.exp(params[1]), jnp.exp(params[2])]
+    own_rot = quat_matrix(params[3], params[4], params[5], params[6])
     return [[own_rot[i][k] * scales[k] for k in range(3)] for i in range(3)]
 
 
@@ -102,9 +106,8 @@
     return view_rot, offset_cam, camera[7], back
 
 
-def project(params, shaped, view):
+def project(center, shaped, harmonics, view):
     view_rot, offset_cam, focal_len, back = view
-    center = [params[0], params[1], params[2]]
     in_camera = [
         sum(view_rot[i][j] * center[j] for j in range(3)) + offset_cam[i] for i in range(3)
     ]
@@ -128,7 +131,7 @@
         toward[0] * toward[0] + toward[1] * toward[1] + toward[2] * toward[2]
     )
     basis = sh_basis(toward[0] * inv_len, toward[1] * inv_len, toward[2] * inv_len)
-    colors = [0.5 + sum(basis[k] * params[11 + 3 * k + h] for k in range(16)) for h in range(3)]
+    colors = [0.5 + sum(basis[k] * harmonics[3 * k + h] for k in range(16)) for h in range(3)]
     return [
         screen_u,
         screen_v,
@@ -191,10 +194,12 @@
     spread_rows(gauss_ref, spread)
 
     def step(i, carry):
-        params = [
-            spread[pl.ds(i * (8 * pitch) + p, 8, stride=pitch), :] for p in range(params_n)
-        ]
-        out = project(params, shape_matrix(params), view)
+        at = i * (8 * pitch)
+        params = [spread[pl.ds(at + p, 8, stride=pitch), :] for p in range(params_n)]
+        shaped = shape_matrix(params[3:10])
+        for k in range(9):
+            spread[pl.ds(at + params_n + k, 8, stride=pitch), :] = shaped[k // 3][k % 3]
+        out = project(params[0:3], shaped, params[11:], view)
         out = out[:5] + [log_opacity(params[10])] + out[5:]
         for f in range(feats):
             held[f, pl.ds(pl.multiple_of(i * 8, 8), 8), :] = out[f]
@@ -202,7 +207,7 @@
 
     lax.fori_loop(0, 8, step, 0)
     for f in range(feats):
-        for part, value in enumerate(pieces(held[f], 3)):
+        for part, value in enumerate(pieces(held[f], 3 if f < 2 else 2)):
             row = (part * feats + f) * 32
             out_ref[row : row + 32, 0:128] = value[0:32].astype(bf16)
             out_ref[row : row + 32, 128:256] = value[32:64].astype(bf16)
@@ -213,73 +218,116 @@
     return (iota((256, index.shape[1]), 0) == place).astype(f32).astype(bf16)
 
 
-def pick_kernel(index_ref, table_ref, out_ref, held):
-    table = table_ref[...]
+def pick_rows(index_ref, table_ref, held, third):
+    rows = feats * 32
 
     def step(pair, carry):
         index = jnp.concatenate(
             [index_ref[pl.ds(2 * pair, 1), :], index_ref[pl.ds(2 * pair + 1, 1), :]], axis=1
         )
-        got = jnp.dot(table, slot_hot(index), preferred_element_type=f32)
-        rows = feats * 32
-        got = got[0:rows] + got[rows : 2 * rows] + got[2 * rows : 3 * rows]
+        got = jnp.dot(table_ref[...], slot_hot(index), preferred_element_type=f32)
         level = (index >> 7) & 31
         keep = iota((32, 256), 0) == level
         for f in range(feats):
-            value = jnp.sum(jnp.where(keep, got[32 * f : 32 * f + 32], 0.0), axis=0, keepdims=True)
-            held[f, pl.ds(2 * pair, 1), :] = value[:, 0:128]
-            held[f, pl.ds(2 * pair + 1, 1), :] = value[:, 128:256]
+            value = got[32 * f : 32 * f + 32] + got[rows + 32 * f : rows + 32 * f + 32]
+            if f < third:
+                value += got[2 * rows + 32 * f : 2 * rows + 32 * f + 32]
+            value = jnp.sum(jnp.where(keep, value, 0.0), axis=0, keepdims=True)
+            held(f, 2 * pair, value[:, 0:128])
+            held(f, 2 * pair + 1, value[:, 128:256])
         return carry
 
-    lax.fori_loop(0, 32, step, 0)
+    lax.fori_loop(0, index_ref.shape[0] // 2, step, 0, unroll=pick_unroll)
+
+
+def pick_kernel(index_ref, table_ref, out_ref, held):
+    def keep(f, row, value):
+        held[f, pl.ds(row, 1), :] = value
+
+    pick_rows(index_ref, table_ref, keep, 2)
     for f in range(feats):
         out_ref[pl.ds(f, 64, stride=feats), :] = held[f]
 
 
-def place_kernel(table_ref, view_ref, index_ref, grad_ref, out_ref, total):
+def inverse_kernel(index_ref, out_ref, total):
     total[...] = jnp.zeros_like(total)
-    rows = feats * 32
 
     def step(pair, carry):
         index = jnp.concatenate(
             [index_ref[pl.ds(2 * pair, 1), :], index_ref[pl.ds(2 * pair + 1, 1), :]], axis=1
         )
-        level = (index >> 7) & 31
-        keep = iota((32, 256), 0) == level
-        parts = [[], []]
-        for f in range(feats):
-            value = jnp.concatenate(
-                [
-                    grad_ref[pl.ds(2 * pair * feats + f, 1), :],
-                    grad_ref[pl.ds((2 * pair + 1) * feats + f, 1), :],
-                ],
-                axis=1,
-            )
-            for part, piece in enumerate(pieces(value, 2)):
-                parts[part].append(jnp.where(keep, piece, 0.0).astype(bf16))
-        hot = slot_hot(index)
-        for part in parts:
-            total[...] += lax.dot_general(
-                jnp.concatenate(part, axis=0),
-                hot,
-                (((1,), (1,)), ((), ())),
-                preferred_element_type=f32,
-            )
+        keep = iota((32, 256), 0) == ((index >> 7) & 31)
+        lane = iota((32, 256), 1)
+        row = (2 * pair + (lane >> 7)).astype(f32)
+        column = (lane & 127).astype(f32)
+        both = jnp.concatenate([jnp.where(keep, row, 0.0), jnp.where(keep, column, 0.0)], axis=0)
+        total[...] += lax.dot_general(
+            both.astype(bf16),
+            slot_hot(index),
+            (((1,), (1,)), ((), ())),
+            preferred_element_type=f32,
+        )
         return carry
 
-    lax.fori_loop(0, 32, step, 0)
+    lax.fori_loop(0, 32, step, 0, unroll=4)
+    spot = (total[0:32] * 128.0 + total[32:64]).astype(jnp.int32)
+    out_ref[0:32, :] = spot[:, 0:128]
+    out_ref[32:64, :] = spot[:, 128:256]
+
+
+def place_kernel(camera_ref, view_ref, index_ref, grad_ref, low_ref, high_ref, table):
+    for f in range(feats):
+        value = grad_ref[pl.ds(f, 64, stride=feats), :]
+        for part, piece in enumerate(pieces(value, 2)):
+            row = (part * feats + f) * 32
+            table[row : row + 32, 0:128] = piece[0:32].astype(bf16)
+            table[row : row + 32, 128:256] = piece[32:64].astype(bf16)
     lane = iota((8, 128), 1)
     camera = jnp.zeros((8, 128), f32)
     for i in range(8):
-        camera = jnp.where(lane == i, table_ref[view_ref[0], i], camera)
-    for half in range(2):
-        row = half * half_rows
-        out_ref[row : row + rows, :] = total[:, 128 * half : 128 * half + 128]
-        out_ref[row + rows : row + rows + 8, :] = camera
+        camera = jnp.where(lane == i, camera_ref[view_ref[0], i], camera)
+    for half, out_ref in enumerate((low_ref, high_ref)):
+        out_ref[feats * 32 :, :] = camera
+
+        def keep(f, row, value, out_ref=out_ref):
+            out_ref[pl.ds(f * 32 + row, 1), :] = value
+
+        pick_rows(index_ref.at[32 * half : 32 * half + 32], table, keep, 0)
+
+
+def pick(incoming, table):
+    return call(
+        pick_kernel,
+        jax.ShapeDtypeStruct((64 * feats, 128), f32),
+        (incoming, table),
+        [vmem, vmem],
+        [pltpu.VMEM((feats, 64, 128), f32)],
+    )
+
+
+def invert(incoming):
+    return call(
+        inverse_kernel,
+        jax.ShapeDtypeStruct((64, 128), jnp.int32),
+        (incoming,),
+        [vmem],
+        [pltpu.VMEM((64, 256), f32)],
+    )
+
+
+def place(camera_table, view_camera, inverse, returned):
+    out = jax.ShapeDtypeStruct((half_rows, 128), f32)
+    return call(
+        place_kernel,
+        (out, out),
+        (camera_table, view_camera, inverse, returned),
+        [smem, smem, vmem, vmem],
+        [pltpu.VMEM((2 * feats * 32, 256), bf16)],
+    )
 
 
 def render_kernel(
-    plan_ref, length_ref, rows_ref, cot_ref, image_ref, out_ref, coef, turned, alphas, weights, moments, shades
+    plan_ref, length_ref, rows_ref, cot_ref, image_ref, out_ref, coef, colors, alphas, weights, shades, moments, tints
 ):
     lane_tile = iota((8, 128), 1) & 15
     lane_step = iota((8, 128), 1) >> 4
@@ -319,18 +367,15 @@
             jnp.where(alive, quad_u, 0.0),
             jnp.where(alive, quad_m, 0.0),
             jnp.where(alive, quad_v, 0.0),
-            feature(i, 6),
-            feature(i, 7),
-            feature(i, 8),
         ]
         for m, value in enumerate(values):
-            coef[pl.ds(i * 128 + m, 8, stride=16), :] = value
+            coef[pl.ds(i * 64 + m, 8, stride=8), :] = value
         return carry
 
     lax.fori_loop(0, 8, prepare, 0)
 
     def monomials(shape):
-        row = iota(shape, 0) & 15
+        row = iota(shape, 0) & 7
         pixel = iota(shape, 1)
         at_x = ((pixel & 15) * 2 - 15).astype(f32)
         at_y = ((pixel >> 4) * 2 - 15).astype(f32)
@@ -341,83 +386,112 @@
         out = jnp.where(row == 4, at_x * at_y, out)
         return jnp.where(row == 5, at_y * at_y, out)
 
-    terms = jnp.where(iota((64, 256), 0) >= 16, monomials((64, 256)), 0.0).astype(bf16)
+    terms = jnp.where(iota((32, 256), 0) < 24, monomials((32, 256)), 0.0).astype(bf16)
     moment_terms = monomials((16, 256)).astype(bf16)
-    cots = [cot_ref[h] for h in range(3)]
-    cot_parts = [pieces(cot, 2) for cot in cots]
+    cot_parts = [pieces(cot_ref[h], 2) for h in range(3)]
     cot_high = jnp.concatenate([p[0] for p in cot_parts], axis=0).astype(bf16)
     cot_low = jnp.concatenate([p[1] for p in cot_parts], axis=0).astype(bf16)
     cot_both = jnp.concatenate([cot_high, cot_low], axis=0)
+    cot_all = jnp.concatenate([cot_high, cot_high, cot_low], axis=0)
     same_tile = (iota((48, 256), 0) & 15) == (iota((48, 256), 1) & 15)
+    own_tile = iota((16, 256), 0) == (iota((16, 256), 1) & 15)
     across = (((1,), (1,)), ((), ()))
+    along = (((0,), (0,)), ((), ()))
+
+    def pair(i, ref, row, step):
+        return jnp.concatenate(
+            [ref[pl.ds(2 * i * step + row, 1), :], ref[pl.ds((2 * i + 1) * step + row, 1), :]],
+            axis=1,
+        )
+
+    def lay(i, carry):
+        raw = jnp.concatenate(
+            [
+                coef[pl.ds(pl.multiple_of(i * 16, 8), 8), :],
+                coef[pl.ds(pl.multiple_of(i * 16 + 8, 8), 8), :],
+            ],
+            axis=1,
+        )
+        block = jnp.concatenate(pieces(raw, 3) + [jnp.zeros((8, 256), f32)], axis=0)
+        base = pl.multiple_of(i * 256, 256)
+        power = lax.dot_general(
+            block.astype(bf16), terms, along, preferred_element_type=f32
+        )
+        alphas[pl.ds(base, 256), :] = jnp.exp2(power)
+        high = []
+        low = []
+        for h in range(3):
+            value = jnp.where(own_tile, pair(i, rows_ref, 6 + h, feats), 0.0)
+            parts = pieces(value, 2)
+            high.append(parts[0])
+            low.append(parts[1])
+        color = jnp.concatenate(high + low + high, axis=0).astype(bf16)
+        colors[i] = color[0:96]
+        shades[pl.ds(base, 256), :] = lax.dot_general(
+            color, cot_all, along, preferred_element_type=f32
+        )
+        return carry
+
+    lax.fori_loop(0, 32, lay, 0, unroll=lay_unroll)
+
+    image_ref[...] = jnp.zeros_like(image_ref)
 
     def forward(i, clear):
-        blocks = []
-        for own in range(2):
-            raw = coef[pl.ds(pl.multiple_of(i * 32 + own * 16, 16), 16), :]
-            blocks.append(jnp.concatenate([raw] + pieces(raw, 3), axis=0).T)
-        block = jnp.concatenate(blocks, axis=0)
         base = pl.multiple_of(i * 256, 256)
-        turned[pl.ds(base, 256), :] = block
-        power = jnp.dot(block.astype(bf16), terms, preferred_element_type=f32)
-        alpha = jnp.exp2(power)
-        alphas[pl.ds(base, 256), :] = alpha
-        pieces_w = []
+        kept = []
         for k in range(16):
-            weight = alpha[16 * k : 16 * k + 16] * clear
+            weight = alphas[pl.ds(base + 16 * k, 16), :] * clear
             clear = clear - weight
-            pieces_w.append(weight)
-        weight = jnp.concatenate(pieces_w, axis=0)
+            kept.append(weight)
+        weight = jnp.concatenate(kept, axis=0)
         weights[pl.ds(base, 256), :] = weight
         top = weight.astype(bf16)
         low = (weight - top.astype(f32)).astype(bf16)
+        color = colors[i]
+        both = jnp.dot(color, top, preferred_element_type=f32)
+        image = both[0:48] + both[48:96]
+        image += jnp.dot(color[0:48], low, preferred_element_type=f32)
+        for h in range(3):
+            image_ref[h] += image[16 * h : 16 * h + 16]
         both = lax.dot_general(cot_both, top, across, preferred_element_type=f32)
-        shade = both[0:48] + both[48:96]
-        shade += lax.dot_general(cot_high, low, across, preferred_element_type=f32)
-        shade = jnp.where(same_tile, shade, 0.0)
+        tint = both[0:48] + both[48:96]
+        tint += lax.dot_general(cot_high, low, across, preferred_element_type=f32)
+        tint = jnp.where(same_tile, tint, 0.0)
         for h in range(3):
-            value = jnp.sum(shade[16 * h : 16 * h + 16], axis=0, keepdims=True)
+            value = jnp.sum(tint[16 * h : 16 * h + 16], axis=0, keepdims=True)
             for own in range(2):
-                shades[h, pl.ds(2 * i + own, 1), :] = value[:, 128 * own : 128 * own + 128]
+                tints[h, pl.ds(2 * i + own, 1), :] = value[:, 128 * own : 128 * own + 128]
         return clear
 
-    lax.fori_loop(0, 32, forward, jnp.ones((16, 256), f32))
+    lax.fori_loop(0, 32, forward, jnp.ones((16, 256), f32), unroll=forward_unroll)
 
     def backward(step, behind):
         i = 31 - step
         base = pl.multiple_of(i * 256, 256)
-        behind = list(behind)
-        pieces_d = [None] * 16
+        kept = [None] * 16
         for k in range(15, -1, -1):
             rows = pl.ds(base + 16 * k, 16)
-            alpha = alphas[rows, :]
-            pull = None
-            for h in range(3):
-                gap = turned[rows, 6 + h : 7 + h] - behind[h]
-                behind[h] = behind[h] + alpha * gap
-                pull = cots[h] * gap if pull is None else pull + cots[h] * gap
-            pieces_d[k] = weights[rows, :] * pull
-        slope = jnp.concatenate(pieces_d, axis=0)
+            gap = shades[rows, :] - behind
+            kept[k] = weights[rows, :] * gap
+            behind = behind + alphas[rows, :] * gap
+        slope = jnp.concatenate(kept, axis=0)
         top = slope.astype(bf16)
         low = (slope - top.astype(f32)).astype(bf16)
         moment = lax.dot_general(moment_terms, top, across, preferred_element_type=f32)
         moment += lax.dot_general(moment_terms, low, across, preferred_element_type=f32)
         for own in range(2):
-            moments[pl.ds(pl.multiple_of(i * 32 + own * 16, 16), 16), :] = moment[
-                :, 128 * own : 128 * own + 128
+            moments[pl.ds(pl.multiple_of(i * 16 + own * 8, 8), 8), :] = moment[
+                0:8, 128 * own : 128 * own + 128
             ]
-        return tuple(behind)
-
-    blank = jnp.zeros((16, 256), f32)
-    image = lax.fori_loop(0, 32, backward, (blank, blank, blank))
-    for h in range(3):
-        image_ref[h] = image[h]
+        return behind
+
+    lax.fori_loop(0, 32, backward, jnp.zeros((16, 256), f32), unroll=backward_unroll)
 
     def finish(i, carry):
         off_u = (feature(i, 0) - center_u) * unit
         off_v = (feature(i, 1) - center_v) * unit
         m_one, m_x, m_y, m_xx, m_xy, m_yy = [
-            moments[pl.ds(i * 128 + m, 8, stride=16), :] for m in range(6)
+            moments[pl.ds(i * 64 + m, 8, stride=8), :] for m in range(6)
         ]
         n_x = m_x - off_u * m_one
         n_y = m_y - off_v * m_one
@@ -433,7 +507,7 @@
             m_one,
         ]
         for h in range(3):
-            values.append(shades[h, pl.ds(pl.multiple_of(i * 8, 8), 8), :])
+            values.append(tints[h, pl.ds(pl.multiple_of(i * 8, 8), 8), :])
         for f, value in enumerate(values):
             out_ref[pl.ds(i * (8 * feats) + f, 8, stride=feats), :] = value
         return carry
@@ -441,44 +515,98 @@
     lax.fori_loop(0, 8, finish, 0)
 
 
-def gradient_kernel(gauss_ref, own_ref, left_ref, right_ref, far_low_ref, far_high_ref, out_ref, spread, held):
-    spread_rows(gauss_ref, spread)
+def render(tile_plan, tile_lengths, arrived, cots):
+    shape = jax.ShapeDtypeStruct
+    return call(
+        render_kernel,
+        (shape((3, 16, 256), f32), shape((64 * feats, 128), f32)),
+        (tile_plan, tile_lengths, arrived, cots),
+        [smem, smem, vmem, vmem],
+        [
+            pltpu.VMEM((512, 128), f32),
+            pltpu.VMEM((32, 96, 256), bf16),
+            pltpu.VMEM((8192, 256), f32),
+            pltpu.VMEM((8192, 256), f32),
+            pltpu.VMEM((8192, 256), f32),
+            pltpu.VMEM((512, 128), f32),
+            pltpu.VMEM((3, 64, 128), f32),
+        ],
+    )
+
+
+def source_views(refs):
+    sources = []
+    for low, high in zip(refs[0::2], refs[1::2]):
+        line = low[feats * 32 : feats * 32 + 8, :]
+        camera = [jnp.broadcast_to(line[:, i : i + 1], (8, 128)) for i in range(8)]
+        sources.append(((low, high), view_values(camera)))
+    return sources
+
+
+def view_gradient(sources, spread, half, step):
+    at = (4 * half + step) * (8 * pitch)
+
+    def param(p):
+        return spread[pl.ds(at + p, 8, stride=pitch), :]
+
+    center = [param(p) for p in range(3)]
+    shaped = [[param(params_n + 3 * j + k) for k in range(3)] for j in range(3)]
+    harmonics = [param(p) for p in range(11, params_n)]
+    total = None
+    for refs, view in sources:
+        rows = [refs[half][pl.ds(32 * f + 8 * step, 8), :] for f in range(feats)]
+
+        def one(center, shaped, harmonics, view=view):
+            return project(center, shaped, harmonics, view)
+
+        _, back = jax.vjp(one, center, shaped, harmonics)
+        d_center, d_shaped, d_harmonics = back(rows[:5] + rows[6:])
+        part = d_center + sum(d_shaped, []) + [rows[5]] + d_harmonics
+        total = part if total is None else [x + y for x, y in zip(total, part)]
+    return total
+
+
+def first_kernel(spread, low_ref, high_ref, out_ref):
+    sources = source_views([low_ref, high_ref])
     for half in range(2):
-        far_ref = (far_low_ref, far_high_ref)[half]
-        sources = [
-            (own_ref, half * half_rows),
-            (left_ref, half * half_rows),
-            (right_ref, half * half_rows),
-            (far_ref, 0),
-        ]
-        views = []
-        for ref, base in sources:
-            line = ref[base + feats * 32 : base + feats * 32 + 8, :]
-            views.append(
-                view_values([jnp.broadcast_to(line[:, i : i + 1], (8, 128)) for i in range(8)])
-            )
-
-        def step(i, carry):
-            at = (i + 4 * half) * (8 * pitch)
-            params = [spread[pl.ds(at + p, 8, stride=pitch), :] for p in range(params_n)]
-
-            def every(*params):
-                shaped = shape_matrix(params)
-                out = []
-                for view in views:
-                    out += project(params, shaped, view)
-                return out + [log_opacity(params[10])]
-
-            _, back = jax.vjp(every, *params)
-            cots = []
-            opaque = None
-            for ref, base in sources:
-                rows = [ref[pl.ds(base + 32 * f + 8 * i, 8), :] for f in range(feats)]
-                cots += rows[:5] + rows[6:]
-                opaque = rows[5] if opaque is None else opaque + rows[5]
-            grads = back(cots + [opaque])
-            for p in range(params_n):
-                held[pl.ds(at + p, 8, stride=pitch), :] = grads[p]
+
+        def step(i, carry, half=half):
+            rows = pl.ds(pl.multiple_of(32 * half + i * 8, 8), 8)
+            for p, value in enumerate(view_gradient(sources, spread, half, i)):
+                out_ref[p, rows, :] = value
+            return carry
+
+        lax.fori_loop(0, 4, step, 0)
+
+
+def middle_kernel(spread, left_low, left_high, right_low, right_high, sum_ref, out_ref):
+    sources = source_views([left_low, left_high, right_low, right_high])
+    for half in range(2):
+
+        def step(i, carry, half=half):
+            rows = pl.ds(pl.multiple_of(32 * half + i * 8, 8), 8)
+            for p, value in enumerate(view_gradient(sources, spread, half, i)):
+                out_ref[p, rows, :] = value + sum_ref[p, rows, :]
+            return carry
+
+        lax.fori_loop(0, 4, step, 0)
+
+
+def last_kernel(spread, low_ref, high_ref, sum_ref, out_ref, held):
+    sources = source_views([low_ref, high_ref])
+    for half in range(2):
+
+        def step(i, carry, half=half):
+            rows = pl.ds(pl.multiple_of(32 * half + i * 8, 8), 8)
+            at = (4 * half + i) * (8 * pitch)
+            total = view_gradient(sources, spread, half, i)
+            total = [value + sum_ref[p, rows, :] for p, value in enumerate(total)]
+            params = [spread[pl.ds(at + p, 8, stride=pitch), :] for p in range(3, 11)]
+            _, back = jax.vjp(lambda *p: shape_matrix(p), *params[:7])
+            d_shape = back([total[3 + 3 * j : 6 + 3 * j] for j in range(3)])
+            d_logit = total[12] / (1.0 + jnp.exp(params[7]))
+            for p, value in enumerate(total[0:3] + list(d_shape) + [d_logit] + total[13:]):
+                held[pl.ds(at + p, 8, stride=pitch), :] = value
             return carry
 
         lax.fori_loop(0, 4, step, 0)
@@ -522,56 +650,44 @@
         [pltpu.VMEM((512, 128), f32)],
     )
     incoming = exchange(ordered, 1)
-    spread = pltpu.VMEM((64 * pitch, 128), f32)
-    table = call(
+    table, spread = call(
         project_kernel,
-        shape((3 * feats * 32, 256), bf16),
+        (shape(((2 * feats + 2) * 32, 256), bf16), shape((64 * pitch, 128), f32)),
         (camera_table, view_camera, gaussians),
         [smem, smem, vmem],
-        [spread, pltpu.VMEM((feats, 64, 128), f32)],
-    )
-    picked = call(
-        pick_kernel,
-        shape((64 * feats, 128), f32),
-        (incoming, table),
-        [vmem, vmem],
         [pltpu.VMEM((feats, 64, 128), f32)],
     )
+    picked = pick(incoming, table)
     arrived = exchange(picked, feats)
-    image, row_grad = call(
-        render_kernel,
-        (shape((3, 16, 256), f32), shape((64 * feats, 128), f32)),
-        (tile_plan, tile_lengths, arrived, jnp.transpose(pixel_grad[0], (1, 0, 2))),
-        [smem, smem, vmem, vmem],
-        [
-            pltpu.VMEM((1024, 128), f32),
-            pltpu.VMEM((8192, 64), f32),
-            pltpu.VMEM((8192, 256), f32),
-            pltpu.VMEM((8192, 256), f32),
-            pltpu.VMEM((1024, 128), f32),
-            pltpu.VMEM((3, 64, 128), f32),
-        ],
+    inverse = invert(incoming)
+    image, row_grad = render(
+        tile_plan, tile_lengths, arrived, jnp.transpose(pixel_grad[0], (1, 0, 2))
     )
     returned = exchange(row_grad, feats)
-    own = call(
-        place_kernel,
-        shape((2 * half_rows, 128), f32),
-        (camera_table, view_camera, incoming, returned),
-        [smem, smem, vmem, vmem],
-        [pltpu.VMEM((feats * 32, 256), f32)],
-    )
+    low, high = place(camera_table, view_camera, inverse, returned)
     ahead = [(i, (i + 1) % 4) for i in range(4)]
     behind = [(i, (i - 1) % 4) for i in range(4)]
-    left = lax.ppermute(own, "view", ahead)
-    right = lax.ppermute(own, "view", behind)
-    far_low = lax.ppermute(left[:half_rows], "view", ahead)
-    far_high = lax.ppermute(right[half_rows:], "view", behind)
+    left_low = lax.ppermute(low, "view", ahead)
+    right_high = lax.ppermute(high, "view", behind)
+    left_high = lax.ppermute(high, "view", ahead)
+    right_low = lax.ppermute(low, "view", behind)
+    far_low = lax.ppermute(left_low, "view", ahead)
+    far_high = lax.ppermute(right_high, "view", behind)
+    part = shape((61, 64, 128), f32)
+    total = call(first_kernel, part, (spread, low, high), [vmem] * 3, [])
     total = call(
-        gradient_kernel,
+        middle_kernel,
+        part,
+        (spread, left_low, left_high, right_low, right_high, total),
+        [vmem] * 6,
+        [],
+    )
+    total = call(
+        last_kernel,
         shape((params_n, slots), f32),
-        (gaussians, own, left, right, far_low, far_high),
-        [vmem] * 6,
-        [spread, spread],
+        (spread, far_low, far_high, total),
+        [vmem] * 4,
+        [pltpu.VMEM((64 * pitch, 128), f32)],
     )
     return (jnp.transpose(image, (1, 0, 2))[None], total)
 

time: 135 us -> 101 us (0.75)
  Pallas kernels: 56.5 us -> 33 us
  blocking collectives: 37.1 us -> 18.7 us
  starting transfers between devices: 18.8 us -> 23.5 us
  waiting for transfers between devices: 15.5 us -> 19.7 us
    pallas_call x6 -> x9, Pallas kernels: 56.5 us -> 33 us  [call(): pl.pallas_call(kernel, out_shape=out, in_specs=specs, out_specs=jax.tree....]
    all_to_all x2 -> x1, blocking collectives: 37.1 us -> 18.7 us  [exchange(): lax.all_to_all(parts, 'space', split_axis=0, concat_axis=0, tiled=True)]
    all_to_all x1 -> x2, waiting for transfers between devices: 4.79 us -> 15.6 us  [exchange(): lax.all_to_all(parts, 'space', split_axis=0, concat_axis=0, tiled=True)]
    ppermute x4 -> x6, waiting for transfers between devices: 10.7 us -> 4.06 us  [the longest x1 2.7 us: per_device(): left_low = lax.ppermute(low, 'view', ahead)]
    all_to_all x1 -> x2, starting transfers between devices: 12.1 us -> 17.3 us  [exchange(): lax.all_to_all(parts, 'space', split_axis=0, concat_axis=0, tiled=True)]
    ppermute x4 -> x6, starting transfers between devices: 6.7 us -> 6.21 us  [the longest x1 1.69 us: per_device(): left_high = lax.ppermute(high, 'view', ahead)]
    unnamed x15 -> x17, local copies, waits for them, and re-layouts: 3.89 us -> 3.89 us
  transfers between devices with their start and end apart: 5 -> 8, of which waited for: 3 -> 5; matrix products, arithmetic and copies ran while one was open for 1% -> 1% of each run, Pallas kernels for 1% -> 9%
where the time goes in v2:
time: 101 us; the launch traced here: 100 us
  Pallas kernels  33 us (33%)
  starting transfers between devices  23.5 us (23%)
  waiting for transfers between devices  19.7 us (20%)
  blocking collectives  18.7 us (19%)
  local copies, waits for them, and re-layouts  3.89 us (4%)
  between operations  1.41 us (1%)
    pallas_call x9, Pallas kernels, call(): pl.pallas_call(kernel, out_shape=out, in_specs=specs, out_specs=jax.tree....  33 us
    all_to_all x1, blocking collectives, exchange(): lax.all_to_all(parts, 'space', split_axis=0, concat_axis=0, tiled=True)  18.7 us
    all_to_all x2, starting transfers between devices, exchange(): lax.all_to_all(parts, 'space', split_axis=0, concat_axis=0, tiled=True)  17.3 us
    all_to_all x2, waiting for transfers between devices, exchange(): lax.all_to_all(parts, 'space', split_axis=0, concat_axis=0, tiled=True)  15.6 us
    unnamed x17, local copies, waits for them, and re-layouts  3.89 us
    ppermute x1, waiting for transfers between devices, per_device(): left_low = lax.ppermute(low, 'view', ahead)  2.7 us
  transfers between devices with their start and end apart: 8, of which 5 were waited for; matrix products, arithmetic and copies ran while one was open for 1% of the time, Pallas kernels for 9%

profile of v2, /device:TPU:6, one launch (start us, length us, event | category | flops | bytes accessed | tf_op | source)
XLA Modules:
  0.0 100.2 jit_solution(18174489961105516010)
XLA Ops:
  0.6 0.0 copy-start.3
  0.6 0.0 copy-start.4
  0.7 0.8 copy-done.4
  1.4 0.0 copy-start.5
  1.4 0.8 copy-done.5
  2.2 0.0 copy-start.6
  2.2 0.0 copy-start.7
  2.2 1.0 shard_map.95
  3.1 12.1 %all-to-all-start = ((s32[64,1,1,128]{3,2,1,0:T(1,128)}), s32[64,1,1,128]{3,2,1,0:T(1,128)S(1)}, u32[]{:S(2)}, u32[]{:S(2)}) async-start(s32[64,1,1,128]{3,2,1,0:T(1,128)} %bitcast.3), calls=%async_computation | async-start | bytes 65536 | tf_op jit(solution)/shard_map/all_to_all | solution.py:637
  15.3 0.8 copy.15.table_ref.camera_ref
  16.7 0.0 copy-start.2
  16.7 1.6 %copy-done.2 = f32[59,8192]{1,0:T(8,128)S(1)} copy-done((f32[59,8192]{1,0:T(8,128)S(1)}, f32[59,8192]{1,0:T(8,128)}, u32[]{:S(2)}) %copy-start.2) | copy-done | bytes 1933336
  18.3 1.7 %shard_map.96 = (bf16[640,256]{1,0:T(8,128)(2,1)S(1)}, f32[4608,128]{1,0:T(8,128)S(1)}) custom-call(f32[16,8]{1,0:T(8,128)S(1)} %copy.15.table_ref.camera_ref, s32[1]{0:T(128)S(6)} %copy.19.view_ref, f32[59,8192]{1,0:T(8,128)S(1)} %copy-done.2), custom_call_target="tpu_custom_call" | custom-call | tf_op jit(solution)/shard_map/pallas_call | solution.py:625
  20.0 0.0 copy-start
  20.0 4.8 %all-to-all-done = s32[64,1,1,128]{3,2,1,0:T(1,128)S(1)} async-done(((s32[64,1,1,128]{3,2,1,0:T(1,128)}), s32[64,1,1,128]{3,2,1,0:T(1,128)S(1)}, u32[]{:S(2)}, u32[]{:S(2)}) %all-to-all-start) | async-done | bytes 32800 | tf_op jit(solution)/shard_map/all_to_all | solution.py:637
  24.8 3.5 %shard_map.97 = f32[576,128]{1,0:T(8,128)S(1)} custom-call(s32[64,128]{1,0:T(8,128)S(1)} %bitcast.19, bf16[640,256]{1,0:T(8,128)(2,1)S(1)} %get-tuple-element.8.table_ref), custom_call_target="tpu_custom_call" | custom-call | tf_op jit(solution)/shard_map/pallas_call | solution.py:625
  28.3 18.7 %all_to_all.15 = f32[64,9,1,128]{3,2,1,0:T(1,128)S(1)} all-to-all(f32[64,9,1,128]{3,2,1,0:T(1,128)S(1)} %bitcast.18), channel_id=1, replica_groups=mesh['space'=64,'view'=4] {'space'}, dimensions={0} | all-to-all | bytes 589824 | tf_op jit(solution)/shard_map/all_to_all | solution.py:637
  47.0 0.0 copy-done.3
  47.0 0.0 copy-done.6
  47.0 0.0 copy-done.7
  47.0 12.8 %shard_map.98 = (f32[3,16,256]{2,1,0:T(8,128)}, f32[576,128]{1,0:T(8,128)}) custom-call(s32[1,16]{1,0:T(1,128)S(1)} %copy-done.6, s32[1,16]{1,0:T(1,128)S(1)} %copy-done.7, f32[576,128]{1,0:T(8,128)S(1)} %bitcast.17, f32[3,16,256]{2,1,0:T(8,128)S(1)} %bitcast.21), custom_call_target="tpu_custom_call" | custom-call | tf_op jit(solution)/shard_map/pallas_call | solution.py:625
  59.8 5.2 %all-to-all-start.2 = ((f32[64,9,1,128]{3,2,1,0:T(1,128)}), f32[64,9,1,128]{3,2,1,0:T(1,128)S(1)}, u32[]{:S(2)}, u32[]{:S(2)}) async-start(f32[64,9,1,128]{3,2,1,0:T(1,128)} %bitcast.11), calls=%async_computation.2 | async-start | bytes 589824 | tf_op jit(solution)/shard_map/all_to_all | solution.py:637
  64.9 2.6 %shard_map.99.index_ref = s32[64,128]{1,0:T(8,128)S(1)} custom-call(s32[64,128]{1,0:T(8,128)S(1)} %bitcast.20), custom_call_target="tpu_custom_call" | custom-call | tf_op jit(solution)/shard_map/pallas_call | solution.py:625
  67.5 10.8 %all-to-all-done.2 = f32[64,9,1,128]{3,2,1,0:T(1,128)S(1)} async-done(((f32[64,9,1,128]{3,2,1,0:T(1,128)}), f32[64,9,1,128]{3,2,1,0:T(1,128)S(1)}, u32[]{:S(2)}, u32[]{:S(2)}) %all-to-all-start.2) | async-done | bytes 294944 | tf_op jit(solution)/shard_map/all_to_all | solution.py:637
  78.3 3.9 %shard_map.100 = (f32[296,128]{1,0:T(8,128)S(1)}, f32[296,128]{1,0:T(8,128)S(1)}) custom-call(f32[16,8]{1,0:T(8,128)S(1)} %copy.15.table_ref.camera_ref, s32[1]{0:T(128)S(6)} %copy.19.view_ref, s32[64,128]{1,0:T(8,128)S(1)} %shard_map.99.index_ref, f32[576,128]{1,0:T(8,128)S(1)} %bitcast.16), custom_call_target="tpu_custom_call" | custom-call | tf_op jit(solution)/shard_map/pallas_call | solution.py:625
  82.3 0.6 collective-permute-start
  82.8 1.5 %collective-permute-start.2 = (f32[296,128]{1,0:T(8,128)S(1)}, f32[296,128]{1,0:T(8,128)S(1)}, u32[]{:S(2)}, u32[]{:S(2)}) collective-permute-start(f32[296,128]{1,0:T(8,128)S(1)} %get-tuple-element.13.high_ref), channel_id=1, source_target_pairs={{0,3},{1,0},{2,1},{3,2},{4,7},{5,4},{6,5},{7,6},{8,11},{9,8},{10,9... | collective-permute-start | bytes 454664 | tf_op jit(solution)/shard_map/ppermute | solution.py:671
  84.4 1.7 %collective-permute-start.4 = (f32[296,128]{1,0:T(8,128)S(1)}, f32[296,128]{1,0:T(8,128)S(1)}, u32[]{:S(2)}, u32[]{:S(2)}) collective-permute-start(f32[296,128]{1,0:T(8,128)S(1)} %get-tuple-element.13.high_ref), channel_id=1, source_target_pairs={{0,1},{1,2},{2,3},{3,0},{4,5},{5,6},{6,7},{7,4},{8,9},{9,10},{10,1... | collective-permute-start | bytes 454664 | tf_op jit(solution)/shard_map/ppermute | solution.py:672
  86.1 0.3 collective-permute-start.5
  86.4 2.7 %collective-permute-done.left_low = f32[296,128]{1,0:T(8,128)S(1)} collective-permute-done((f32[296,128]{1,0:T(8,128)S(1)}, f32[296,128]{1,0:T(8,128)S(1)}, u32[]{:S(2)}, u32[]{:S(2)}) %collective-permute-start) | collective-permute-done | bytes 151584 | tf_op jit(solution)/shard_map/ppermute | solution.py:670
  89.1 1.7 %collective-permute-start.1 = (f32[296,128]{1,0:T(8,128)S(1)}, f32[296,128]{1,0:T(8,128)S(1)}, u32[]{:S(2)}, u32[]{:S(2)}) collective-permute-start(f32[296,128]{1,0:T(8,128)S(1)} %collective-permute-done.left_low), channel_id=1, source_target_pairs={{0,1},{1,2},{2,3},{3,0},{4,5},{5,6},{6,7},{7,4},{8,9},{9,10},{10,1... | collective-permute-start | bytes 454664 | tf_op jit(solution)/shard_map/ppermute | solution.py:674
  90.8 0.0 collective-permute-done.2.right_high
  90.8 0.4 collective-permute-start.3
  91.2 1.1 %shard_map.101.sum_ref = f32[61,64,128]{2,1,0:T(8,128)S(1)} custom-call(f32[4608,128]{1,0:T(8,128)S(1)} %get-tuple-element.10.spread, f32[296,128]{1,0:T(8,128)S(1)} %get-tuple-element.12.low_ref, f32[296,128]{1,0:T(8,128)S(1)} %get-tuple-element.13.high_ref), custom_call_target="tpu_custom_call" | custom-call | tf_op jit(solution)/shard_map/pallas_call | solution.py:625
  92.3 0.0 copy-done
  92.3 0.0 collective-permute-done.4.left_high
  92.4 0.0 copy-start.1
  92.4 0.9 collective-permute-done.5.right_low
  93.2 3.5 %shard_map.102.sum_ref = f32[61,64,128]{2,1,0:T(8,128)S(1)} custom-call(f32[4608,128]{1,0:T(8,128)} %copy-done, f32[296,128]{1,0:T(8,128)S(1)} %collective-permute-done.left_low, f32[296,128]{1,0:T(8,128)S(1)} %collective-permute-done.4.left_high, f32[296,128]{1,0:T(8,128)S(1)} %collective-permute-done.5.right_low, ...), custom_call_target="tpu_custom_call" | custom-call | tf_op jit(solution)/shard_map/pallas_call | solution.py:625
  96.7 0.0 collective-permute-done.1.low_ref
  96.7 0.5 collective-permute-done.3.high_ref
  97.2 0.0 copy-done.1
  97.2 3.0 %shard_map.103 = f32[59,8192]{1,0:T(8,128)} custom-call(f32[4608,128]{1,0:T(8,128)S(1)} %copy-done.1, f32[296,128]{1,0:T(8,128)S(1)} %collective-permute-done.1.low_ref, f32[296,128]{1,0:T(8,128)S(1)} %collective-permute-done.3.high_ref, f32[61,64,128]{2,1,0:T(8,128)S(1)} %shard_map.102.sum_ref), custom_call_target="tpu_custom_call" | custom-call | tf_op jit(solution)/shard_map/pallas_call | solution.py:625
Async XLA Ops:
  0.6 46.3 %copy-start.3 = (f32[1,16,3,256]{3,1,2,0:T(8,128)S(1)}, f32[1,16,3,256]{3,1,2,0:T(8,128)}, u32[]{:S(2)}) copy-start(f32[1,16,3,256]{3,1,2,0:T(8,128)} %param.15) | copy-start | bytes 147460
  0.6 0.8 copy-start.4
  1.4 0.8 copy-start.5
  2.2 44.8 %copy-start.6 = (s32[1,16]{1,0:T(1,128)S(1)}, s32[1,16]{1,0:T(1,128)}, u32[]{:S(2)}) copy-start(s32[1,16]{1,0:T(1,128)} %plan_ref.1) | copy-start | bytes 196
  2.2 44.8 %copy-start.7 = (s32[1,16]{1,0:T(1,128)S(1)}, s32[1,16]{1,0:T(1,128)}, u32[]{:S(2)}) copy-start(s32[1,16]{1,0:T(1,128)} %length_ref.1) | copy-start | bytes 196
  3.1 21.6 %all-to-all-start = ((s32[64,1,1,128]{3,2,1,0:T(1,128)}), s32[64,1,1,128]{3,2,1,0:T(1,128)S(1)}, u32[]{:S(2)}, u32[]{:S(2)}) async-start(s32[64,1,1,128]{3,2,1,0:T(1,128)} %bitcast.3), calls=%async_computation | async-start | bytes 65536 | tf_op jit(solution)/shard_map/all_to_all | solution.py:637
  16.7 1.6 %copy-start.2 = (f32[59,8192]{1,0:T(8,128)S(1)}, f32[59,8192]{1,0:T(8,128)}, u32[]{:S(2)}) copy-start(f32[59,8192]{1,0:T(8,128)} %gauss_ref.1) | copy-start | bytes 5799940
  20.0 72.3 %copy-start = (f32[4608,128]{1,0:T(8,128)}, f32[4608,128]{1,0:T(8,128)S(1)}, u32[]{:S(2)}) copy-start(f32[4608,128]{1,0:T(8,128)S(1)} %get-tuple-element.10.spread) | copy-start | bytes 7077892
  59.8 18.6 %all-to-all-start.2 = ((f32[64,9,1,128]{3,2,1,0:T(1,128)}), f32[64,9,1,128]{3,2,1,0:T(1,128)S(1)}, u32[]{:S(2)}, u32[]{:S(2)}) async-start(f32[64,9,1,128]{3,2,1,0:T(1,128)} %bitcast.11), calls=%async_computation.2 | async-start | bytes 589824 | tf_op jit(solution)/shard_map/all_to_all | solution.py:637
  82.3 6.9 %collective-permute-start = (f32[296,128]{1,0:T(8,128)S(1)}, f32[296,128]{1,0:T(8,128)S(1)}, u32[]{:S(2)}, u32[]{:S(2)}) collective-permute-start(f32[296,128]{1,0:T(8,128)S(1)} %get-tuple-element.12.low_ref), channel_id=1, source_target_pairs={{0,1},{1,2},{2,3},{3,0},{4,5},{5,6},{6,7},{7,4},{8,9},{9,10},{10,1... | collective-permute-start | bytes 454664 | tf_op jit(solution)/shard_map/ppermute | solution.py:670
  82.8 8.0 %collective-permute-start.2 = (f32[296,128]{1,0:T(8,128)S(1)}, f32[296,128]{1,0:T(8,128)S(1)}, u32[]{:S(2)}, u32[]{:S(2)}) collective-permute-start(f32[296,128]{1,0:T(8,128)S(1)} %get-tuple-element.13.high_ref), channel_id=1, source_target_pairs={{0,3},{1,0},{2,1},{3,2},{4,7},{5,4},{6,5},{7,6},{8,11},{9,8},{10,9... | collective-permute-start | bytes 454664 | tf_op jit(solution)/shard_map/ppermute | solution.py:671
  84.4 8.0 %collective-permute-start.4 = (f32[296,128]{1,0:T(8,128)S(1)}, f32[296,128]{1,0:T(8,128)S(1)}, u32[]{:S(2)}, u32[]{:S(2)}) collective-permute-start(f32[296,128]{1,0:T(8,128)S(1)} %get-tuple-element.13.high_ref), channel_id=1, source_target_pairs={{0,1},{1,2},{2,3},{3,0},{4,5},{5,6},{6,7},{7,4},{8,9},{9,10},{10,1... | collective-permute-start | bytes 454664 | tf_op jit(solution)/shard_map/ppermute | solution.py:672
  86.1 7.1 %collective-permute-start.5 = (f32[296,128]{1,0:T(8,128)S(1)}, f32[296,128]{1,0:T(8,128)S(1)}, u32[]{:S(2)}, u32[]{:S(2)}) collective-permute-start(f32[296,128]{1,0:T(8,128)S(1)} %get-tuple-element.12.low_ref), channel_id=1, source_target_pairs={{0,3},{1,0},{2,1},{3,2},{4,7},{5,4},{6,5},{7,6},{8,11},{9,8},{10,9... | collective-permute-start | bytes 454664 | tf_op jit(solution)/shard_map/ppermute | solution.py:673
  89.1 7.6 %collective-permute-start.1 = (f32[296,128]{1,0:T(8,128)S(1)}, f32[296,128]{1,0:T(8,128)S(1)}, u32[]{:S(2)}, u32[]{:S(2)}) collective-permute-start(f32[296,128]{1,0:T(8,128)S(1)} %collective-permute-done.left_low), channel_id=1, source_target_pairs={{0,1},{1,2},{2,3},{3,0},{4,5},{5,6},{6,7},{7,4},{8,9},{9,10},{10,1... | collective-permute-start | bytes 454664 | tf_op jit(solution)/shard_map/ppermute | solution.py:674
  90.8 6.4 %collective-permute-start.3 = (f32[296,128]{1,0:T(8,128)S(1)}, f32[296,128]{1,0:T(8,128)S(1)}, u32[]{:S(2)}, u32[]{:S(2)}) collective-permute-start(f32[296,128]{1,0:T(8,128)S(1)} %collective-permute-done.2.right_high), channel_id=1, source_target_pairs={{0,3},{1,0},{2,1},{3,2},{4,7},{5,4},{6,5},{7,6},{8,11},{9,8},{10,9... | collective-permute-start | bytes 454664 | tf_op jit(solution)/shard_map/ppermute | solution.py:675
  92.4 4.8 %copy-start.1 = (f32[4608,128]{1,0:T(8,128)S(1)}, f32[4608,128]{1,0:T(8,128)}, u32[]{:S(2)}) copy-start(f32[4608,128]{1,0:T(8,128)} %copy-done) | copy-start | bytes 7077892

commit v3 on v2

--- a/solution.py
+++ b/solution.py
@@ -32,10 +32,12 @@
 slots = 8192
 pitch = 72
 half_rows = 296
-lay_unroll = 4
-forward_unroll = 8
-backward_unroll = 8
-pick_unroll = 8
+lay_unroll = 16
+image_step = 8
+colors_at = 8448
+forward_unroll = 16
+backward_unroll = 16
+pick_unroll = 16
 vmem = pl.BlockSpec(memory_space=pltpu.VMEM)
 smem = pl.BlockSpec(memory_space=pltpu.SMEM)
 f32 = jnp.float32
@@ -159,42 +161,68 @@
     return lax.broadcasted_iota(jnp.int32, shape, axis)
 
 
-def spread_rows(gauss_ref, spread):
-    def step(tile, carry):
-        column = pl.ds(pl.multiple_of(tile * 128, 128), 128)
-        row = pl.multiple_of(tile * pitch, 8)
-        spread[pl.ds(row, 56), :] = gauss_ref[0:56, column]
-        spread[pl.ds(row + 56, 3), :] = gauss_ref[56:59, column]
-        return carry
-
-    lax.fori_loop(0, 64, step, 0, unroll=4)
-
-
-def order_kernel(requests_ref, lists_ref, out_ref, turned):
-    lists = lists_ref[...].astype(f32)
-    turned[...] = jnp.concatenate([lists, jnp.zeros((112, 512), f32)], axis=0).T
+def order_kernel(requests_hbm, lists_hbm, out_ref, requests, lists, turned, sems):
+    copies = [
+        pltpu.make_async_copy(lists_hbm, lists.at[0:16], sems.at[0]),
+        pltpu.make_async_copy(requests_hbm, requests, sems.at[1]),
+    ]
+    for copy in copies:
+        copy.start()
+    lists[16:128] = jnp.zeros((112, 512), jnp.int32)
+    for copy in copies:
+        copy.wait()
+    turned[...] = lists[...].T
     group = iota((64, 128), 1) // 16
-    entry = jnp.zeros((64, 128), f32)
+    entry = jnp.zeros((64, 128), jnp.int32)
     for j in range(8):
         piece = turned[pl.ds(j, 64, stride=8), :]
         if j:
             piece = pltpu.roll(piece, 16 * j, 1)
         entry = jnp.where(group == j, piece, entry)
-    place = entry.astype(jnp.int32) & 127
-    out_ref[...] = jnp.take_along_axis(requests_ref[...], place, axis=1)
+    out_ref[...] = jnp.take_along_axis(requests[...], entry & 127, axis=1)
 
 
 def camera_values(table_ref, view_ref):
     row = view_ref[0]
-    return [jnp.full((8, 128), table_ref[row, i], f32) for i in range(8)]
-
-
-def project_kernel(table_ref, view_ref, gauss_ref, out_ref, spread, held):
+    return [jnp.full((8, 128), table_ref[i, row], f32) for i in range(8)]
+
+
+def tile_frame(plan_ref, length_ref):
+    lane_tile = iota((8, 128), 1) & 15
+    center_u = jnp.zeros((8, 128), f32)
+    center_v = jnp.zeros((8, 128), f32)
+    length = jnp.zeros((8, 128), jnp.int32)
+    for t in range(16):
+        tile = plan_ref[0, t]
+        down = tile // 120
+        across = tile - down * 120
+        at_u = (across * 16 + 8 - 960).astype(f32)
+        at_v = (down * 16 + 8 - 540).astype(f32)
+        center_u = jnp.where(lane_tile == t, at_u, center_u)
+        center_v = jnp.where(lane_tile == t, at_v, center_v)
+        length = jnp.where(lane_tile == t, length_ref[0, t], length)
+    return center_u / 540.0, center_v / 540.0, length
+
+
+def project_kernel(
+    table_ref, view_ref, gauss_hbm, out_ref, spread, gauss, held, sems
+):
+    def fetch(i):
+        column = pl.ds(pl.multiple_of(i * 1024, 1024), 1024)
+        return pltpu.make_async_copy(gauss_hbm.at[:, column], gauss.at[:, column], sems.at[i])
+
+    for i in range(8):
+        fetch(i).start()
     view = view_values(camera_values(table_ref, view_ref))
-    spread_rows(gauss_ref, spread)
 
     def step(i, carry):
         at = i * (8 * pitch)
+        fetch(i).wait()
+        for tile in range(8):
+            column = pl.ds(pl.multiple_of(i * 1024 + tile * 128, 128), 128)
+            row = pl.multiple_of(at + tile * pitch, 8)
+            spread[pl.ds(row, 56), :] = gauss[0:56, column]
+            spread[pl.ds(row + 56, 3), :] = gauss[56:59, column]
         params = [spread[pl.ds(at + p, 8, stride=pitch), :] for p in range(params_n)]
         shaped = shape_matrix(params[3:10])
         for k in range(9):
@@ -285,7 +313,7 @@
     lane = iota((8, 128), 1)
     camera = jnp.zeros((8, 128), f32)
     for i in range(8):
-        camera = jnp.where(lane == i, camera_ref[view_ref[0], i], camera)
+        camera = jnp.where(lane == i, camera_ref[i, view_ref[0]], camera)
     for half, out_ref in enumerate((low_ref, high_ref)):
         out_ref[feats * 32 :, :] = camera
 
@@ -327,24 +355,23 @@
 
 
 def render_kernel(
-    plan_ref, length_ref, rows_ref, cot_ref, image_ref, out_ref, coef, colors, alphas, weights, shades, moments, tints
+    plan_ref,
+    length_ref,
+    rows_ref,
+    cot_ref,
+    made_hbm,
+    out_ref,
+    weights,
+    colors,
+    coef,
+    alphas,
+    shades,
+    moments,
+    tints,
+    sems,
 ):
-    lane_tile = iota((8, 128), 1) & 15
     lane_step = iota((8, 128), 1) >> 4
-    center_u = jnp.zeros((8, 128), f32)
-    center_v = jnp.zeros((8, 128), f32)
-    length = jnp.zeros((8, 128), jnp.int32)
-    for t in range(16):
-        tile = plan_ref[0, t]
-        down = tile // 120
-        across = tile - down * 120
-        at_u = (across * 16 + 8 - 960).astype(f32)
-        at_v = (down * 16 + 8 - 540).astype(f32)
-        center_u = jnp.where(lane_tile == t, at_u, center_u)
-        center_v = jnp.where(lane_tile == t, at_v, center_v)
-        length = jnp.where(lane_tile == t, length_ref[0, t], length)
-    center_u = center_u / 540.0
-    center_v = center_v / 540.0
+    center_u, center_v, length = tile_frame(plan_ref, length_ref)
 
     def feature(i, f):
         return rows_ref[pl.ds(i * (8 * feats) + f, 8, stride=feats), :]
@@ -425,8 +452,9 @@
             parts = pieces(value, 2)
             high.append(parts[0])
             low.append(parts[1])
-        color = jnp.concatenate(high + low + high, axis=0).astype(bf16)
-        colors[i] = color[0:96]
+        color = jnp.concatenate(high + low, axis=0)
+        colors[pl.ds(pl.multiple_of(i * 96, 8), 96), :] = color
+        color = jnp.concatenate([color] + high, axis=0).astype(bf16)
         shades[pl.ds(base, 256), :] = lax.dot_general(
             color, cot_all, along, preferred_element_type=f32
         )
@@ -434,7 +462,12 @@
 
     lax.fori_loop(0, 32, lay, 0, unroll=lay_unroll)
 
-    image_ref[...] = jnp.zeros_like(image_ref)
+    def store(i):
+        rows = pl.ds(pl.multiple_of(i * 256, 256), 256)
+        return pltpu.make_async_copy(weights.at[rows], made_hbm.at[rows], sems.at[i])
+
+    store_colors = pltpu.make_async_copy(colors, made_hbm.at[colors_at : colors_at + 3072], sems.at[32])
+    store_colors.start()
 
     def forward(i, clear):
         base = pl.multiple_of(i * 256, 256)
@@ -445,14 +478,9 @@
             kept.append(weight)
         weight = jnp.concatenate(kept, axis=0)
         weights[pl.ds(base, 256), :] = weight
+        store(i).start()
         top = weight.astype(bf16)
         low = (weight - top.astype(f32)).astype(bf16)
-        color = colors[i]
-        both = jnp.dot(color, top, preferred_element_type=f32)
-        image = both[0:48] + both[48:96]
-        image += jnp.dot(color[0:48], low, preferred_element_type=f32)
-        for h in range(3):
-            image_ref[h] += image[16 * h : 16 * h + 16]
         both = lax.dot_general(cot_both, top, across, preferred_element_type=f32)
         tint = both[0:48] + both[48:96]
         tint += lax.dot_general(cot_high, low, across, preferred_element_type=f32)
@@ -471,9 +499,10 @@
         kept = [None] * 16
         for k in range(15, -1, -1):
             rows = pl.ds(base + 16 * k, 16)
-            gap = shades[rows, :] - behind
-            kept[k] = weights[rows, :] * gap
-            behind = behind + alphas[rows, :] * gap
+            alpha = alphas[rows, :]
+            shown = shades[rows, :]
+            kept[k] = weights[rows, :] * (shown - behind)
+            behind = (1.0 - alpha) * behind + alpha * shown
         slope = jnp.concatenate(kept, axis=0)
         top = slope.astype(bf16)
         low = (slope - top.astype(f32)).astype(bf16)
@@ -513,25 +542,66 @@
         return carry
 
     lax.fori_loop(0, 8, finish, 0)
+    store_colors.wait()
+    for i in range(32):
+        store(i).wait()
+
+
+def image_kernel(weights, colors, image_ref):
+    @pl.when(pl.program_id(0) == 0)
+    def _():
+        image_ref[...] = jnp.zeros_like(image_ref)
+
+    for i in range(image_step):
+        weight = weights[256 * i : 256 * i + 256, :]
+        top = weight.astype(bf16)
+        low = (weight - top.astype(f32)).astype(bf16)
+        color = colors[96 * i : 96 * i + 96, :].astype(bf16)
+        both = jnp.dot(color, top, preferred_element_type=f32)
+        image = both[0:48] + both[48:96]
+        image += jnp.dot(color[0:48], low, preferred_element_type=f32)
+        for h in range(3):
+            image_ref[h] += image[16 * h : 16 * h + 16]
 
 
 def render(tile_plan, tile_lengths, arrived, cots):
     shape = jax.ShapeDtypeStruct
+    hbm = pl.BlockSpec(memory_space=pltpu.HBM)
     return call(
         render_kernel,
-        (shape((3, 16, 256), f32), shape((64 * feats, 128), f32)),
+        (
+            shape((colors_at + 3072, 256), f32),
+            shape((64 * feats, 128), f32),
+        ),
         (tile_plan, tile_lengths, arrived, cots),
         [smem, smem, vmem, vmem],
         [
+            pltpu.VMEM((8192, 256), f32),
+            pltpu.VMEM((3072, 256), f32),
             pltpu.VMEM((512, 128), f32),
-            pltpu.VMEM((32, 96, 256), bf16),
-            pltpu.VMEM((8192, 256), f32),
             pltpu.VMEM((8192, 256), f32),
             pltpu.VMEM((8192, 256), f32),
             pltpu.VMEM((512, 128), f32),
             pltpu.VMEM((3, 64, 128), f32),
+            pltpu.SemaphoreType.DMA((33,)),
         ],
-    )
+        52,
+        (hbm, vmem),
+    )
+
+
+def compose(made):
+    return pl.pallas_call(
+        image_kernel,
+        out_shape=jax.ShapeDtypeStruct((3, 16, 256), f32),
+        grid=(32 // image_step,),
+        in_specs=[
+            pl.BlockSpec((256 * image_step, 256), lambda i: (i, 0)),
+            pl.BlockSpec((96 * image_step, 256), lambda i: (i + colors_at // (96 * image_step), 0)),
+        ],
+        out_specs=pl.BlockSpec((3, 16, 256), lambda i: (0, 0, 0)),
+        compiler_params=pltpu.CompilerParams(vmem_limit_bytes=60 * 1024 * 1024),
+    )(made, made)
 
 
 def source_views(refs):
@@ -543,8 +613,9 @@
     return sources
 
 
-def view_gradient(sources, spread, half, step):
-    at = (4 * half + step) * (8 * pitch)
+def view_gradient(sources, spread, step):
+    at = step * (8 * pitch)
+    first = step < 4
 
     def param(p):
         return spread[pl.ds(at + p, 8, stride=pitch), :]
@@ -553,8 +624,9 @@
     shaped = [[param(params_n + 3 * j + k) for k in range(3)] for j in range(3)]
     harmonics = [param(p) for p in range(11, params_n)]
     total = None
-    for refs, view in sources:
-        rows = [refs[half][pl.ds(32 * f + 8 * step, 8), :] for f in range(feats)]
+    for (low, high), view in sources:
+        lines = [pl.ds(32 * f + 8 * (step & 3), 8) for f in range(feats)]
+        rows = [jnp.where(first, low[line, :], high[line, :]) for line in lines]
 
         def one(center, shaped, harmonics, view=view):
             return project(center, shaped, harmonics, view)
@@ -568,65 +640,64 @@
 
 def first_kernel(spread, low_ref, high_ref, out_ref):
     sources = source_views([low_ref, high_ref])
-    for half in range(2):
-
-        def step(i, carry, half=half):
-            rows = pl.ds(pl.multiple_of(32 * half + i * 8, 8), 8)
-            for p, value in enumerate(view_gradient(sources, spread, half, i)):
-                out_ref[p, rows, :] = value
-            return carry
-
-        lax.fori_loop(0, 4, step, 0)
+
+    def step(i, carry):
+        rows = pl.ds(pl.multiple_of(i * 8, 8), 8)
+        for p, value in enumerate(view_gradient(sources, spread, i)):
+            out_ref[p, rows, :] = value
+        return carry
+
+    lax.fori_loop(0, 8, step, 0)
 
 
 def middle_kernel(spread, left_low, left_high, right_low, right_high, sum_ref, out_ref):
     sources = source_views([left_low, left_high, right_low, right_high])
-    for half in range(2):
-
-        def step(i, carry, half=half):
-            rows = pl.ds(pl.multiple_of(32 * half + i * 8, 8), 8)
-            for p, value in enumerate(view_gradient(sources, spread, half, i)):
-                out_ref[p, rows, :] = value + sum_ref[p, rows, :]
-            return carry
-
-        lax.fori_loop(0, 4, step, 0)
-
-
-def last_kernel(spread, low_ref, high_ref, sum_ref, out_ref, held):
+
+    def step(i, carry):
+        rows = pl.ds(pl.multiple_of(i * 8, 8), 8)
+        for p, value in enumerate(view_gradient(sources, spread, i)):
+            out_ref[p, rows, :] = value + sum_ref[p, rows, :]
+        return carry
+
+    lax.fori_loop(0, 8, step, 0)
+
+
+def last_kernel(spread, low_ref, high_ref, sum_ref, out_hbm, held, out_ref, sems):
     sources = source_views([low_ref, high_ref])
-    for half in range(2):
-
-        def step(i, carry, half=half):
-            rows = pl.ds(pl.multiple_of(32 * half + i * 8, 8), 8)
-            at = (4 * half + i) * (8 * pitch)
-            total = view_gradient(sources, spread, half, i)
-            total = [value + sum_ref[p, rows, :] for p, value in enumerate(total)]
-            params = [spread[pl.ds(at + p, 8, stride=pitch), :] for p in range(3, 11)]
-            _, back = jax.vjp(lambda *p: shape_matrix(p), *params[:7])
-            d_shape = back([total[3 + 3 * j : 6 + 3 * j] for j in range(3)])
-            d_logit = total[12] / (1.0 + jnp.exp(params[7]))
-            for p, value in enumerate(total[0:3] + list(d_shape) + [d_logit] + total[13:]):
-                held[pl.ds(at + p, 8, stride=pitch), :] = value
-            return carry
-
-        lax.fori_loop(0, 4, step, 0)
-
-    def collect(tile, carry):
-        column = pl.ds(pl.multiple_of(tile * 128, 128), 128)
-        row = pl.multiple_of(tile * pitch, 8)
-        out_ref[0:56, column] = held[pl.ds(row, 56), :]
-        out_ref[56:59, column] = held[pl.ds(row + 56, 3), :]
+
+    def copy(i):
+        column = pl.ds(pl.multiple_of(i * 1024, 1024), 1024)
+        return pltpu.make_async_copy(out_ref.at[:, column], out_hbm.at[:, column], sems.at[i])
+
+    def step(i, carry):
+        rows = pl.ds(pl.multiple_of(i * 8, 8), 8)
+        total = view_gradient(sources, spread, i)
+        total = [value + sum_ref[p, rows, :] for p, value in enumerate(total)]
+        params = [spread[pl.ds(i * (8 * pitch) + p, 8, stride=pitch), :] for p in range(3, 11)]
+        _, back = jax.vjp(lambda *p: shape_matrix(p), *params[:7])
+        d_shape = back([total[3 + 3 * j : 6 + 3 * j] for j in range(3)])
+        d_logit = total[12] / (1.0 + jnp.exp(params[7]))
+        for p, value in enumerate(total[0:3] + list(d_shape) + [d_logit] + total[13:]):
+            held[pl.ds(p, 8, stride=pitch), :] = value
+        for tile in range(8):
+            column = pl.ds(pl.multiple_of(i * 1024 + tile * 128, 128), 128)
+            row = tile * pitch
+            out_ref[0:56, column] = held[row : row + 56, :]
+            out_ref[56:59, column] = held[row + 56 : row + 59, :]
+        copy(i).start()
         return carry
 
-    lax.fori_loop(0, 64, collect, 0, unroll=4)
-
-
-def call(kernel, out, args, specs, scratch, limit=48):
+    lax.fori_loop(0, 8, step, 0)
+    for i in range(8):
+        copy(i).wait()
+
+
+def call(kernel, out, args, specs, scratch, limit=8, out_specs=None):
     return pl.pallas_call(
         kernel,
         out_shape=out,
         in_specs=specs,
-        out_specs=jax.tree.map(lambda _: vmem, out),
+        out_specs=out_specs or jax.tree.map(lambda _: vmem, out),
         scratch_shapes=scratch,
         compiler_params=pltpu.CompilerParams(vmem_limit_bytes=limit * 1024 * 1024),
     )(*args)
@@ -646,48 +717,72 @@
         order_kernel,
         shape((64, 128), jnp.int32),
         (requests[0, 0], tile_lists[0]),
-        [vmem, vmem],
-        [pltpu.VMEM((512, 128), f32)],
+        [pl.BlockSpec(memory_space=pltpu.HBM)] * 2,
+        [
+            pltpu.VMEM((64, 128), jnp.int32),
+            pltpu.VMEM((128, 512), jnp.int32),
+            pltpu.VMEM((512, 128), jnp.int32),
+            pltpu.SemaphoreType.DMA((2,)),
+        ],
+        60,
     )
     incoming = exchange(ordered, 1)
     table, spread = call(
         project_kernel,
-        (shape(((2 * feats + 2) * 32, 256), bf16), shape((64 * pitch, 128), f32)),
-        (camera_table, view_camera, gaussians),
-        [smem, smem, vmem],
-        [pltpu.VMEM((feats, 64, 128), f32)],
+        (
+            shape(((2 * feats + 2) * 32, 256), bf16),
+            shape((64 * pitch, 128), f32),
+        ),
+        (camera_table.T, view_camera, gaussians),
+        [smem, smem, pl.BlockSpec(memory_space=pltpu.HBM)],
+        [
+            pltpu.VMEM((params_n, slots), f32),
+            pltpu.VMEM((feats, 64, 128), f32),
+            pltpu.SemaphoreType.DMA((8,)),
+        ],
+        16,
     )
     picked = pick(incoming, table)
     arrived = exchange(picked, feats)
     inverse = invert(incoming)
-    image, row_grad = render(
+    made, row_grad = render(
         tile_plan, tile_lengths, arrived, jnp.transpose(pixel_grad[0], (1, 0, 2))
     )
     returned = exchange(row_grad, feats)
-    low, high = place(camera_table, view_camera, inverse, returned)
+    image = compose(made)
+    returned, image = lax.optimization_barrier((returned, image))
+    low, high = place(camera_table.T, view_camera, inverse, returned)
     ahead = [(i, (i + 1) % 4) for i in range(4)]
     behind = [(i, (i - 1) % 4) for i in range(4)]
     left_low = lax.ppermute(low, "view", ahead)
     right_high = lax.ppermute(high, "view", behind)
     left_high = lax.ppermute(high, "view", ahead)
     right_low = lax.ppermute(low, "view", behind)
+    part = shape((61, 64, 128), f32)
+    total = call(first_kernel, part, (spread, low, high), [vmem] * 3, [], 12)
+    left_low, right_high, total = lax.optimization_barrier((left_low, right_high, total))
     far_low = lax.ppermute(left_low, "view", ahead)
     far_high = lax.ppermute(right_high, "view", behind)
-    part = shape((61, 64, 128), f32)
-    total = call(first_kernel, part, (spread, low, high), [vmem] * 3, [])
     total = call(
         middle_kernel,
         part,
         (spread, left_low, left_high, right_low, right_high, total),
         [vmem] * 6,
         [],
+        16,
     )
     total = call(
         last_kernel,
         shape((params_n, slots), f32),
         (spread, far_low, far_high, total),
         [vmem] * 4,
-        [pltpu.VMEM((64 * pitch, 128), f32)],
+        [
+            pltpu.VMEM((8 * pitch, 128), f32),
+            pltpu.VMEM((params_n, slots), f32),
+            pltpu.SemaphoreType.DMA((8,)),
+        ],
+        16,
+        pl.BlockSpec(memory_space=pltpu.HBM),
     )
     return (jnp.transpose(image, (1, 0, 2))[None], total)
 

time: 101 us -> 97.1 us (0.961)
  waiting for transfers between devices: 19.7 us -> 15 us
  Pallas kernels: 33 us -> 35.4 us
  local copies, waits for them, and re-layouts: 3.89 us -> 2.29 us
    all_to_all x2, waiting for transfers between devices: 15.6 us -> 9.08 us  [exchange(): lax.all_to_all(parts, 'space', split_axis=0, concat_axis=0, tiled=True)]
    pallas_call x9 -> x10, Pallas kernels: 33 us -> 35.4 us  [the longest x9 29.1 us: call(): pl.pallas_call(kernel, out_shape=out, in_specs=specs, out_specs=out_specs...]
    unnamed x17 -> x12, local copies, waits for them, and re-layouts: 3.89 us -> 2.29 us
    ppermute x1, waiting for transfers between devices: 0.47 us -> 1.86 us  [per_device(): far_high = lax.ppermute(right_high, 'view', behind)]
    ppermute x1, waiting for transfers between devices: 0.01 us -> 1.36 us  [per_device(): right_high = lax.ppermute(high, 'view', behind)]
    ppermute x1, waiting for transfers between devices: 2.7 us -> 1.49 us  [per_device(): left_low = lax.ppermute(low, 'view', ahead)]
    ppermute x1, starting transfers between devices: 1.69 us -> 0.65 us  [per_device(): far_low = lax.ppermute(left_low, 'view', ahead)]
  transfers between devices with their start and end apart: 8 -> 8, of which waited for: 5 -> 7; matrix products, arithmetic and copies ran while one was open for 1% -> 0% of each run, Pallas kernels for 9% -> 14%
where the time goes in v3:
time: 97.1 us; the launch traced here: 96.7 us
  Pallas kernels  35.4 us (36%)
  starting transfers between devices  23.7 us (24%)
  blocking collectives  18.8 us (19%)
  waiting for transfers between devices  15 us (15%)
  local copies, waits for them, and re-layouts  2.29 us (2%)
  between operations  1.57 us (2%)
    pallas_call x9, Pallas kernels, call(): pl.pallas_call(kernel, out_shape=out, in_specs=specs, out_specs=out_specs...  29.1 us
    all_to_all x1, blocking collectives, exchange(): lax.all_to_all(parts, 'space', split_axis=0, concat_axis=0, tiled=True)  18.8 us
    all_to_all x2, starting transfers between devices, exchange(): lax.all_to_all(parts, 'space', split_axis=0, concat_axis=0, tiled=True)  17.5 us
    all_to_all x2, waiting for transfers between devices, exchange(): lax.all_to_all(parts, 'space', split_axis=0, concat_axis=0, tiled=True)  9.08 us
    pallas_call x1, Pallas kernels, compose(): pl.pallas_call(image_kernel, out_shape=jax.ShapeDtypeStruct((3, 16, 256),...  6.27 us
    unnamed x12, local copies, waits for them, and re-layouts  2.29 us
  transfers between devices with their start and end apart: 8, of which 7 were waited for; matrix products, arithmetic and copies ran while one was open for 0% of the time, Pallas kernels for 14%

profile of v3, /device:TPU:6, one launch (start us, length us, event | category | flops | bytes accessed | tf_op | source)
XLA Modules:
  0.0 96.7 jit_solution(10726968049018450629)
XLA Ops:
  0.6 0.0 copy-start.1
  0.6 0.0 copy-start.4
  0.7 0.0 copy-start.5
  0.7 1.8 %shard_map.95 = s32[64,128]{1,0:T(8,128)} custom-call(s32[64,128]{1,0:T(8,128)} %bitcast.27, s32[16,512]{1,0:T(8,128)} %bitcast.28), custom_call_target="tpu_custom_call" | custom-call | tf_op jit(solution)/shard_map/pallas_call | solution.py:696
  2.5 12.1 %all-to-all-start = ((s32[64,1,1,128]{3,2,1,0:T(1,128)}), s32[64,1,1,128]{3,2,1,0:T(1,128)S(1)}, u32[]{:S(2)}, u32[]{:S(2)}) async-start(s32[64,1,1,128]{3,2,1,0:T(1,128)} %bitcast.25), calls=%async_computation | async-start | bytes 65536 | tf_op jit(solution)/shard_map/all_to_all | solution.py:708
  15.2 0.0 copy-start
  15.2 1.6 %copy-done = f32[59,8192]{1,0:T(8,128)S(1)} copy-done((f32[59,8192]{1,0:T(8,128)S(1)}, f32[59,8192]{1,0:T(8,128)}, u32[]{:S(2)}) %copy-start) | copy-done | bytes 1933336
  16.8 0.0 copy-start.2
  16.8 0.7 copy-done.2
  17.5 1.9 %shard_map.96 = (bf16[640,256]{1,0:T(8,128)(2,1)S(1)}, f32[4608,128]{1,0:T(8,128)S(1)}) custom-call(f32[8,16]{1,0:T(8,128)S(1)} %bitcast.23, s32[1]{0:T(128)S(6)} %copy.13.view_ref, f32[59,8192]{1,0:T(8,128)S(1)} %copy-done), custom_call_target="tpu_custom_call" | custom-call | tf_op jit(solution)/shard_map/pallas_call | solution.py:696
  19.4 4.7 %all-to-all-done = s32[64,1,1,128]{3,2,1,0:T(1,128)S(1)} async-done(((s32[64,1,1,128]{3,2,1,0:T(1,128)}), s32[64,1,1,128]{3,2,1,0:T(1,128)S(1)}, u32[]{:S(2)}, u32[]{:S(2)}) %all-to-all-start) | async-done | bytes 32800 | tf_op jit(solution)/shard_map/all_to_all | solution.py:708
  24.1 3.1 %shard_map.97 = f32[576,128]{1,0:T(8,128)S(1)} custom-call(s32[64,128]{1,0:T(8,128)S(1)} %bitcast.20, bf16[640,256]{1,0:T(8,128)(2,1)S(1)} %get-tuple-element.13.table_ref), custom_call_target="tpu_custom_call" | custom-call | tf_op jit(solution)/shard_map/pallas_call | solution.py:696
  27.2 18.8 %all_to_all.15 = f32[64,9,1,128]{3,2,1,0:T(1,128)S(1)} all-to-all(f32[64,9,1,128]{3,2,1,0:T(1,128)S(1)} %bitcast.19), channel_id=1, replica_groups=mesh['space'=64,'view'=4] {'space'}, dimensions={0} | all-to-all | bytes 589824 | tf_op jit(solution)/shard_map/all_to_all | solution.py:708
  46.0 0.0 copy-done.1
  46.0 0.0 copy-done.4
  46.0 0.0 copy-done.5
  46.0 10.5 %shard_map.98 = (f32[11520,256]{1,0:T(8,128)}, f32[576,128]{1,0:T(8,128)}) custom-call(s32[1,16]{1,0:T(1,128)S(1)} %copy-done.4, s32[1,16]{1,0:T(1,128)S(1)} %copy-done.5, f32[576,128]{1,0:T(8,128)S(1)} %bitcast.18, f32[3,16,256]{2,1,0:T(8,128)S(1)} %bitcast.22), custom_call_target="tpu_custom_call" | custom-call | tf_op jit(solution)/shard_map/pallas_call | solution.py:696
  56.6 5.4 %all-to-all-start.2 = ((f32[64,9,1,128]{3,2,1,0:T(1,128)}), f32[64,9,1,128]{3,2,1,0:T(1,128)S(1)}, u32[]{:S(2)}, u32[]{:S(2)}) async-start(f32[64,9,1,128]{3,2,1,0:T(1,128)} %bitcast.10), calls=%async_computation.2 | async-start | bytes 589824 | tf_op jit(solution)/shard_map/all_to_all | solution.py:708
  62.0 2.6 %shard_map.100.index_ref = s32[64,128]{1,0:T(8,128)S(1)} custom-call(s32[64,128]{1,0:T(8,128)S(1)} %bitcast.21), custom_call_target="tpu_custom_call" | custom-call | tf_op jit(solution)/shard_map/pallas_call | solution.py:696
  64.5 0.0 copy-start.3
  64.5 6.3 %shard_map.99 = f32[3,16,256]{2,1,0:T(8,128)} custom-call(f32[11520,256]{1,0:T(8,128)} %get-tuple-element.15.weights.colors, f32[11520,256]{1,0:T(8,128)} %get-tuple-element.15.weights.colors), custom_call_target="tpu_custom_call" | custom-call | tf_op jit(solution)/shard_map/pallas_call | solution.py:594
  70.8 4.4 %all-to-all-done.2 = f32[64,9,1,128]{3,2,1,0:T(1,128)S(1)} async-done(((f32[64,9,1,128]{3,2,1,0:T(1,128)}), f32[64,9,1,128]{3,2,1,0:T(1,128)S(1)}, u32[]{:S(2)}, u32[]{:S(2)}) %all-to-all-start.2) | async-done | bytes 294944 | tf_op jit(solution)/shard_map/all_to_all | solution.py:708
  75.2 0.0 copy-done.3
  75.2 3.3 %shard_map.101 = (f32[296,128]{1,0:T(8,128)S(1)}, f32[296,128]{1,0:T(8,128)S(1)}) custom-call(f32[8,16]{1,0:T(8,128)S(1)} %bitcast.24, s32[1]{0:T(128)S(6)} %copy.13.view_ref, s32[64,128]{1,0:T(8,128)S(1)} %shard_map.100.index_ref, f32[576,128]{1,0:T(8,128)S(1)} %bitcast.17), custom_call_target="tpu_custom_call" | custom-call | tf_op jit(solution)/shard_map/pallas_call | solution.py:696
  78.5 0.6 collective-permute-start
  79.1 1.5 %collective-permute-start.1 = (f32[296,128]{1,0:T(8,128)S(1)}, f32[296,128]{1,0:T(8,128)S(1)}, u32[]{:S(2)}, u32[]{:S(2)}) collective-permute-start(f32[296,128]{1,0:T(8,128)S(1)} %get-tuple-element.20.high_ref), channel_id=1, source_target_pairs={{0,3},{1,0},{2,1},{3,2},{4,7},{5,4},{6,5},{7,6},{8,11},{9,8},{10,9... | collective-permute-start | bytes 454664 | tf_op jit(solution)/shard_map/ppermute | solution.py:758
  80.6 1.7 %collective-permute-start.4 = (f32[296,128]{1,0:T(8,128)S(1)}, f32[296,128]{1,0:T(8,128)S(1)}, u32[]{:S(2)}, u32[]{:S(2)}) collective-permute-start(f32[296,128]{1,0:T(8,128)S(1)} %get-tuple-element.20.high_ref), channel_id=1, source_target_pairs={{0,1},{1,2},{2,3},{3,0},{4,5},{5,6},{6,7},{7,4},{8,9},{9,10},{10,1... | collective-permute-start | bytes 454664 | tf_op jit(solution)/shard_map/ppermute | solution.py:759
  82.3 0.3 collective-permute-start.5
  82.6 1.2 %shard_map.102.sum_ref = f32[61,64,128]{2,1,0:T(8,128)S(1)} custom-call(f32[4608,128]{1,0:T(8,128)S(1)} %get-tuple-element.17.spread, f32[296,128]{1,0:T(8,128)S(1)} %get-tuple-element.19.low_ref, f32[296,128]{1,0:T(8,128)S(1)} %get-tuple-element.20.high_ref), custom_call_target="tpu_custom_call" | custom-call | tf_op jit(solution)/shard_map/pallas_call | solution.py:696
  83.8 1.5 %collective-permute-done.left_low = f32[296,128]{1,0:T(8,128)S(1)} collective-permute-done((f32[296,128]{1,0:T(8,128)S(1)}, f32[296,128]{1,0:T(8,128)S(1)}, u32[]{:S(2)}, u32[]{:S(2)}) %collective-permute-start) | collective-permute-done | bytes 151584 | tf_op jit(solution)/shard_map/ppermute | solution.py:757
  85.3 1.4 %collective-permute-done.1.right_high = f32[296,128]{1,0:T(8,128)S(1)} collective-permute-done((f32[296,128]{1,0:T(8,128)S(1)}, f32[296,128]{1,0:T(8,128)S(1)}, u32[]{:S(2)}, u32[]{:S(2)}) %collective-permute-start.1) | collective-permute-done | bytes 151584 | tf_op jit(solution)/shard_map/ppermute | solution.py:758
  86.7 0.6 collective-permute-start.2
  87.3 1.4 %collective-permute-start.3 = (f32[296,128]{1,0:T(8,128)S(1)}, f32[296,128]{1,0:T(8,128)S(1)}, u32[]{:S(2)}, u32[]{:S(2)}) collective-permute-start(f32[296,128]{1,0:T(8,128)S(1)} %collective-permute-done.1.right_high), channel_id=1, source_target_pairs={{0,3},{1,0},{2,1},{3,2},{4,7},{5,4},{6,5},{7,6},{8,11},{9,8},{10,9... | collective-permute-start | bytes 454664 | tf_op jit(solution)/shard_map/ppermute | solution.py:765
  88.7 0.0 collective-permute-done.4.left_high
  88.7 0.7 collective-permute-done.5.right_low
  89.4 1.9 %shard_map.103.sum_ref = f32[61,64,128]{2,1,0:T(8,128)S(1)} custom-call(f32[4608,128]{1,0:T(8,128)S(1)} %get-tuple-element.17.spread, f32[296,128]{1,0:T(8,128)S(1)} %collective-permute-done.left_low, f32[296,128]{1,0:T(8,128)S(1)} %collective-permute-done.4.left_high, f32[296,128]{1,0:T(8,128)S(1)} %collective-permute-done.5.right_low, ...), custom_call_target="tpu_custom_call" | custom-call | tf_op jit(solution)/shard_map/pallas_call | solution.py:696
  91.3 0.5 collective-permute-done.2.low_ref
  91.9 1.9 %collective-permute-done.3.high_ref = f32[296,128]{1,0:T(8,128)S(1)} collective-permute-done((f32[296,128]{1,0:T(8,128)S(1)}, f32[296,128]{1,0:T(8,128)S(1)}, u32[]{:S(2)}, u32[]{:S(2)}) %collective-permute-start.3) | collective-permute-done | bytes 151584 | tf_op jit(solution)/shard_map/ppermute | solution.py:765
  93.7 2.8 %shard_map.104 = f32[59,8192]{1,0:T(8,128)} custom-call(f32[4608,128]{1,0:T(8,128)S(1)} %get-tuple-element.17.spread, f32[296,128]{1,0:T(8,128)S(1)} %collective-permute-done.2.low_ref, f32[296,128]{1,0:T(8,128)S(1)} %collective-permute-done.3.high_ref, f32[61,64,128]{2,1,0:T(8,128)S(1)} %shard_map.103.sum_ref), custom_call_target="tpu_custom_call" | custom-call | tf_op jit(solution)/shard_map/pallas_call | solution.py:696
Async XLA Ops:
  0.6 45.4 %copy-start.1 = (f32[1,16,3,256]{3,1,2,0:T(8,128)S(1)}, f32[1,16,3,256]{3,1,2,0:T(8,128)}, u32[]{:S(2)}) copy-start(f32[1,16,3,256]{3,1,2,0:T(8,128)} %param.15) | copy-start | bytes 147460
  0.6 45.4 %copy-start.4 = (s32[1,16]{1,0:T(1,128)S(1)}, s32[1,16]{1,0:T(1,128)}, u32[]{:S(2)}) copy-start(s32[1,16]{1,0:T(1,128)} %plan_ref.1) | copy-start | bytes 196
  0.7 45.4 %copy-start.5 = (s32[1,16]{1,0:T(1,128)S(1)}, s32[1,16]{1,0:T(1,128)}, u32[]{:S(2)}) copy-start(s32[1,16]{1,0:T(1,128)} %length_ref.1) | copy-start | bytes 196
  2.5 21.7 %all-to-all-start = ((s32[64,1,1,128]{3,2,1,0:T(1,128)}), s32[64,1,1,128]{3,2,1,0:T(1,128)S(1)}, u32[]{:S(2)}, u32[]{:S(2)}) async-start(s32[64,1,1,128]{3,2,1,0:T(1,128)} %bitcast.25), calls=%async_computation | async-start | bytes 65536 | tf_op jit(solution)/shard_map/all_to_all | solution.py:708
  15.2 1.6 %copy-start = (f32[59,8192]{1,0:T(8,128)S(1)}, f32[59,8192]{1,0:T(8,128)}, u32[]{:S(2)}) copy-start(f32[59,8192]{1,0:T(8,128)} %gauss_hbm.1) | copy-start | bytes 5799940
  16.8 0.7 copy-start.2
  56.6 18.6 %all-to-all-start.2 = ((f32[64,9,1,128]{3,2,1,0:T(1,128)}), f32[64,9,1,128]{3,2,1,0:T(1,128)S(1)}, u32[]{:S(2)}, u32[]{:S(2)}) async-start(f32[64,9,1,128]{3,2,1,0:T(1,128)} %bitcast.10), calls=%async_computation.2 | async-start | bytes 589824 | tf_op jit(solution)/shard_map/all_to_all | solution.py:708
  64.5 10.6 %copy-start.3 = (f32[16,8]{0,1:T(8,128)S(1)}, f32[16,8]{0,1:T(8,128)}, u32[]{:S(2)}) copy-start(f32[16,8]{0,1:T(8,128)} %param.9) | copy-start | bytes 1540
  78.5 6.9 %collective-permute-start = (f32[296,128]{1,0:T(8,128)S(1)}, f32[296,128]{1,0:T(8,128)S(1)}, u32[]{:S(2)}, u32[]{:S(2)}) collective-permute-start(f32[296,128]{1,0:T(8,128)S(1)} %get-tuple-element.19.low_ref), channel_id=1, source_target_pairs={{0,1},{1,2},{2,3},{3,0},{4,5},{5,6},{6,7},{7,4},{8,9},{9,10},{10,1... | collective-permute-start | bytes 454664 | tf_op jit(solution)/shard_map/ppermute | solution.py:757
  79.1 7.6 %collective-permute-start.1 = (f32[296,128]{1,0:T(8,128)S(1)}, f32[296,128]{1,0:T(8,128)S(1)}, u32[]{:S(2)}, u32[]{:S(2)}) collective-permute-start(f32[296,128]{1,0:T(8,128)S(1)} %get-tuple-element.20.high_ref), channel_id=1, source_target_pairs={{0,3},{1,0},{2,1},{3,2},{4,7},{5,4},{6,5},{7,6},{8,11},{9,8},{10,9... | collective-permute-start | bytes 454664 | tf_op jit(solution)/shard_map/ppermute | solution.py:758
  80.6 8.1 %collective-permute-start.4 = (f32[296,128]{1,0:T(8,128)S(1)}, f32[296,128]{1,0:T(8,128)S(1)}, u32[]{:S(2)}, u32[]{:S(2)}) collective-permute-start(f32[296,128]{1,0:T(8,128)S(1)} %get-tuple-element.20.high_ref), channel_id=1, source_target_pairs={{0,1},{1,2},{2,3},{3,0},{4,5},{5,6},{6,7},{7,4},{8,9},{9,10},{10,1... | collective-permute-start | bytes 454664 | tf_op jit(solution)/shard_map/ppermute | solution.py:759
  82.3 7.1 %collective-permute-start.5 = (f32[296,128]{1,0:T(8,128)S(1)}, f32[296,128]{1,0:T(8,128)S(1)}, u32[]{:S(2)}, u32[]{:S(2)}) collective-permute-start(f32[296,128]{1,0:T(8,128)S(1)} %get-tuple-element.19.low_ref), channel_id=1, source_target_pairs={{0,3},{1,0},{2,1},{3,2},{4,7},{5,4},{6,5},{7,6},{8,11},{9,8},{10,9... | collective-permute-start | bytes 454664 | tf_op jit(solution)/shard_map/ppermute | solution.py:760
  86.7 5.2 %collective-permute-start.2 = (f32[296,128]{1,0:T(8,128)S(1)}, f32[296,128]{1,0:T(8,128)S(1)}, u32[]{:S(2)}, u32[]{:S(2)}) collective-permute-start(f32[296,128]{1,0:T(8,128)S(1)} %collective-permute-done.left_low), channel_id=1, source_target_pairs={{0,1},{1,2},{2,3},{3,0},{4,5},{5,6},{6,7},{7,4},{8,9},{9,10},{10,1... | collective-permute-start | bytes 454664 | tf_op jit(solution)/shard_map/ppermute | solution.py:764
  87.3 6.4 %collective-permute-start.3 = (f32[296,128]{1,0:T(8,128)S(1)}, f32[296,128]{1,0:T(8,128)S(1)}, u32[]{:S(2)}, u32[]{:S(2)}) collective-permute-start(f32[296,128]{1,0:T(8,128)S(1)} %collective-permute-done.1.right_high), channel_id=1, source_target_pairs={{0,3},{1,0},{2,1},{3,2},{4,7},{5,4},{6,5},{7,6},{8,11},{9,8},{10,9... | collective-permute-start | bytes 454664 | tf_op jit(solution)/shard_map/ppermute | solution.py:765

commit v4 on v3

--- a/solution.py
+++ b/solution.py
@@ -163,15 +163,14 @@
 
 def order_kernel(requests_hbm, lists_hbm, out_ref, requests, lists, turned, sems):
     copies = [
-        pltpu.make_async_copy(lists_hbm, lists.at[0:16], sems.at[0]),
+        pltpu.make_async_copy(lists_hbm, lists, sems.at[0]),
         pltpu.make_async_copy(requests_hbm, requests, sems.at[1]),
     ]
     for copy in copies:
         copy.start()
-    lists[16:128] = jnp.zeros((112, 512), jnp.int32)
     for copy in copies:
         copy.wait()
-    turned[...] = lists[...].T
+    turned[:, 0:16] = lists[...].T
     group = iota((64, 128), 1) // 16
     entry = jnp.zeros((64, 128), jnp.int32)
     for j in range(8):
@@ -277,7 +276,7 @@
         out_ref[pl.ds(f, 64, stride=feats), :] = held[f]
 
 
-def inverse_kernel(index_ref, out_ref, total):
+def inverse_kernel(index_ref, low_ref, high_ref, total):
     total[...] = jnp.zeros_like(total)
 
     def step(pair, carry):
@@ -299,11 +298,11 @@
 
     lax.fori_loop(0, 32, step, 0, unroll=4)
     spot = (total[0:32] * 128.0 + total[32:64]).astype(jnp.int32)
-    out_ref[0:32, :] = spot[:, 0:128]
-    out_ref[32:64, :] = spot[:, 128:256]
-
-
-def place_kernel(camera_ref, view_ref, index_ref, grad_ref, low_ref, high_ref, table):
+    low_ref[...] = spot[:, 0:128]
+    high_ref[...] = spot[:, 128:256]
+
+
+def place_kernel(camera_ref, view_ref, index_ref, grad_ref, out_ref, table):
     for f in range(feats):
         value = grad_ref[pl.ds(f, 64, stride=feats), :]
         for part, piece in enumerate(pieces(value, 2)):
@@ -314,13 +313,12 @@
     camera = jnp.zeros((8, 128), f32)
     for i in range(8):
         camera = jnp.where(lane == i, camera_ref[i, view_ref[0]], camera)
-    for half, out_ref in enumerate((low_ref, high_ref)):
-        out_ref[feats * 32 :, :] = camera
-
-        def keep(f, row, value, out_ref=out_ref):
-            out_ref[pl.ds(f * 32 + row, 1), :] = value
-
-        pick_rows(index_ref.at[32 * half : 32 * half + 32], table, keep, 0)
+    out_ref[feats * 32 :, :] = camera
+
+    def keep(f, row, value):
+        out_ref[pl.ds(f * 32 + row, 1), :] = value
+
+    pick_rows(index_ref, table, keep, 0)
 
 
 def pick(incoming, table):
@@ -334,9 +332,10 @@
 
 
 def invert(incoming):
+    half = jax.ShapeDtypeStruct((32, 128), jnp.int32)
     return call(
         inverse_kernel,
-        jax.ShapeDtypeStruct((64, 128), jnp.int32),
+        (half, half),
         (incoming,),
         [vmem],
         [pltpu.VMEM((64, 256), f32)],
@@ -344,10 +343,9 @@
 
 
 def place(camera_table, view_camera, inverse, returned):
-    out = jax.ShapeDtypeStruct((half_rows, 128), f32)
     return call(
         place_kernel,
-        (out, out),
+        jax.ShapeDtypeStruct((half_rows, 128), f32),
         (camera_table, view_camera, inverse, returned),
         [smem, smem, vmem, vmem],
         [pltpu.VMEM((2 * feats * 32, 256), bf16)],
@@ -720,7 +718,7 @@
         [pl.BlockSpec(memory_space=pltpu.HBM)] * 2,
         [
             pltpu.VMEM((64, 128), jnp.int32),
-            pltpu.VMEM((128, 512), jnp.int32),
+            pltpu.VMEM((16, 512), jnp.int32),
             pltpu.VMEM((512, 128), jnp.int32),
             pltpu.SemaphoreType.DMA((2,)),
         ],
@@ -744,20 +742,21 @@
     )
     picked = pick(incoming, table)
     arrived = exchange(picked, feats)
-    inverse = invert(incoming)
+    inverse_low, inverse_high = invert(incoming)
     made, row_grad = render(
         tile_plan, tile_lengths, arrived, jnp.transpose(pixel_grad[0], (1, 0, 2))
     )
     returned = exchange(row_grad, feats)
     image = compose(made)
     returned, image = lax.optimization_barrier((returned, image))
-    low, high = place(camera_table.T, view_camera, inverse, returned)
+    low = place(camera_table.T, view_camera, inverse_low, returned)
     ahead = [(i, (i + 1) % 4) for i in range(4)]
     behind = [(i, (i - 1) % 4) for i in range(4)]
     left_low = lax.ppermute(low, "view", ahead)
+    right_low = lax.ppermute(low, "view", behind)
+    high = place(camera_table.T, view_camera, inverse_high, returned)
     right_high = lax.ppermute(high, "view", behind)
     left_high = lax.ppermute(high, "view", ahead)
-    right_low = lax.ppermute(low, "view", behind)
     part = shape((61, 64, 128), f32)
     total = call(first_kernel, part, (spread, low, high), [vmem] * 3, [], 12)
     left_low, right_high, total = lax.optimization_barrier((left_low, right_high, total))

time: 97.1 us -> 100 us (1.030)
  starting transfers between devices: 23.7 us -> 26.2 us
    ppermute x1, starting transfers between devices: 0.65 us -> 3.35 us  [per_device(): far_low = lax.ppermute(left_low, 'view', ahead)]
    ppermute x1, starting transfers between devices: 0.58 us -> 2.41 us  [per_device(): left_low = lax.ppermute(low, 'view', ahead)]
    ppermute x1, waiting for transfers between devices: 1.86 us -> 3.68 us  [per_device(): far_high = lax.ppermute(right_high, 'view', behind)]
    ppermute x1, starting transfers between devices: 1.69 us -> 0.03 us  [per_device(): left_high = lax.ppermute(high, 'view', ahead)]
    ppermute x1, starting transfers between devices: 0.34 us -> 1.99 us  [per_device(): right_low = lax.ppermute(low, 'view', behind)]
    ppermute x1, waiting for transfers between devices: 1.49 us -> 0.01 us  [per_device(): left_low = lax.ppermute(low, 'view', ahead)]
    ppermute x1, starting transfers between devices: 1.38 us -> 0.01 us  [per_device(): far_high = lax.ppermute(right_high, 'view', behind)]
    pallas_call x9 -> x10, Pallas kernels: 29.1 us -> 29.9 us  [call(): pl.pallas_call(kernel, out_shape=out, in_specs=specs, out_specs=out_specs...]
  transfers between devices with their start and end apart: 8 -> 8, of which waited for: 7 -> 5; matrix products, arithmetic and copies ran while one was open for 0% -> 0% of each run, Pallas kernels for 14% -> 14%
where the time goes in v4:
time: 100 us
  Pallas kernels  36.2 us (36%)
  starting transfers between devices  26.2 us (26%)
  blocking collectives  18.8 us (19%)
  waiting for transfers between devices  15 us (15%)
  local copies, waits for them, and re-layouts  2.29 us (2%)
  between operations  1.58 us (2%)
    pallas_call x10, Pallas kernels, call(): pl.pallas_call(kernel, out_shape=out, in_specs=specs, out_specs=out_specs...  29.9 us
    all_to_all x1, blocking collectives, exchange(): lax.all_to_all(parts, 'space', split_axis=0, concat_axis=0, tiled=True)  18.8 us
    all_to_all x2, starting transfers between devices, exchange(): lax.all_to_all(parts, 'space', split_axis=0, concat_axis=0, tiled=True)  17.5 us
    all_to_all x2, waiting for transfers between devices, exchange(): lax.all_to_all(parts, 'space', split_axis=0, concat_axis=0, tiled=True)  9.08 us
    pallas_call x1, Pallas kernels, compose(): pl.pallas_call(image_kernel, out_shape=jax.ShapeDtypeStruct((3, 16, 256),...  6.26 us
    ppermute x1, waiting for transfers between devices, per_device(): far_high = lax.ppermute(right_high, 'view', behind)  3.68 us
    ppermute x1, starting transfers between devices, per_device(): far_low = lax.ppermute(left_low, 'view', ahead)  3.35 us
    ppermute x1, starting transfers between devices, per_device(): left_low = lax.ppermute(low, 'view', ahead)  2.41 us
  transfers between devices with their start and end apart: 8, of which 5 were waited for; matrix products, arithmetic and copies ran while one was open for 0% of the time, Pallas kernels for 14%

profile of v4, /device:TPU:6, one launch (start us, length us, event | category | flops | bytes accessed | tf_op | source)
XLA Modules:
  0.0 100.0 jit_solution(6795350935319276642)
XLA Ops:
  0.6 0.0 copy-start.1
  0.6 0.0 copy-start.4
  0.7 0.0 copy-start.5
  0.7 1.8 %shard_map.95 = s32[64,128]{1,0:T(8,128)} custom-call(s32[64,128]{1,0:T(8,128)} %bitcast.29, s32[16,512]{1,0:T(8,128)} %bitcast.30), custom_call_target="tpu_custom_call" | custom-call | tf_op jit(solution)/shard_map/pallas_call | solution.py:694
  2.5 12.1 %all-to-all-start = ((s32[64,1,1,128]{3,2,1,0:T(1,128)}), s32[64,1,1,128]{3,2,1,0:T(1,128)S(1)}, u32[]{:S(2)}, u32[]{:S(2)}) async-start(s32[64,1,1,128]{3,2,1,0:T(1,128)} %bitcast.27), calls=%async_computation | async-start | bytes 65536 | tf_op jit(solution)/shard_map/all_to_all | solution.py:706
  15.2 0.0 copy-start
  15.2 1.6 %copy-done = f32[59,8192]{1,0:T(8,128)S(1)} copy-done((f32[59,8192]{1,0:T(8,128)S(1)}, f32[59,8192]{1,0:T(8,128)}, u32[]{:S(2)}) %copy-start) | copy-done | bytes 1933336
  16.8 0.0 copy-start.2
  16.8 0.7 copy-done.2
  17.5 1.9 %shard_map.96 = (bf16[640,256]{1,0:T(8,128)(2,1)S(1)}, f32[4608,128]{1,0:T(8,128)S(1)}) custom-call(f32[8,16]{1,0:T(8,128)S(1)} %bitcast.24, s32[1]{0:T(128)S(6)} %copy.13.view_ref, f32[59,8192]{1,0:T(8,128)S(1)} %copy-done), custom_call_target="tpu_custom_call" | custom-call | tf_op jit(solution)/shard_map/pallas_call | solution.py:694
  19.4 4.7 %all-to-all-done = s32[64,1,1,128]{3,2,1,0:T(1,128)S(1)} async-done(((s32[64,1,1,128]{3,2,1,0:T(1,128)}), s32[64,1,1,128]{3,2,1,0:T(1,128)S(1)}, u32[]{:S(2)}, u32[]{:S(2)}) %all-to-all-start) | async-done | bytes 32800 | tf_op jit(solution)/shard_map/all_to_all | solution.py:706
  24.1 3.1 %shard_map.97 = f32[576,128]{1,0:T(8,128)S(1)} custom-call(s32[64,128]{1,0:T(8,128)S(1)} %bitcast.21, bf16[640,256]{1,0:T(8,128)(2,1)S(1)} %get-tuple-element.13.table_ref), custom_call_target="tpu_custom_call" | custom-call | tf_op jit(solution)/shard_map/pallas_call | solution.py:694
  27.2 18.8 %all_to_all.15 = f32[64,9,1,128]{3,2,1,0:T(1,128)S(1)} all-to-all(f32[64,9,1,128]{3,2,1,0:T(1,128)S(1)} %bitcast.20), channel_id=1, replica_groups=mesh['space'=64,'view'=4] {'space'}, dimensions={0} | all-to-all | bytes 589824 | tf_op jit(solution)/shard_map/all_to_all | solution.py:706
  46.0 0.0 copy-done.1
  46.0 0.0 copy-done.4
  46.0 0.0 copy-done.5
  46.0 10.5 %shard_map.98 = (f32[11520,256]{1,0:T(8,128)}, f32[576,128]{1,0:T(8,128)}) custom-call(s32[1,16]{1,0:T(1,128)S(1)} %copy-done.4, s32[1,16]{1,0:T(1,128)S(1)} %copy-done.5, f32[576,128]{1,0:T(8,128)S(1)} %bitcast.19, f32[3,16,256]{2,1,0:T(8,128)S(1)} %bitcast.23), custom_call_target="tpu_custom_call" | custom-call | tf_op jit(solution)/shard_map/pallas_call | solution.py:694
  56.6 5.4 %all-to-all-start.2 = ((f32[64,9,1,128]{3,2,1,0:T(1,128)}), f32[64,9,1,128]{3,2,1,0:T(1,128)S(1)}, u32[]{:S(2)}, u32[]{:S(2)}) async-start(f32[64,9,1,128]{3,2,1,0:T(1,128)} %bitcast.10), calls=%async_computation.2 | async-start | bytes 589824 | tf_op jit(solution)/shard_map/all_to_all | solution.py:706
  62.0 2.6 %shard_map.100 = (s32[32,128]{1,0:T(8,128)S(1)}, s32[32,128]{1,0:T(8,128)S(1)}) custom-call(s32[64,128]{1,0:T(8,128)S(1)} %bitcast.22), custom_call_target="tpu_custom_call" | custom-call | tf_op jit(solution)/shard_map/pallas_call | solution.py:694
  64.5 0.0 copy-start.3
  64.5 6.3 %shard_map.99 = f32[3,16,256]{2,1,0:T(8,128)} custom-call(f32[11520,256]{1,0:T(8,128)} %get-tuple-element.15.weights.colors, f32[11520,256]{1,0:T(8,128)} %get-tuple-element.15.weights.colors), custom_call_target="tpu_custom_call" | custom-call | tf_op jit(solution)/shard_map/pallas_call | solution.py:592
  70.8 4.4 %all-to-all-done.2 = f32[64,9,1,128]{3,2,1,0:T(1,128)S(1)} async-done(((f32[64,9,1,128]{3,2,1,0:T(1,128)}), f32[64,9,1,128]{3,2,1,0:T(1,128)S(1)}, u32[]{:S(2)}, u32[]{:S(2)}) %all-to-all-start.2) | async-done | bytes 294944 | tf_op jit(solution)/shard_map/all_to_all | solution.py:706
  75.2 0.0 copy-done.3
  75.2 2.1 %shard_map.102.high_ref = f32[296,128]{1,0:T(8,128)S(1)} custom-call(f32[8,16]{1,0:T(8,128)S(1)} %bitcast.25, s32[1]{0:T(128)S(6)} %copy.13.view_ref, s32[32,128]{1,0:T(8,128)S(1)} %get-tuple-element.20.index_ref, f32[576,128]{1,0:T(8,128)S(1)} %bitcast.17), custom_call_target="tpu_custom_call" | custom-call | tf_op jit(solution)/shard_map/pallas_call | solution.py:694
  77.2 2.1 %shard_map.101.low_ref = f32[296,128]{1,0:T(8,128)S(1)} custom-call(f32[8,16]{1,0:T(8,128)S(1)} %bitcast.26, s32[1]{0:T(128)S(6)} %copy.13.view_ref, s32[32,128]{1,0:T(8,128)S(1)} %get-tuple-element.18.index_ref, f32[576,128]{1,0:T(8,128)S(1)} %bitcast.18), custom_call_target="tpu_custom_call" | custom-call | tf_op jit(solution)/shard_map/pallas_call | solution.py:694
  79.3 0.9 collective-permute-start.1
  80.2 2.4 %collective-permute-start = (f32[296,128]{1,0:T(8,128)S(1)}, f32[296,128]{1,0:T(8,128)S(1)}, u32[]{:S(2)}, u32[]{:S(2)}) collective-permute-start(f32[296,128]{1,0:T(8,128)S(1)} %shard_map.101.low_ref), channel_id=1, source_target_pairs={{0,1},{1,2},{2,3},{3,0},{4,5},{5,6},{6,7},{7,4},{8,9},{9,10},{10,1... | collective-permute-start | bytes 454664 | tf_op jit(solution)/shard_map/ppermute | solution.py:755
  82.6 0.0 collective-permute-start.4
  82.7 2.0 %collective-permute-start.5 = (f32[296,128]{1,0:T(8,128)S(1)}, f32[296,128]{1,0:T(8,128)S(1)}, u32[]{:S(2)}, u32[]{:S(2)}) collective-permute-start(f32[296,128]{1,0:T(8,128)S(1)} %shard_map.101.low_ref), channel_id=1, source_target_pairs={{0,3},{1,0},{2,1},{3,2},{4,7},{5,4},{6,5},{7,6},{8,11},{9,8},{10,9... | collective-permute-start | bytes 454664 | tf_op jit(solution)/shard_map/ppermute | solution.py:756
  84.7 1.2 %shard_map.103.sum_ref = f32[61,64,128]{2,1,0:T(8,128)S(1)} custom-call(f32[4608,128]{1,0:T(8,128)S(1)} %get-tuple-element.17.spread, f32[296,128]{1,0:T(8,128)S(1)} %shard_map.101.low_ref, f32[296,128]{1,0:T(8,128)S(1)} %shard_map.102.high_ref), custom_call_target="tpu_custom_call" | custom-call | tf_op jit(solution)/shard_map/pallas_call | solution.py:694
  85.9 1.4 %collective-permute-done.1.right_high = f32[296,128]{1,0:T(8,128)S(1)} collective-permute-done((f32[296,128]{1,0:T(8,128)S(1)}, f32[296,128]{1,0:T(8,128)S(1)}, u32[]{:S(2)}, u32[]{:S(2)}) %collective-permute-start.1) | collective-permute-done | bytes 151584 | tf_op jit(solution)/shard_map/ppermute | solution.py:758
  87.3 0.0 collective-permute-done.left_low
  87.3 3.4 %collective-permute-start.2 = (f32[296,128]{1,0:T(8,128)S(1)}, f32[296,128]{1,0:T(8,128)S(1)}, u32[]{:S(2)}, u32[]{:S(2)}) collective-permute-start(f32[296,128]{1,0:T(8,128)S(1)} %collective-permute-done.left_low), channel_id=1, source_target_pairs={{0,1},{1,2},{2,3},{3,0},{4,5},{5,6},{6,7},{7,4},{8,9},{9,10},{10,1... | collective-permute-start | bytes 454664 | tf_op jit(solution)/shard_map/ppermute | solution.py:763
  90.6 0.0 collective-permute-start.3
  90.7 0.0 collective-permute-done.4.left_high
  90.7 0.0 collective-permute-done.5.right_low
  90.7 1.9 %shard_map.104.sum_ref = f32[61,64,128]{2,1,0:T(8,128)S(1)} custom-call(f32[4608,128]{1,0:T(8,128)S(1)} %get-tuple-element.17.spread, f32[296,128]{1,0:T(8,128)S(1)} %collective-permute-done.left_low, f32[296,128]{1,0:T(8,128)S(1)} %collective-permute-done.4.left_high, f32[296,128]{1,0:T(8,128)S(1)} %collective-permute-done.5.right_low, ...), custom_call_target="tpu_custom_call" | custom-call | tf_op jit(solution)/shard_map/pallas_call | solution.py:694
  92.6 0.8 collective-permute-done.2.low_ref
  93.4 3.7 %collective-permute-done.3.high_ref = f32[296,128]{1,0:T(8,128)S(1)} collective-permute-done((f32[296,128]{1,0:T(8,128)S(1)}, f32[296,128]{1,0:T(8,128)S(1)}, u32[]{:S(2)}, u32[]{:S(2)}) %collective-permute-start.3) | collective-permute-done | bytes 151584 | tf_op jit(solution)/shard_map/ppermute | solution.py:764
  97.0 2.8 %shard_map.105 = f32[59,8192]{1,0:T(8,128)} custom-call(f32[4608,128]{1,0:T(8,128)S(1)} %get-tuple-element.17.spread, f32[296,128]{1,0:T(8,128)S(1)} %collective-permute-done.2.low_ref, f32[296,128]{1,0:T(8,128)S(1)} %collective-permute-done.3.high_ref, f32[61,64,128]{2,1,0:T(8,128)S(1)} %shard_map.104.sum_ref), custom_call_target="tpu_custom_call" | custom-call | tf_op jit(solution)/shard_map/pallas_call | solution.py:694
Async XLA Ops:
  0.6 45.4 %copy-start.1 = (f32[1,16,3,256]{3,1,2,0:T(8,128)S(1)}, f32[1,16,3,256]{3,1,2,0:T(8,128)}, u32[]{:S(2)}) copy-start(f32[1,16,3,256]{3,1,2,0:T(8,128)} %param.15) | copy-start | bytes 147460
  0.6 45.4 %copy-start.4 = (s32[1,16]{1,0:T(1,128)S(1)}, s32[1,16]{1,0:T(1,128)}, u32[]{:S(2)}) copy-start(s32[1,16]{1,0:T(1,128)} %plan_ref.1) | copy-start | bytes 196
  0.7 45.4 %copy-start.5 = (s32[1,16]{1,0:T(1,128)S(1)}, s32[1,16]{1,0:T(1,128)}, u32[]{:S(2)}) copy-start(s32[1,16]{1,0:T(1,128)} %length_ref.1) | copy-start | bytes 196
  2.5 21.7 %all-to-all-start = ((s32[64,1,1,128]{3,2,1,0:T(1,128)}), s32[64,1,1,128]{3,2,1,0:T(1,128)S(1)}, u32[]{:S(2)}, u32[]{:S(2)}) async-start(s32[64,1,1,128]{3,2,1,0:T(1,128)} %bitcast.27), calls=%async_computation | async-start | bytes 65536 | tf_op jit(solution)/shard_map/all_to_all | solution.py:706
  15.2 1.6 %copy-start = (f32[59,8192]{1,0:T(8,128)S(1)}, f32[59,8192]{1,0:T(8,128)}, u32[]{:S(2)}) copy-start(f32[59,8192]{1,0:T(8,128)} %gauss_hbm.1) | copy-start | bytes 5799940
  16.8 0.7 copy-start.2
  56.6 18.6 %all-to-all-start.2 = ((f32[64,9,1,128]{3,2,1,0:T(1,128)}), f32[64,9,1,128]{3,2,1,0:T(1,128)S(1)}, u32[]{:S(2)}, u32[]{:S(2)}) async-start(f32[64,9,1,128]{3,2,1,0:T(1,128)} %bitcast.10), calls=%async_computation.2 | async-start | bytes 589824 | tf_op jit(solution)/shard_map/all_to_all | solution.py:706
  64.5 10.6 %copy-start.3 = (f32[16,8]{0,1:T(8,128)S(1)}, f32[16,8]{0,1:T(8,128)}, u32[]{:S(2)}) copy-start(f32[16,8]{0,1:T(8,128)} %param.9) | copy-start | bytes 1540
  79.3 8.0 %collective-permute-start.1 = (f32[296,128]{1,0:T(8,128)S(1)}, f32[296,128]{1,0:T(8,128)S(1)}, u32[]{:S(2)}, u32[]{:S(2)}) collective-permute-start(f32[296,128]{1,0:T(8,128)S(1)} %shard_map.102.high_ref), channel_id=1, source_target_pairs={{0,3},{1,0},{2,1},{3,2},{4,7},{5,4},{6,5},{7,6},{8,11},{9,8},{10,9... | collective-permute-start | bytes 454664 | tf_op jit(solution)/shard_map/ppermute | solution.py:758
  80.2 7.1 %collective-permute-start = (f32[296,128]{1,0:T(8,128)S(1)}, f32[296,128]{1,0:T(8,128)S(1)}, u32[]{:S(2)}, u32[]{:S(2)}) collective-permute-start(f32[296,128]{1,0:T(8,128)S(1)} %shard_map.101.low_ref), channel_id=1, source_target_pairs={{0,1},{1,2},{2,3},{3,0},{4,5},{5,6},{6,7},{7,4},{8,9},{9,10},{10,1... | collective-permute-start | bytes 454664 | tf_op jit(solution)/shard_map/ppermute | solution.py:755
  82.6 8.0 %collective-permute-start.4 = (f32[296,128]{1,0:T(8,128)S(1)}, f32[296,128]{1,0:T(8,128)S(1)}, u32[]{:S(2)}, u32[]{:S(2)}) collective-permute-start(f32[296,128]{1,0:T(8,128)S(1)} %shard_map.102.high_ref), channel_id=1, source_target_pairs={{0,1},{1,2},{2,3},{3,0},{4,5},{5,6},{6,7},{7,4},{8,9},{9,10},{10,1... | collective-permute-start | bytes 454664 | tf_op jit(solution)/shard_map/ppermute | solution.py:759
  82.7 8.0 %collective-permute-start.5 = (f32[296,128]{1,0:T(8,128)S(1)}, f32[296,128]{1,0:T(8,128)S(1)}, u32[]{:S(2)}, u32[]{:S(2)}) collective-permute-start(f32[296,128]{1,0:T(8,128)S(1)} %shard_map.101.low_ref), channel_id=1, source_target_pairs={{0,3},{1,0},{2,1},{3,2},{4,7},{5,4},{6,5},{7,6},{8,11},{9,8},{10,9... | collective-permute-start | bytes 454664 | tf_op jit(solution)/shard_map/ppermute | solution.py:756
  87.3 6.1 %collective-permute-start.2 = (f32[296,128]{1,0:T(8,128)S(1)}, f32[296,128]{1,0:T(8,128)S(1)}, u32[]{:S(2)}, u32[]{:S(2)}) collective-permute-start(f32[296,128]{1,0:T(8,128)S(1)} %collective-permute-done.left_low), channel_id=1, source_target_pairs={{0,1},{1,2},{2,3},{3,0},{4,5},{5,6},{6,7},{7,4},{8,9},{9,10},{10,1... | collective-permute-start | bytes 454664 | tf_op jit(solution)/shard_map/ppermute | solution.py:763
  90.6 6.4 %collective-permute-start.3 = (f32[296,128]{1,0:T(8,128)S(1)}, f32[296,128]{1,0:T(8,128)S(1)}, u32[]{:S(2)}, u32[]{:S(2)}) collective-permute-start(f32[296,128]{1,0:T(8,128)S(1)} %collective-permute-done.1.right_high), channel_id=1, source_target_pairs={{0,3},{1,0},{2,1},{3,2},{4,7},{5,4},{6,5},{7,6},{8,11},{9,8},{10,9... | collective-permute-start | bytes 454664 | tf_op jit(solution)/shard_map/ppermute | solution.py:764

commit v5 on v3

--- a/solution.py
+++ b/solution.py
@@ -34,9 +34,9 @@
 half_rows = 296
 lay_unroll = 16
 image_step = 8
-colors_at = 8448
-forward_unroll = 16
-backward_unroll = 16
+features_at = 9216
+forward_unroll = 32
+backward_unroll = 32
 pick_unroll = 16
 vmem = pl.BlockSpec(memory_space=pltpu.VMEM)
 smem = pl.BlockSpec(memory_space=pltpu.SMEM)
@@ -354,6 +354,19 @@
     )
 
 
+def tile_colors(rows_ref, i):
+    own_tile = iota((16, 256), 0) == (iota((16, 256), 1) & 15)
+    high = []
+    low = []
+    for h in range(3):
+        lines = [pl.ds((2 * i + own) * feats + 6 + h, 1) for own in range(2)]
+        value = jnp.concatenate([rows_ref[line, :] for line in lines], axis=1)
+        parts = pieces(jnp.where(own_tile, value, 0.0), 2)
+        high.append(parts[0])
+        low.append(parts[1])
+    return jnp.concatenate(high + low, axis=0)
+
+
 def render_kernel(
     plan_ref,
     length_ref,
@@ -362,7 +375,6 @@
     made_hbm,
     out_ref,
     weights,
-    colors,
     coef,
     alphas,
     shades,
@@ -370,6 +382,10 @@
     tints,
     sems,
 ):
+    store_rows = pltpu.make_async_copy(
+        rows_ref, made_hbm.at[features_at : features_at + 64 * feats, 0:128], sems.at[32]
+    )
+    store_rows.start()
     lane_step = iota((8, 128), 1) >> 4
     center_u, center_v, length = tile_frame(plan_ref, length_ref)
 
@@ -421,15 +437,8 @@
     cot_both = jnp.concatenate([cot_high, cot_low], axis=0)
     cot_all = jnp.concatenate([cot_high, cot_high, cot_low], axis=0)
     same_tile = (iota((48, 256), 0) & 15) == (iota((48, 256), 1) & 15)
-    own_tile = iota((16, 256), 0) == (iota((16, 256), 1) & 15)
     across = (((1,), (1,)), ((), ()))
     along = (((0,), (0,)), ((), ()))
-
-    def pair(i, ref, row, step):
-        return jnp.concatenate(
-            [ref[pl.ds(2 * i * step + row, 1), :], ref[pl.ds((2 * i + 1) * step + row, 1), :]],
-            axis=1,
-        )
 
     def lay(i, carry):
         raw = jnp.concatenate(
@@ -445,16 +454,8 @@
             block.astype(bf16), terms, along, preferred_element_type=f32
         )
         alphas[pl.ds(base, 256), :] = jnp.exp2(power)
-        high = []
-        low = []
-        for h in range(3):
-            value = jnp.where(own_tile, pair(i, rows_ref, 6 + h, feats), 0.0)
-            parts = pieces(value, 2)
-            high.append(parts[0])
-            low.append(parts[1])
-        color = jnp.concatenate(high + low, axis=0)
-        colors[pl.ds(pl.multiple_of(i * 96, 8), 96), :] = color
-        color = jnp.concatenate([color] + high, axis=0).astype(bf16)
+        color = tile_colors(rows_ref, i)
+        color = jnp.concatenate([color, color[0:48]], axis=0).astype(bf16)
         shades[pl.ds(base, 256), :] = lax.dot_general(
             color, cot_all, along, preferred_element_type=f32
         )
@@ -466,8 +467,6 @@
         rows = pl.ds(pl.multiple_of(i * 256, 256), 256)
         return pltpu.make_async_copy(weights.at[rows], made_hbm.at[rows], sems.at[i])
 
-    store_colors = pltpu.make_async_copy(colors, made_hbm.at[colors_at : colors_at + 3072], sems.at[32])
-    store_colors.start()
 
     def forward(i, clear):
         base = pl.multiple_of(i * 256, 256)
@@ -542,12 +541,12 @@
         return carry
 
     lax.fori_loop(0, 8, finish, 0)
-    store_colors.wait()
+    store_rows.wait()
     for i in range(32):
         store(i).wait()
 
 
-def image_kernel(weights, colors, image_ref):
+def image_kernel(weights, rows_ref, image_ref):
     @pl.when(pl.program_id(0) == 0)
     def _():
         image_ref[...] = jnp.zeros_like(image_ref)
@@ -556,7 +555,7 @@
         weight = weights[256 * i : 256 * i + 256, :]
         top = weight.astype(bf16)
         low = (weight - top.astype(f32)).astype(bf16)
-        color = colors[96 * i : 96 * i + 96, :].astype(bf16)
+        color = tile_colors(rows_ref, pl.program_id(0) * image_step + i).astype(bf16)
         both = jnp.dot(color, top, preferred_element_type=f32)
         image = both[0:48] + both[48:96]
         image += jnp.dot(color[0:48], low, preferred_element_type=f32)
@@ -570,14 +569,13 @@
     return call(
         render_kernel,
         (
-            shape((colors_at + 3072, 256), f32),
+            shape((features_at + 64 * feats, 256), f32),
             shape((64 * feats, 128), f32),
         ),
         (tile_plan, tile_lengths, arrived, cots),
         [smem, smem, vmem, vmem],
         [
             pltpu.VMEM((8192, 256), f32),
-            pltpu.VMEM((3072, 256), f32),
             pltpu.VMEM((512, 128), f32),
             pltpu.VMEM((8192, 256), f32),
             pltpu.VMEM((8192, 256), f32),
@@ -597,7 +595,7 @@
         grid=(32 // image_step,),
         in_specs=[
             pl.BlockSpec((256 * image_step, 256), lambda i: (i, 0)),
-            pl.BlockSpec((96 * image_step, 256), lambda i: (i + colors_at // (96 * image_step), 0)),
+            pl.BlockSpec((64 * feats, 128), lambda i: (features_at // (64 * feats), 0)),
         ],
         out_specs=pl.BlockSpec((3, 16, 256), lambda i: (0, 0, 0)),
         compiler_params=pltpu.CompilerParams(vmem_limit_bytes=60 * 1024 * 1024),

time: 97.1 us -> 96.7 us (level)
  no operation moved by 1% of the time
where the time goes in v5:
time: 96.7 us; the launch traced here: 96.3 us
  Pallas kernels  34.5 us (36%)
  starting transfers between devices  23.5 us (24%)
  blocking collectives  18.8 us (19%)
  waiting for transfers between devices  15.7 us (16%)
  local copies, waits for them, and re-layouts  2.29 us (2%)
  between operations  1.57 us (2%)
    pallas_call x9, Pallas kernels, call(): pl.pallas_call(kernel, out_shape=out, in_specs=specs, out_specs=out_specs...  28.7 us
    all_to_all x1, blocking collectives, exchange(): lax.all_to_all(parts, 'space', split_axis=0, concat_axis=0, tiled=True)  18.8 us
    all_to_all x2, starting transfers between devices, exchange(): lax.all_to_all(parts, 'space', split_axis=0, concat_axis=0, tiled=True)  17.3 us
    all_to_all x2, waiting for transfers between devices, exchange(): lax.all_to_all(parts, 'space', split_axis=0, concat_axis=0, tiled=True)  9.69 us
    pallas_call x1, Pallas kernels, compose(): pl.pallas_call(image_kernel, out_shape=jax.ShapeDtypeStruct((3, 16, 256),...  5.83 us
    unnamed x12, local copies, waits for them, and re-layouts  2.29 us
  transfers between devices with their start and end apart: 8, of which 7 were waited for; matrix products, arithmetic and copies ran while one was open for 0% of the time, Pallas kernels for 14%

profile of v5, /device:TPU:6, one launch (start us, length us, event | category | flops | bytes accessed | tf_op | source)
XLA Modules:
  0.0 96.3 jit_solution(9763086744766560120)
XLA Ops:
  0.6 0.0 copy-start.1
  0.6 0.0 copy-start.4
  0.7 0.0 copy-start.5
  0.7 1.8 %shard_map.95 = s32[64,128]{1,0:T(8,128)} custom-call(s32[64,128]{1,0:T(8,128)} %bitcast.27, s32[16,512]{1,0:T(8,128)} %bitcast.28), custom_call_target="tpu_custom_call" | custom-call | tf_op jit(solution)/shard_map/pallas_call | solution.py:694
  2.5 12.1 %all-to-all-start = ((s32[64,1,1,128]{3,2,1,0:T(1,128)}), s32[64,1,1,128]{3,2,1,0:T(1,128)S(1)}, u32[]{:S(2)}, u32[]{:S(2)}) async-start(s32[64,1,1,128]{3,2,1,0:T(1,128)} %bitcast.25), calls=%async_computation | async-start | bytes 65536 | tf_op jit(solution)/shard_map/all_to_all | solution.py:706
  15.2 0.0 copy-start
  15.2 1.6 %copy-done = f32[59,8192]{1,0:T(8,128)S(1)} copy-done((f32[59,8192]{1,0:T(8,128)S(1)}, f32[59,8192]{1,0:T(8,128)}, u32[]{:S(2)}) %copy-start) | copy-done | bytes 1933336
  16.8 0.0 copy-start.2
  16.8 0.7 copy-done.2
  17.5 1.9 %shard_map.96 = (bf16[640,256]{1,0:T(8,128)(2,1)S(1)}, f32[4608,128]{1,0:T(8,128)S(1)}) custom-call(f32[8,16]{1,0:T(8,128)S(1)} %bitcast.23, s32[1]{0:T(128)S(6)} %copy.13.view_ref, f32[59,8192]{1,0:T(8,128)S(1)} %copy-done), custom_call_target="tpu_custom_call" | custom-call | tf_op jit(solution)/shard_map/pallas_call | solution.py:694
  19.4 4.7 %all-to-all-done = s32[64,1,1,128]{3,2,1,0:T(1,128)S(1)} async-done(((s32[64,1,1,128]{3,2,1,0:T(1,128)}), s32[64,1,1,128]{3,2,1,0:T(1,128)S(1)}, u32[]{:S(2)}, u32[]{:S(2)}) %all-to-all-start) | async-done | bytes 32800 | tf_op jit(solution)/shard_map/all_to_all | solution.py:706
  24.1 3.1 %shard_map.97 = f32[576,128]{1,0:T(8,128)S(1)} custom-call(s32[64,128]{1,0:T(8,128)S(1)} %bitcast.20, bf16[640,256]{1,0:T(8,128)(2,1)S(1)} %get-tuple-element.13.table_ref), custom_call_target="tpu_custom_call" | custom-call | tf_op jit(solution)/shard_map/pallas_call | solution.py:694
  27.2 18.8 %all_to_all.15 = f32[64,9,1,128]{3,2,1,0:T(1,128)S(1)} all-to-all(f32[64,9,1,128]{3,2,1,0:T(1,128)S(1)} %bitcast.19), channel_id=1, replica_groups=mesh['space'=64,'view'=4] {'space'}, dimensions={0} | all-to-all | bytes 589824 | tf_op jit(solution)/shard_map/all_to_all | solution.py:706
  46.0 0.0 copy-done.1
  46.0 0.0 copy-done.4
  46.0 0.0 copy-done.5
  46.0 10.1 %shard_map.98 = (f32[9792,256]{1,0:T(8,128)}, f32[576,128]{1,0:T(8,128)}) custom-call(s32[1,16]{1,0:T(1,128)S(1)} %copy-done.4, s32[1,16]{1,0:T(1,128)S(1)} %copy-done.5, f32[576,128]{1,0:T(8,128)S(1)} %bitcast.18, f32[3,16,256]{2,1,0:T(8,128)S(1)} %bitcast.22), custom_call_target="tpu_custom_call" | custom-call | tf_op jit(solution)/shard_map/pallas_call | solution.py:694
  56.2 5.2 %all-to-all-start.2 = ((f32[64,9,1,128]{3,2,1,0:T(1,128)}), f32[64,9,1,128]{3,2,1,0:T(1,128)S(1)}, u32[]{:S(2)}, u32[]{:S(2)}) async-start(f32[64,9,1,128]{3,2,1,0:T(1,128)} %bitcast.10), calls=%async_computation.2 | async-start | bytes 589824 | tf_op jit(solution)/shard_map/all_to_all | solution.py:706
  61.3 2.6 %shard_map.100.index_ref = s32[64,128]{1,0:T(8,128)S(1)} custom-call(s32[64,128]{1,0:T(8,128)S(1)} %bitcast.21), custom_call_target="tpu_custom_call" | custom-call | tf_op jit(solution)/shard_map/pallas_call | solution.py:694
  63.9 0.0 copy-start.3
  63.9 5.8 %shard_map.99 = f32[3,16,256]{2,1,0:T(8,128)} custom-call(f32[9792,256]{1,0:T(8,128)} %get-tuple-element.15.weights.rows_ref, f32[9792,256]{1,0:T(8,128)} %get-tuple-element.15.weights.rows_ref), custom_call_target="tpu_custom_call" | custom-call | tf_op jit(solution)/shard_map/pallas_call | solution.py:592
  69.8 5.0 %all-to-all-done.2 = f32[64,9,1,128]{3,2,1,0:T(1,128)S(1)} async-done(((f32[64,9,1,128]{3,2,1,0:T(1,128)}), f32[64,9,1,128]{3,2,1,0:T(1,128)S(1)}, u32[]{:S(2)}, u32[]{:S(2)}) %all-to-all-start.2) | async-done | bytes 294944 | tf_op jit(solution)/shard_map/all_to_all | solution.py:706
  74.7 0.0 copy-done.3
  74.7 3.3 %shard_map.101 = (f32[296,128]{1,0:T(8,128)S(1)}, f32[296,128]{1,0:T(8,128)S(1)}) custom-call(f32[8,16]{1,0:T(8,128)S(1)} %bitcast.24, s32[1]{0:T(128)S(6)} %copy.13.view_ref, s32[64,128]{1,0:T(8,128)S(1)} %shard_map.100.index_ref, f32[576,128]{1,0:T(8,128)S(1)} %bitcast.17), custom_call_target="tpu_custom_call" | custom-call | tf_op jit(solution)/shard_map/pallas_call | solution.py:694
  78.1 0.6 collective-permute-start
  78.6 1.5 %collective-permute-start.1 = (f32[296,128]{1,0:T(8,128)S(1)}, f32[296,128]{1,0:T(8,128)S(1)}, u32[]{:S(2)}, u32[]{:S(2)}) collective-permute-start(f32[296,128]{1,0:T(8,128)S(1)} %get-tuple-element.20.high_ref), channel_id=1, source_target_pairs={{0,3},{1,0},{2,1},{3,2},{4,7},{5,4},{6,5},{7,6},{8,11},{9,8},{10,9... | collective-permute-start | bytes 454664 | tf_op jit(solution)/shard_map/ppermute | solution.py:756
  80.2 1.7 %collective-permute-start.4 = (f32[296,128]{1,0:T(8,128)S(1)}, f32[296,128]{1,0:T(8,128)S(1)}, u32[]{:S(2)}, u32[]{:S(2)}) collective-permute-start(f32[296,128]{1,0:T(8,128)S(1)} %get-tuple-element.20.high_ref), channel_id=1, source_target_pairs={{0,1},{1,2},{2,3},{3,0},{4,5},{5,6},{6,7},{7,4},{8,9},{9,10},{10,1... | collective-permute-start | bytes 454664 | tf_op jit(solution)/shard_map/ppermute | solution.py:757
  81.9 0.3 collective-permute-start.5
  82.2 1.2 %shard_map.102.sum_ref = f32[61,64,128]{2,1,0:T(8,128)S(1)} custom-call(f32[4608,128]{1,0:T(8,128)S(1)} %get-tuple-element.17.spread, f32[296,128]{1,0:T(8,128)S(1)} %get-tuple-element.19.low_ref, f32[296,128]{1,0:T(8,128)S(1)} %get-tuple-element.20.high_ref), custom_call_target="tpu_custom_call" | custom-call | tf_op jit(solution)/shard_map/pallas_call | solution.py:694
  83.4 1.5 %collective-permute-done.left_low = f32[296,128]{1,0:T(8,128)S(1)} collective-permute-done((f32[296,128]{1,0:T(8,128)S(1)}, f32[296,128]{1,0:T(8,128)S(1)}, u32[]{:S(2)}, u32[]{:S(2)}) %collective-permute-start) | collective-permute-done | bytes 151584 | tf_op jit(solution)/shard_map/ppermute | solution.py:755
  84.9 1.4 %collective-permute-done.1.right_high = f32[296,128]{1,0:T(8,128)S(1)} collective-permute-done((f32[296,128]{1,0:T(8,128)S(1)}, f32[296,128]{1,0:T(8,128)S(1)}, u32[]{:S(2)}, u32[]{:S(2)}) %collective-permute-start.1) | collective-permute-done | bytes 151584 | tf_op jit(solution)/shard_map/ppermute | solution.py:756
  86.3 0.6 collective-permute-start.2
  86.9 1.4 %collective-permute-start.3 = (f32[296,128]{1,0:T(8,128)S(1)}, f32[296,128]{1,0:T(8,128)S(1)}, u32[]{:S(2)}, u32[]{:S(2)}) collective-permute-start(f32[296,128]{1,0:T(8,128)S(1)} %collective-permute-done.1.right_high), channel_id=1, source_target_pairs={{0,3},{1,0},{2,1},{3,2},{4,7},{5,4},{6,5},{7,6},{8,11},{9,8},{10,9... | collective-permute-start | bytes 454664 | tf_op jit(solution)/shard_map/ppermute | solution.py:763
  88.3 0.0 collective-permute-done.4.left_high
  88.3 0.7 collective-permute-done.5.right_low
  89.0 1.9 %shard_map.103.sum_ref = f32[61,64,128]{2,1,0:T(8,128)S(1)} custom-call(f32[4608,128]{1,0:T(8,128)S(1)} %get-tuple-element.17.spread, f32[296,128]{1,0:T(8,128)S(1)} %collective-permute-done.left_low, f32[296,128]{1,0:T(8,128)S(1)} %collective-permute-done.4.left_high, f32[296,128]{1,0:T(8,128)S(1)} %collective-permute-done.5.right_low, ...), custom_call_target="tpu_custom_call" | custom-call | tf_op jit(solution)/shard_map/pallas_call | solution.py:694
  90.9 0.5 collective-permute-done.2.low_ref
  91.5 1.9 %collective-permute-done.3.high_ref = f32[296,128]{1,0:T(8,128)S(1)} collective-permute-done((f32[296,128]{1,0:T(8,128)S(1)}, f32[296,128]{1,0:T(8,128)S(1)}, u32[]{:S(2)}, u32[]{:S(2)}) %collective-permute-start.3) | collective-permute-done | bytes 151584 | tf_op jit(solution)/shard_map/ppermute | solution.py:763
  93.3 2.8 %shard_map.104 = f32[59,8192]{1,0:T(8,128)} custom-call(f32[4608,128]{1,0:T(8,128)S(1)} %get-tuple-element.17.spread, f32[296,128]{1,0:T(8,128)S(1)} %collective-permute-done.2.low_ref, f32[296,128]{1,0:T(8,128)S(1)} %collective-permute-done.3.high_ref, f32[61,64,128]{2,1,0:T(8,128)S(1)} %shard_map.103.sum_ref), custom_call_target="tpu_custom_call" | custom-call | tf_op jit(solution)/shard_map/pallas_call | solution.py:694
Async XLA Ops:
  0.6 45.4 %copy-start.1 = (f32[1,16,3,256]{3,1,2,0:T(8,128)S(1)}, f32[1,16,3,256]{3,1,2,0:T(8,128)}, u32[]{:S(2)}) copy-start(f32[1,16,3,256]{3,1,2,0:T(8,128)} %param.15) | copy-start | bytes 147460
  0.6 45.4 %copy-start.4 = (s32[1,16]{1,0:T(1,128)S(1)}, s32[1,16]{1,0:T(1,128)}, u32[]{:S(2)}) copy-start(s32[1,16]{1,0:T(1,128)} %plan_ref.1) | copy-start | bytes 196
  0.7 45.4 %copy-start.5 = (s32[1,16]{1,0:T(1,128)S(1)}, s32[1,16]{1,0:T(1,128)}, u32[]{:S(2)}) copy-start(s32[1,16]{1,0:T(1,128)} %length_ref.1) | copy-start | bytes 196
  2.5 21.7 %all-to-all-start = ((s32[64,1,1,128]{3,2,1,0:T(1,128)}), s32[64,1,1,128]{3,2,1,0:T(1,128)S(1)}, u32[]{:S(2)}, u32[]{:S(2)}) async-start(s32[64,1,1,128]{3,2,1,0:T(1,128)} %bitcast.25), calls=%async_computation | async-start | bytes 65536 | tf_op jit(solution)/shard_map/all_to_all | solution.py:706
  15.2 1.6 %copy-start = (f32[59,8192]{1,0:T(8,128)S(1)}, f32[59,8192]{1,0:T(8,128)}, u32[]{:S(2)}) copy-start(f32[59,8192]{1,0:T(8,128)} %gauss_hbm.1) | copy-start | bytes 5799940
  16.8 0.7 copy-start.2
  56.2 18.6 %all-to-all-start.2 = ((f32[64,9,1,128]{3,2,1,0:T(1,128)}), f32[64,9,1,128]{3,2,1,0:T(1,128)S(1)}, u32[]{:S(2)}, u32[]{:S(2)}) async-start(f32[64,9,1,128]{3,2,1,0:T(1,128)} %bitcast.10), calls=%async_computation.2 | async-start | bytes 589824 | tf_op jit(solution)/shard_map/all_to_all | solution.py:706
  63.9 10.8 %copy-start.3 = (f32[16,8]{0,1:T(8,128)S(1)}, f32[16,8]{0,1:T(8,128)}, u32[]{:S(2)}) copy-start(f32[16,8]{0,1:T(8,128)} %param.9) | copy-start | bytes 1540
  78.1 6.8 %collective-permute-start = (f32[296,128]{1,0:T(8,128)S(1)}, f32[296,128]{1,0:T(8,128)S(1)}, u32[]{:S(2)}, u32[]{:S(2)}) collective-permute-start(f32[296,128]{1,0:T(8,128)S(1)} %get-tuple-element.19.low_ref), channel_id=1, source_target_pairs={{0,1},{1,2},{2,3},{3,0},{4,5},{5,6},{6,7},{7,4},{8,9},{9,10},{10,1... | collective-permute-start | bytes 454664 | tf_op jit(solution)/shard_map/ppermute | solution.py:755
  78.6 7.6 %collective-permute-start.1 = (f32[296,128]{1,0:T(8,128)S(1)}, f32[296,128]{1,0:T(8,128)S(1)}, u32[]{:S(2)}, u32[]{:S(2)}) collective-permute-start(f32[296,128]{1,0:T(8,128)S(1)} %get-tuple-element.20.high_ref), channel_id=1, source_target_pairs={{0,3},{1,0},{2,1},{3,2},{4,7},{5,4},{6,5},{7,6},{8,11},{9,8},{10,9... | collective-permute-start | bytes 454664 | tf_op jit(solution)/shard_map/ppermute | solution.py:756
  80.2 8.1 %collective-permute-start.4 = (f32[296,128]{1,0:T(8,128)S(1)}, f32[296,128]{1,0:T(8,128)S(1)}, u32[]{:S(2)}, u32[]{:S(2)}) collective-permute-start(f32[296,128]{1,0:T(8,128)S(1)} %get-tuple-element.20.high_ref), channel_id=1, source_target_pairs={{0,1},{1,2},{2,3},{3,0},{4,5},{5,6},{6,7},{7,4},{8,9},{9,10},{10,1... | collective-permute-start | bytes 454664 | tf_op jit(solution)/shard_map/ppermute | solution.py:757
  81.9 7.1 %collective-permute-start.5 = (f32[296,128]{1,0:T(8,128)S(1)}, f32[296,128]{1,0:T(8,128)S(1)}, u32[]{:S(2)}, u32[]{:S(2)}) collective-permute-start(f32[296,128]{1,0:T(8,128)S(1)} %get-tuple-element.19.low_ref), channel_id=1, source_target_pairs={{0,3},{1,0},{2,1},{3,2},{4,7},{5,4},{6,5},{7,6},{8,11},{9,8},{10,9... | collective-permute-start | bytes 454664 | tf_op jit(solution)/shard_map/ppermute | solution.py:758
  86.3 5.2 %collective-permute-start.2 = (f32[296,128]{1,0:T(8,128)S(1)}, f32[296,128]{1,0:T(8,128)S(1)}, u32[]{:S(2)}, u32[]{:S(2)}) collective-permute-start(f32[296,128]{1,0:T(8,128)S(1)} %collective-permute-done.left_low), channel_id=1, source_target_pairs={{0,1},{1,2},{2,3},{3,0},{4,5},{5,6},{6,7},{7,4},{8,9},{9,10},{10,1... | collective-permute-start | bytes 454664 | tf_op jit(solution)/shard_map/ppermute | solution.py:762
  86.9 6.4 %collective-permute-start.3 = (f32[296,128]{1,0:T(8,128)S(1)}, f32[296,128]{1,0:T(8,128)S(1)}, u32[]{:S(2)}, u32[]{:S(2)}) collective-permute-start(f32[296,128]{1,0:T(8,128)S(1)} %collective-permute-done.1.right_high), channel_id=1, source_target_pairs={{0,3},{1,0},{2,1},{3,2},{4,7},{5,4},{6,5},{7,6},{8,11},{9,8},{10,9... | collective-permute-start | bytes 454664 | tf_op jit(solution)/shard_map/ppermute | solution.py:763
